TPU v7x, 32 devices: a whole 2x2x4 slice. The times are simulated.
32 devices in a mesh: req: 8 (over z, x), ep: 4 (over y, core).
Axes of the slice: x: 2, y: 2, z: 4, core: 2. Of those that a mesh axis runs over, the one named last changes fastest.
Arguments:
- hidden: bfloat16 [4096, 1536], P(('req', 'ep')), may hold values from -6 to 6
- parents: int32 [64, 64], P(('req', 'ep')), may hold values from 0 to 62, as said below
- path: int32 [64, 64], P(('req', 'ep')), may hold values from -1 to 63, as said below
- cache_len: int32 [64], P(('req', 'ep')), may hold values from 64 to 1024
- page_table: int32 [64, 8], P(('req', 'ep')), may hold values from 0 to 15, as said below
- kv_pool: bfloat16 [512, 128, 512], P(('req', 'ep')), may hold values from -90 to 90
- mig_slot: int32 [32], P(('req', 'ep')), may hold values from 0 to 1
- mig_dest: int32 [32], P(('req', 'ep')), may hold values from 0 to 3, as said below
- attn_gain: bfloat16 [1536], replicated, may hold values from 0.25 to 1.75
- w_qkv: bfloat16 [1536, 2048], replicated, may hold values from -0.15625 to 0.15625
- w_out: bfloat16 [1536, 1536], replicated, may hold values from -0.15625 to 0.15625
- moe_gain: bfloat16 [1536], replicated, may hold values from 0.25 to 1.75
- w_router: bfloat16 [1536, 32], replicated, may hold values from -0.15625 to 0.15625
- expert_ids: int32 [4096, 4], P(('req', 'ep')), may hold values from 0 to 31, all different within a row; in each aligned block of 128 rows (0 to 127, 128 to 255, ...) at most 32 rows name the same one
- w_gate: bfloat16 [32, 1536, 768], P(('req', 'ep')), may hold values from -0.15625 to 0.15625
- w_up: bfloat16 [32, 1536, 768], P(('req', 'ep')), may hold values from -0.15625 to 0.15625
- w_down: bfloat16 [32, 768, 1536], P(('req', 'ep')), may hold values from -0.21875 to 0.21875
Outputs:
- layer_out: bfloat16 [4096, 1536], P(('req', 'ep'))
- compact_kv: bfloat16 [64, 64, 512], P(('req', 'ep'))
Inputs may be any that keep to these rules, and one draw needn't show every extreme that they name: parents[r, 0] = 0 marks the root; for i >= 1, parents[r, i] < i. `path`: row r lists a chain of the tree of parents[r] from the root 0 down to some token, each entry the parent of the next, then -1. `page_table`: the 2 requests of one device name each of its 16 pool pages once. `mig_dest`: within each index of req, the entries of its 4 devices form a permutation. `expert_ids`: each row names 4 different experts; among the rows of one device no expert is named by more than 32 rows.
All inputs are finite; a program needn't handle non-finite values.
Results may differ from a plain program's by a relative error of at most 0.015.
Values may be sent and summed in bfloat16 or wider, within the bound.
No kernel may reach another device: no remote copies, remote signals or barrier semaphores. Data moves between devices by JAX's collectives and lax.ppermute only.
A program may use at most 128 MiB of HBM per device.

v0:
```python
import jax
import jax.numpy as jnp
from jax import lax
from jax.sharding import PartitionSpec as P

QUERY_HEADS = 12
KEY_VALUE_HEADS = 2
HEAD_SIZE = 128
CAP = 32


EPSILON = 1e-06
ROPE_BASE = 1000000.0
PRECISE = lax.Precision.HIGHEST
MASKED = -1e30


def rms_scale(values, scaling):
    widened = values.astype(jnp.float32)
    spread = jnp.mean(widened * widened, axis=-1, keepdims=True)
    return (widened * lax.rsqrt(spread + EPSILON) * scaling.astype(jnp.float32)).astype(
        jnp.bfloat16
    )


def ancestry(parent_row):
    length = parent_row.shape[-1]
    indices = jnp.arange(length, dtype=jnp.int32)
    linked = (parent_row[:, None] == indices[None, :]).astype(jnp.float32)
    reached = jnp.minimum(linked + jnp.eye(length, dtype=jnp.float32), 1.0)
    for repeat_index in range(max(1, (length - 1).bit_length())):
        reached = jnp.minimum(jnp.dot(reached, reached, precision=PRECISE), 1.0)
    return reached


def apply_rotary(tensor, token_positions):
    halfway = tensor.shape[-1] // 2
    spectrum = ROPE_BASE ** (-2.0 * jnp.arange(halfway, dtype=jnp.float32) / tensor.shape[-1])
    angles = token_positions[..., None] * spectrum
    cosine = jnp.cos(angles)[..., None, :]
    sine_part = jnp.sin(angles)[..., None, :]
    former = tensor[..., :halfway]
    latter = tensor[..., halfway:]
    return jnp.concatenate(
        [former * cosine - latter * sine_part, latter * cosine + former * sine_part], axis=-1
    )


def take_rows(source_rows, row_ids):
    return source_rows[row_ids]


def split_into_heads(cache_rows, kv_heads):
    key_width = cache_rows.shape[-1] // 2
    leading = cache_rows.shape[:-1]
    head_shape = leading + (kv_heads, key_width // kv_heads)
    return (
        cache_rows[..., :key_width].reshape(head_shape),
        cache_rows[..., key_width:].reshape(head_shape),
    )


def attend(grouped_query, key_head_rows, value_head_rows, allowed):
    scores = jnp.einsum(
        "skgd,lkd->kgsl", grouped_query, key_head_rows, preferred_element_type=jnp.float32
    ) * grouped_query.shape[-1] ** (-0.5)
    scores = jnp.where(allowed[None, None], scores, MASKED)
    highest = jnp.max(scores, axis=-1)
    weights = jnp.exp(scores - highest[..., None])
    totals = jnp.sum(weights, axis=-1)
    summed = jnp.einsum(
        "kgsl,lkd->kgsd", weights, value_head_rows.astype(jnp.float32), precision=PRECISE
    )
    return (highest, totals, summed)


def blend(first_part, second_part):
    highest = jnp.maximum(first_part[0], second_part[0])
    first_factor = jnp.exp(first_part[0] - highest)
    second_factor = jnp.exp(second_part[0] - highest)
    totals = first_part[1] * first_factor + second_part[1] * second_factor
    summed = first_part[2] * first_factor[..., None] + second_part[2] * second_factor[..., None]
    return summed / totals[..., None]


def per_device(
    hidden,
    parents,
    path,
    cache_len,
    page_table,
    kv_pool,
    mig_slot,
    mig_dest,
    attn_gain,
    w_qkv,
    w_out,
    moe_gain,
    w_router,
    expert_ids,
    w_gate,
    w_up,
    w_down,
):
    cache_slot_count, draft_length = parents.shape
    req_count = lax.axis_size("req")
    ep_count = lax.axis_size("ep")
    device_count = req_count * ep_count
    query_width = w_out.shape[0]
    kv_width = kv_pool.shape[2]
    key_width = kv_width // 2
    context = page_table.shape[1] * kv_pool.shape[1]
    query_group_width = QUERY_HEADS // KEY_VALUE_HEADS
    model_dim = hidden.shape[1]
    tree_reach = jax.vmap(ancestry)(parents)
    tree_depth = jnp.sum(tree_reach, axis=-1) - 1.0
    leaving_slot = mig_slot[0]
    destination = mig_dest[0]
    ep_ids = jnp.arange(ep_count, dtype=jnp.int32)
    to_dest = ep_ids == destination
    own_cache = kv_pool[page_table].reshape(cache_slot_count, context, kv_width)
    leaving = lax.dynamic_index_in_dim(own_cache, leaving_slot, 0, keepdims=False)
    leave_len = lax.dynamic_index_in_dim(cache_len, leaving_slot, 0, keepdims=False)
    context_ids = jnp.arange(context, dtype=jnp.int32)
    normed = rms_scale(hidden, attn_gain)
    projected_input = jnp.dot(normed, w_qkv, preferred_element_type=jnp.float32).reshape(
        cache_slot_count, draft_length, -1
    )
    outgoing = jnp.where(to_dest[:, None, None], leaving[None], jnp.zeros((), jnp.bfloat16))
    length_out = jnp.where(to_dest, leave_len, 0)
    arrived_pages, arrived_lens = (
        lax.all_to_all(outgoing, "ep", split_axis=0, concat_axis=0, tiled=True),
        lax.all_to_all(length_out, "ep", split_axis=0, concat_axis=0, tiled=True),
    )
    anchor_ep = jnp.sum(jnp.where(arrived_lens > 0, ep_ids, 0))
    lengths = cache_len.at[leaving_slot].set(jnp.sum(arrived_lens))
    paged_caches = own_cache.at[leaving_slot].set(
        lax.dynamic_index_in_dim(arrived_pages, anchor_ep, 0, keepdims=False)
    )
    token_positions = lengths.astype(jnp.float32)[:, None] + tree_depth
    query_rows = apply_rotary(
        projected_input[..., :query_width].reshape(
            cache_slot_count, draft_length, QUERY_HEADS, HEAD_SIZE
        ),
        token_positions,
    ).astype(jnp.bfloat16)
    newest_keys = apply_rotary(
        projected_input[..., query_width : query_width + key_width].reshape(
            cache_slot_count, draft_length, KEY_VALUE_HEADS, HEAD_SIZE
        ),
        token_positions,
    ).astype(jnp.bfloat16)
    newest_values = projected_input[..., query_width + key_width :].astype(jnp.bfloat16)
    query_rows, newest_keys, newest_values = (
        query_rows.reshape(
            cache_slot_count, draft_length, KEY_VALUE_HEADS, query_group_width, HEAD_SIZE
        ),
        newest_keys,
        newest_values.reshape(cache_slot_count, draft_length, KEY_VALUE_HEADS, HEAD_SIZE),
    )
    stored_keys, stored_values = split_into_heads(paged_caches, KEY_VALUE_HEADS)
    cache_part = jax.vmap(attend)(
        query_rows,
        stored_keys,
        stored_values,
        jnp.broadcast_to(
            context_ids[None, None, :] < lengths[:, None, None],
            (cache_slot_count, draft_length, context),
        ),
    )
    draft_part = jax.vmap(attend)(query_rows, newest_keys, newest_values, tree_reach > 0.5)
    mixed = blend(cache_part, draft_part)
    attended = (
        jnp.transpose(mixed, (0, 3, 1, 2, 4))
        .reshape(cache_slot_count * draft_length, query_width)
        .astype(jnp.bfloat16)
    )
    projected_out = jnp.dot(attended, w_out, preferred_element_type=jnp.float32)
    residual_mid = (hidden.astype(jnp.float32) + projected_out).astype(jnp.bfloat16)
    fresh_kv = jnp.concatenate(
        [
            newest_keys.reshape(cache_slot_count, draft_length, key_width),
            newest_values.reshape(cache_slot_count, draft_length, key_width),
        ],
        axis=-1,
    )
    picked_kv = jax.vmap(take_rows)(fresh_kv, jnp.maximum(path, 0))
    compact_kv = jnp.where((path >= 0)[..., None], picked_kv, jnp.zeros((), jnp.bfloat16))
    normed_moe = rms_scale(residual_mid, moe_gain)
    logits = jnp.dot(normed_moe, w_router, preferred_element_type=jnp.float32)
    experts = w_router.shape[1]
    split = device_count // experts
    chosen = jnp.take_along_axis(logits, expert_ids, axis=1)
    squashed = jax.nn.sigmoid(chosen)
    gate_share = squashed / jnp.sum(squashed, axis=1, keepdims=True)
    marks = expert_ids[:, :, None] == jnp.arange(experts, dtype=jnp.int32)[None, None, :]
    assigned = jnp.sum(marks.astype(jnp.int32), axis=1)
    ranks = jnp.cumsum(assigned, axis=0) - assigned
    slot_ids = jnp.arange(CAP, dtype=jnp.int32)
    dispatch_table = (
        (ranks.T[:, None, :] == slot_ids[None, :, None]) & (assigned.T[:, None, :] > 0)
    ).astype(jnp.bfloat16)
    packed = jnp.einsum(
        "ect,td->ecd", dispatch_table, normed_moe, preferred_element_type=jnp.float32
    ).astype(jnp.bfloat16)
    outgoing_rows = jnp.repeat(packed, split, axis=0)
    tok_rows = lax.all_to_all(outgoing_rows, ("req", "ep"), split_axis=0, concat_axis=0, tiled=True)
    flat_rows = tok_rows.reshape(-1, model_dim)
    gate_val = jnp.dot(flat_rows, w_gate[0], preferred_element_type=jnp.float32)
    up_val = jnp.dot(flat_rows, w_up[0], preferred_element_type=jnp.float32)
    activated = (jnp.maximum(gate_val, 0.0) * up_val).astype(jnp.bfloat16)
    result = jnp.dot(activated, w_down[0], preferred_element_type=jnp.float32).astype(jnp.bfloat16)
    returned = lax.all_to_all(
        result.reshape(tok_rows.shape), ("req", "ep"), split_axis=0, concat_axis=0, tiled=True
    )
    expert_out = jnp.sum(
        returned.astype(jnp.float32).reshape(experts, split, CAP, model_dim), axis=1
    ).reshape(experts * CAP, model_dim)
    slot_pick = expert_ids * CAP + jnp.take_along_axis(ranks, expert_ids, axis=1)
    gathered_rows = expert_out[slot_pick]
    moe_sum = jnp.sum(gate_share[..., None] * gathered_rows, axis=1)
    layer_out = (residual_mid.astype(jnp.float32) + moe_sum).astype(jnp.bfloat16)
    return (layer_out, compact_kv)


def solution(mesh):
    in_specs = (
        P(("req", "ep"), None),
        P(("req", "ep"), None),
        P(("req", "ep"), None),
        P(("req", "ep")),
        P(("req", "ep"), None),
        P(("req", "ep"), None, None),
        P(("req", "ep")),
        P(("req", "ep")),
        P(),
        P(),
        P(),
        P(),
        P(),
        P(("req", "ep"), None),
        P(("req", "ep"), None, None),
        P(("req", "ep"), None, None),
        P(("req", "ep"), None, None),
    )
    out_specs = (P(("req", "ep"), None), P(("req", "ep"), None, None))
    return jax.shard_map(
        per_device, mesh=mesh, in_specs=in_specs, out_specs=out_specs, check_vma=False
    )
```

profile of v0, /device:TPU:0, one launch (start us, length us, event | category | flops | bytes accessed | tf_op | source)
XLA Modules:
  0.0 289.2 jit_solution(7695748653599515473)
XLA Ops:
  4.5 4.2 %all-to-all-start = ((s32[4,1,1]{2,1,0:T(1,128)}), s32[4,1,1]{2,1,0:T(1,128)S(1)}, u32[]{:S(2)}, u32[]{:S(2)}) async-start(s32[4,1,1]{2,1,0:T(1,128)} %compare_select_fusion), calls=%async_computation | async-start | bytes 4096 | tf_op jit(solution)/shard_map/all_to_all | solution.py:133
  9.5 3.7 %gather_fusion = bf16[16,128,512]{2,1,0:T(8,128)(2,1)} fusion(bf16[16,128,512]{2,1,0:T(8,128)(2,1)} %param.26, s32[1024]{0:T(1024)S(1)} %pad_clamp_fusion.1), kind=kCustom, calls=%fused_computation | custom fusion | bytes 4194368 | tf_op jit(solution)/shard_map/gather | solution.py:121
  13.2 1.3 dynamic-slice_bitcast_fusion
  15.7 2.3 broadcast_select_fusion
  19.9 4.8 %all-to-all-start.1 = ((bf16[4,1024,512]{2,1,0:T(8,128)(2,1)}), bf16[4,1024,512]{2,1,0:T(8,128)(2,1)}, u32[]{:S(2)}, u32[]{:S(2)}) async-start(bf16[4,1024,512]{2,1,0:T(8,128)(2,1)} %broadcast_select_fusion), calls=%async_computation.1 | async-start | bytes 8388608 | tf_op jit(solution)/shard_map/all_to_all | solution.py:132
  30.0 1.6 reshape.265
  31.6 1.5 reshape.266
  38.0 1.4 and_reduce_fusion
  40.1 1.9 fusion.69
  45.9 2.3 fusion.58
  54.7 18.3 %all-to-all-done.1 = bf16[4,1024,512]{2,1,0:T(8,128)(2,1)} async-done(((bf16[4,1024,512]{2,1,0:T(8,128)(2,1)}), bf16[4,1024,512]{2,1,0:T(8,128)(2,1)}, u32[]{:S(2)}, u32[]{:S(2)}) %all-to-all-start.1) | async-done | bytes 4194336 | tf_op jit(solution)/shard_map/all_to_all | solution.py:132
  73.0 3.5 %select_dynamic-update-slice_fusion = bf16[2,1024,512]{2,1,0:T(8,128)(2,1)} fusion(bf16[2,1024,512]{2,1,0:T(8,128)(2,1)} %bitcast.140, s32[]{:T(128)} %select_n.71, bf16[4,1024,512]{2,1,0:T(8,128)(2,1)} %all-to-all-done.1, s32[]{:T(128)S(6)} %select_n.77, pred[]{:T(512)} %and_reduce_fusion), kind=kLoop, calls=%fused_computation.49 | loop fusion | flops 524288 | bytes 3146756 | tf_op jit(solution)/shard_map/scatter | solution.py:137
  76.5 2.6 fusion.68
  79.2 1.3 copy.154
  80.5 1.5 copy.148
  82.0 2.4 bitcast_reduce_fusion
  84.4 1.8 fusion.1
  86.2 4.0 %fusion.25 = f32[2,64,2,6,128]{4,1,3,2,0:T(8,128)S(1)} fusion(bf16[2,1024,2,128,1]{1,3,4,2,0:T(8,128)(2,1)S(1)} %bitcast.152, f32[2,2,1024,64,6]{2,3,4,1,0:T(8,128)S(1)} %get-tuple-element.42, f32[2,2,6,64]{3,2,1,0:T(8,128)S(1)} %get-tuple-element.41, pred[2,1024]{1,0:T(4,128)(4,1)S(1)} %iota_compare_fusion.5, f32[2,64,2,6]{1,3,2,0:T(8,128)S(1)} %get-tuple-element.28), kind=kOutput, calls=%fused_computation.37 | convolution fusion | flops 2420834304 | bytes 8140800 | tf_op jit(solution)/shard_map/vmap(kgsl,lkd->kgsd)/dot_general | solution.py:71
  92.8 3.4 %multiply_reduce_fusion.1 = (f32[128]{0:T(128)S(1)}, f32[128,1536]{1,0:T(8,128)S(1)}) fusion(bf16[128,1536]{1,0:T(8,128)(2,1)} %convert_element_type.79, bf16[1536,1536]{1,0:T(8,128)(2,1)} %param.31, bf16[128,1536]{1,0:T(8,128)(2,1)} %param.21), kind=kOutput, calls=%fused_computation.56 | convolution fusion | flops 605159296 | bytes 6291968 | tf_op jit(solution)/shard_map/dot_general | solution.py:178
  97.3 76.3 %all_to_all.21 = bf16[32,32,1536]{2,1,0:T(8,128)(2,1)S(1)} all-to-all(bf16[32,32,1536]{2,1,0:T(8,128)(2,1)S(1)} %convolution_convert_fusion.1), channel_id=1, replica_groups=mesh['req'=8,'ep'=4] {'req','ep'}, dimensions={0} | all-to-all | bytes 6291456 | tf_op jit(solution)/shard_map/all_to_all | solution.py:207
  173.6 1.7 copy-done.7
  175.3 4.3 %fusion.11 = f32[1024,768]{1,0:T(8,128)} fusion(bf16[1024,1536]{1,0:T(8,128)(2,1)S(1)} %bitcast.150, bf16[1,1536,768]{2,1,0:T(8,128)(2,1)S(1)} %copy-done.30), kind=kOutput, calls=%fused_computation.25 | convolution fusion | flops 2415919104 | bytes 8650752 | tf_op jit(solution)/shard_map/dot_general | solution.py:210
  179.6 11.2 %convolution_convert_fusion = bf16[1024,1536]{1,0:T(8,128)(2,1)} fusion(bf16[1,768,1536]{2,1,0:T(8,128)(2,1)S(1)} %copy-done, f32[1024,768]{1,0:T(8,128)} %fusion.11, bf16[1024,1536]{1,0:T(8,128)(2,1)} %bitcast.151, bf16[1,1536,768]{2,1,0:T(8,128)(2,1)} %param.35), kind=kOutput, calls=%fused_computation.12 | convolution fusion | flops 4835770368 | bytes 14155776 | tf_op jit(solution)/shard_map/dot_general | solution.py:212
  190.8 4.0 %all-to-all-start.3 = ((bf16[32,32,1536]{2,1,0:T(8,128)(2,1)}), bf16[32,32,1536]{2,1,0:T(8,128)(2,1)}, u32[]{:S(2)}, u32[]{:S(2)}) async-start(bf16[32,32,1536]{2,1,0:T(8,128)(2,1)} %bitcast.149), calls=%async_computation.3 | async-start | bytes 6291456 | tf_op jit(solution)/shard_map/all_to_all | solution.py:213
  195.1 3.8 %gather_fusion.3 = s32[512]{0:T(512)S(1)} fusion(s32[128,32]{1,0:T(8,128)S(1)} %sub.66, s32[512]{0:T(512)S(1)} %reshape.290), kind=kCustom, calls=%fused_computation.3 | custom fusion | bytes 8192 | tf_op jit(solution)/shard_map/jit(take_along_axis)/gather | solution.py:219
  199.6 1.3 gather_fusion.4
  202.0 3.8 %gather_fusion.2 = f32[512]{0:T(512)S(1)} fusion(f32[128,32]{0,1:T(8,128)S(1)} %fusion.65, s32[512]{0:T(512)S(1)} %reshape.290), kind=kCustom, calls=%fused_computation.2 | custom fusion | bytes 8192 | tf_op jit(solution)/shard_map/jit(take_along_axis)/gather | solution.py:193
  206.1 60.2 %all-to-all-done.3 = bf16[32,32,1536]{2,1,0:T(8,128)(2,1)} async-done(((bf16[32,32,1536]{2,1,0:T(8,128)(2,1)}), bf16[32,32,1536]{2,1,0:T(8,128)(2,1)}, u32[]{:S(2)}, u32[]{:S(2)}) %all-to-all-start.3) | async-done | bytes 3145760 | tf_op jit(solution)/shard_map/all_to_all | solution.py:213
  266.3 5.4 %bitcast_convert_fusion = f32[1024,1536]{1,0:T(8,128)} fusion(bf16[32,32,1536]{2,1,0:T(8,128)(2,1)} %all-to-all-done.3), kind=kLoop, calls=%fused_computation.14 | loop fusion | flops 1572864 | bytes 9437184 | tf_op jit(solution)/shard_map/reshape | solution.py:218
  271.8 7.4 %gather_fusion.1 = f32[512,1536]{1,0:T(8,128)} fusion(f32[1024,1536]{1,0:T(8,128)} %bitcast_convert_fusion, s32[1024]{0:T(1024)S(1)} %pad_clamp_fusion), kind=kCustom, calls=%fused_computation.1 | custom fusion | bytes 6293504 | tf_op jit(solution)/shard_map/gather | solution.py:220
  279.2 5.0 %reshape.283 = f32[128,4,1536]{2,1,0:T(4,128)} reshape(f32[512,1536]{1,0:T(8,128)} %gather_fusion.1) | data formatting | bytes 6291456 | tf_op jit(solution)/shard_map/gather | solution.py:220
  284.1 4.2 %multiply_reduce_fusion = f32[128,1536]{1,0:T(8,128)S(1)} fusion(f32[128,4,1536]{2,1,0:T(4,128)} %reshape.283, f32[128,4]{1,0:T(8,128)S(1)} %copy.164), kind=kLoop, calls=%fused_computation.15 | loop fusion | flops 1376256 | bytes 3934208 | tf_op jit(solution)/shard_map/reduce_sum | solution.py:221
  (135 shorter events, 32.2 us)
Async XLA Ops:
  0.6 179.0 %copy-start = (bf16[1,768,1536]{2,1,0:T(8,128)(2,1)S(1)}, bf16[1,768,1536]{2,1,0:T(8,128)(2,1)}, u32[]{:S(2)}) copy-start(bf16[1,768,1536]{2,1,0:T(8,128)(2,1)} %param.37) | copy-start | bytes 7077892
  1.5 7.3 %copy-start.28 = (s32[2]{0:T(128)}, s32[2]{0:T(128)S(1)}, u32[]{:S(2)}) copy-start(s32[2]{0:T(128)S(1)} %copy.199) | copy-start | bytes 28
  4.5 14.9 %all-to-all-start = ((s32[4,1,1]{2,1,0:T(1,128)}), s32[4,1,1]{2,1,0:T(1,128)S(1)}, u32[]{:S(2)}, u32[]{:S(2)}) async-start(s32[4,1,1]{2,1,0:T(1,128)} %compare_select_fusion), calls=%async_computation | async-start | bytes 4096 | tf_op jit(solution)/shard_map/all_to_all | solution.py:133
  9.5 5.1 %copy-start.25 = (bf16[1536]{0:T(1024)(128)(2,1)S(1)}, bf16[1536]{0:T(1024)(128)(2,1)}, u32[]{:S(2)}) copy-start(bf16[1536]{0:T(1024)(128)(2,1)} %param.29) | copy-start | bytes 9220
  9.5 5.1 %copy-start.3 = (bf16[128,1536]{1,0:T(8,128)(2,1)S(1)}, bf16[128,1536]{1,0:T(8,128)(2,1)}, u32[]{:S(2)}) copy-start(bf16[128,1536]{1,0:T(8,128)(2,1)} %param.21) | copy-start | bytes 1179652
  9.5 5.3 %copy-start.26 = (s32[2,64]{1,0:T(2,128)S(1)}, s32[2,64]{1,0:T(2,128)}, u32[]{:S(2)}) copy-start(s32[2,64]{1,0:T(2,128)} %param.22) | copy-start | bytes 1540
  13.2 4.8 %copy-start.4 = (bf16[128,1536]{1,0:T(8,128)(2,1)S(1)}, bf16[128,1536]{1,0:T(8,128)(2,1)}, u32[]{:S(2)}) copy-start(bf16[128,1536]{1,0:T(8,128)(2,1)} %param.21) | copy-start | bytes 1179652
  14.6 3.7 %copy-start.2 = (bf16[1536,2048]{1,0:T(8,128)(2,1)S(1)}, bf16[1536,2048]{1,0:T(8,128)(2,1)}, u32[]{:S(2)}) copy-start(bf16[1536,2048]{1,0:T(8,128)(2,1)} %param.30) | copy-start | bytes 18874372
  19.9 53.1 %all-to-all-start.1 = ((bf16[4,1024,512]{2,1,0:T(8,128)(2,1)}), bf16[4,1024,512]{2,1,0:T(8,128)(2,1)}, u32[]{:S(2)}, u32[]{:S(2)}) async-start(bf16[4,1024,512]{2,1,0:T(8,128)(2,1)} %broadcast_select_fusion), calls=%async_computation.1 | async-start | bytes 8388608 | tf_op jit(solution)/shard_map/all_to_all | solution.py:132
  40.1 12.9 %copy-start.20 = (pred[2,64,64]{1,2,0:T(8,128)(4,1)S(1)}, pred[2,64,64]{1,2,0:T(8,128)(4,1)}, u32[]{:S(2)}) copy-start(pred[2,64,64]{1,2,0:T(8,128)(4,1)} %copy.156) | copy-start | bytes 24580
  51.0 3.6 %copy-start.29 = (s32[2]{0:T(128)S(1)}, s32[2]{0:T(128)}, u32[]{:S(2)}) copy-start(s32[2]{0:T(128)} %fusion.58) | copy-start | bytes 28
  51.1 21.9 %copy-start.5 = (bf16[2,64,12,64]{3,1,2,0:T(8,128)(2,1)}, bf16[2,64,12,64]{3,1,2,0:T(8,128)(2,1)S(1)}, u32[]{:S(2)}) copy-start(bf16[2,64,12,64]{3,1,2,0:T(8,128)(2,1)S(1)} %copy.152) | copy-start | bytes 589828
  51.3 21.8 %copy-start.6 = (bf16[2,64,12,64]{3,1,2,0:T(8,128)(2,1)}, bf16[2,64,12,64]{3,1,2,0:T(8,128)(2,1)S(1)}, u32[]{:S(2)}) copy-start(bf16[2,64,12,64]{3,1,2,0:T(8,128)(2,1)S(1)} %copy.151) | copy-start | bytes 589828
  52.9 20.1 %copy-start.13 = (bf16[2,64,2,64]{3,1,2,0:T(8,128)(2,1)}, bf16[2,64,2,64]{3,1,2,0:T(8,128)(2,1)S(1)}, u32[]{:S(2)}) copy-start(bf16[2,64,2,64]{3,1,2,0:T(8,128)(2,1)S(1)} %get-tuple-element.33) | copy-start | bytes 98308
  52.9 20.1 %copy-start.15 = (bf16[2,64,2,64]{3,1,2,0:T(8,128)(2,1)}, bf16[2,64,2,64]{3,1,2,0:T(8,128)(2,1)S(1)}, u32[]{:S(2)}) copy-start(bf16[2,64,2,64]{3,1,2,0:T(8,128)(2,1)S(1)} %get-tuple-element.34) | copy-start | bytes 98308
  53.6 0.9 copy-start.8
  84.4 1.8 copy-start.10
  86.2 4.0 %copy-start.9 = (f32[2,2,6,64,64]{3,4,2,1,0:T(8,128)S(1)}, f32[2,2,6,64,64]{3,4,2,1,0:T(8,128)}, u32[]{:S(2)}) copy-start(f32[2,2,6,64,64]{3,4,2,1,0:T(8,128)} %copy-done.8) | copy-start | bytes 1179652
  86.2 4.0 %copy-start.21 = (bf16[2,64,2,128]{3,2,1,0:T(2,128)(2,1)S(1)}, bf16[2,64,2,128]{3,2,1,0:T(2,128)(2,1)}, u32[]{:S(2)}) copy-start(bf16[2,64,2,128]{3,2,1,0:T(2,128)(2,1)} %reshape.266) | copy-start | bytes 196612
  92.8 3.5 %copy-start.18 = (f32[1536]{0:T(1024)S(1)}, f32[1536]{0:T(1024)}, u32[]{:S(2)}) copy-start(f32[1536]{0:T(1024)} %convert_element_type.82) | copy-start | bytes 18436
  92.8 3.5 %copy-start.19 = (s32[32,128]{1,0:T(8,128)S(1)}, s32[32,128]{1,0:T(8,128)}, u32[]{:S(2)}) copy-start(s32[32,128]{1,0:T(8,128)} %copy.167) | copy-start | bytes 49156
  92.8 3.5 %copy-start.24 = (pred[32,128]{1,0:T(8,128)(4,1)S(1)}, pred[32,128]{1,0:T(8,128)(4,1)}, u32[]{:S(2)}) copy-start(pred[32,128]{1,0:T(8,128)(4,1)} %compare_bitcast_fusion) | copy-start | bytes 12292
  97.3 78.0 %copy-start.30 = (bf16[1,1536,768]{2,1,0:T(8,128)(2,1)S(1)}, bf16[1,1536,768]{2,1,0:T(8,128)(2,1)}, u32[]{:S(2)}) copy-start(bf16[1,1536,768]{2,1,0:T(8,128)(2,1)} %param.36) | copy-start | bytes 7077892
  173.6 1.7 copy-start.7
  190.8 4.1 %copy-start.22 = (s32[128,4]{0,1:T(4,128)S(1)}, s32[128,4]{0,1:T(4,128)}, u32[]{:S(2)}) copy-start(s32[128,4]{0,1:T(4,128)} %param.34) | copy-start | bytes 6148
  190.8 75.6 %all-to-all-start.3 = ((bf16[32,32,1536]{2,1,0:T(8,128)(2,1)}), bf16[32,32,1536]{2,1,0:T(8,128)(2,1)}, u32[]{:S(2)}, u32[]{:S(2)}) async-start(bf16[32,32,1536]{2,1,0:T(8,128)(2,1)} %bitcast.149), calls=%async_computation.3 | async-start | bytes 6291456 | tf_op jit(solution)/shard_map/all_to_all | solution.py:213
  195.1 4.3 %copy-start.27 = (s32[2,64]{1,0:T(2,128)S(1)}, s32[2,64]{1,0:T(2,128)}, u32[]{:S(2)}) copy-start(s32[2,64]{1,0:T(2,128)} %param.23) | copy-start | bytes 1540
  195.1 4.4 %copy-start.14 = (bf16[2,64,2,64]{3,1,2,0:T(8,128)(2,1)S(1)}, bf16[2,64,2,64]{3,1,2,0:T(8,128)(2,1)}, u32[]{:S(2)}) copy-start(bf16[2,64,2,64]{3,1,2,0:T(8,128)(2,1)} %copy-done.13) | copy-start | bytes 98308
  195.1 4.4 %copy-start.16 = (bf16[2,64,2,64]{3,1,2,0:T(8,128)(2,1)S(1)}, bf16[2,64,2,64]{3,1,2,0:T(8,128)(2,1)}, u32[]{:S(2)}) copy-start(bf16[2,64,2,64]{3,1,2,0:T(8,128)(2,1)} %copy-done.15) | copy-start | bytes 98308
  195.1 4.5 %copy-start.11 = (bf16[2,64,256]{2,1,0:T(8,128)(2,1)S(1)}, bf16[2,64,256]{2,1,0:T(8,128)(2,1)}, u32[]{:S(2)}) copy-start(bf16[2,64,256]{2,1,0:T(8,128)(2,1)} %slice.89) | copy-start | bytes 196612
  195.1 6.6 %copy-start.17 = (bf16[1536,32]{0,1:T(8,128)(2,1)S(1)}, bf16[1536,32]{0,1:T(8,128)(2,1)}, u32[]{:S(2)}) copy-start(bf16[1536,32]{0,1:T(8,128)(2,1)} %param.33) | copy-start | bytes 294916
  279.2 10.0 %copy-start.1 = (bf16[1,768,1536]{2,1,0:T(8,128)(2,1)S(1)}, bf16[1,768,1536]{2,1,0:T(8,128)(2,1)}, u32[]{:S(2)}) copy-start(bf16[1,768,1536]{2,1,0:T(8,128)(2,1)} %param.37) | copy-start | bytes 7077892
  (2 other events, 1.2 us)
where the time goes:
time: 290 us; the launch traced here: 289 us
  waiting for transfers between devices  78.6 us (27%)
  blocking collectives  76.3 us (26%)
  local copies, waits for them, and re-layouts  49.3 us (17%)
  other arithmetic  36.2 us (12%)
  matrix products  31.2 us (11%)
  starting transfers between devices  13.1 us (5%)
  between operations  4.49 us (2%)
    all_to_all x1, blocking collectives, per_device(): lax.all_to_all(outgoing_rows, ('req', 'ep'), split_axis=0, concat_axis=0,...  76.3 us
    all_to_all x1, waiting for transfers between devices, per_device(): lax.all_to_all(result.reshape(tok_rows.shape), ('req', 'ep'), split_axis=...  60.2 us
    all_to_all x1, waiting for transfers between devices, per_device(): lax.all_to_all(outgoing, 'ep', split_axis=0, concat_axis=0, tiled=True)  18.3 us
    gather x2, local copies, waits for them, and re-layouts, per_device(): gathered_rows = expert_out[slot_pick]  12.4 us
    dot_general x1, matrix products, per_device(): jnp.dot(activated, w_down[0], preferred_element_type=jnp.float32)  11.2 us
  transfers between devices with their start and end apart: 3, of which 2 were waited for; matrix products, arithmetic and copies ran while one was open for 17% of the time, Pallas kernels for 0%

commit v1 on v0

v1 whole, which is shorter than its diff:
```python
import functools

import jax
import jax.numpy as jnp
import numpy as np
from jax import lax
from jax.experimental import pallas as pl
from jax.experimental.pallas import tpu as pltpu
from jax.sharding import PartitionSpec as P

QUERY_HEADS = 12
KEY_VALUE_HEADS = 2
HEAD_SIZE = 128
GROUP = QUERY_HEADS // KEY_VALUE_HEADS
CAP = 32
EPSILON = 1e-06
ROPE_BASE = 1000000.0
MASKED = -1e30
MIB = 1024 * 1024
AXES = ("req", "ep")

VMEM = pl.BlockSpec(memory_space=pltpu.VMEM)
SMEM = pl.BlockSpec(memory_space=pltpu.SMEM)
ANY = pl.BlockSpec(memory_space=pl.ANY)


def dot(a, b, dims=((1,), (0,))):
    return lax.dot_general(a, b, (dims, ((), ())), preferred_element_type=jnp.float32)


def rms_scale(values, scaling):
    widened = values.astype(jnp.float32)
    spread = jnp.mean(widened * widened, axis=-1, keepdims=True)
    return (widened * lax.rsqrt(spread + EPSILON) * scaling.astype(jnp.float32)).astype(
        jnp.bfloat16
    )


def attend(queries, cached, fresh, reach, length):
    scale = HEAD_SIZE ** (-0.5)
    key_width = KEY_VALUE_HEADS * HEAD_SIZE
    context = cached.shape[0]
    rows = queries.shape[0] * GROUP
    in_cache = lax.broadcasted_iota(jnp.int32, (rows, context), 1) < length
    in_tree = jnp.concatenate([reach] * GROUP, axis=0) > 0.5
    outs = []
    for kv in range(KEY_VALUE_HEADS):
        cols = slice(kv * HEAD_SIZE, (kv + 1) * HEAD_SIZE)
        vcols = slice(key_width + kv * HEAD_SIZE, key_width + (kv + 1) * HEAD_SIZE)
        heads = [
            queries[:, (kv * GROUP + g) * HEAD_SIZE : (kv * GROUP + g + 1) * HEAD_SIZE]
            for g in range(GROUP)
        ]
        stacked = jnp.concatenate(heads, axis=0)
        first = dot(stacked, cached[:, cols], ((1,), (1,))) * scale
        first = jnp.where(in_cache, first, MASKED)
        second = dot(stacked, fresh[:, cols], ((1,), (1,))) * scale
        second = jnp.where(in_tree, second, MASKED)
        highest = jnp.maximum(
            jnp.max(first, axis=-1, keepdims=True), jnp.max(second, axis=-1, keepdims=True)
        )
        first = jnp.exp(first - highest)
        second = jnp.exp(second - highest)
        total = jnp.sum(first, axis=-1, keepdims=True) + jnp.sum(second, axis=-1, keepdims=True)
        mixed = dot(first.astype(jnp.bfloat16), cached[:, vcols])
        mixed = mixed + dot(second.astype(jnp.bfloat16), fresh[:, vcols])
        mixed = (mixed / total).astype(jnp.bfloat16)
        step = queries.shape[0]
        outs += [mixed[g * step : (g + 1) * step] for g in range(GROUP)]
    return jnp.concatenate(outs, axis=1)


def leaving_kernel(meta, table, pool, out, sems):
    slot = meta[0]
    page = pool.shape[1]
    copies = []
    for i in range(table.shape[1]):
        copies.append(
            pltpu.make_async_copy(
                pool.at[table[slot, i]], out.at[pl.ds(i * page, page)], sems.at[i]
            )
        )
    for copy in copies:
        copy.start()
    for copy in copies:
        copy.wait()


def routes_kernel(base, split, ids_t, table):
    tokens = ids_t.shape[1]
    shown = table.shape[0] // (split * CAP)
    names = lax.broadcasted_iota(jnp.int32, (shown, tokens), 0) + base[0]
    assigned = jnp.zeros((shown, tokens), jnp.bool_)
    for k in range(ids_t.shape[0]):
        assigned = assigned | (ids_t[k : k + 1, :] == names)
    before = lax.broadcasted_iota(jnp.int32, (tokens, tokens), 0) < lax.broadcasted_iota(
        jnp.int32, (tokens, tokens), 1
    )
    ones = assigned.astype(jnp.float32)
    ranks = dot(ones.astype(jnp.bfloat16), before.astype(jnp.float32).astype(jnp.bfloat16))
    slots = jnp.where(assigned, ranks.astype(jnp.int32), -1)
    wanted = lax.broadcasted_iota(jnp.int32, (shown, split * CAP, tokens), 1) % CAP
    hot = jnp.where(slots[:, None, :] == wanted, 1.0, 0.0)
    table[...] = hot.reshape(table.shape).astype(jnp.bfloat16)


def shares_kernel(base, split, experts, normed, w_router, ids, high, low):
    tokens = ids.shape[0]
    width = high.shape[1]
    shown = width // (split * CAP)
    logits = dot(normed[...], w_router[...])
    names = lax.broadcasted_iota(jnp.int32, (tokens, experts), 1)
    assigned = jnp.zeros((tokens, experts), jnp.bool_)
    for k in range(ids.shape[1]):
        assigned = assigned | (ids[:, k : k + 1] == names)
    squashed = jnp.where(assigned, jax.nn.sigmoid(logits), 0.0)
    share = squashed / jnp.sum(squashed, axis=1, keepdims=True)
    before = lax.broadcasted_iota(jnp.int32, (tokens, tokens), 1) < lax.broadcasted_iota(
        jnp.int32, (tokens, tokens), 0
    )
    ones = assigned.astype(jnp.float32).astype(jnp.bfloat16)
    ranks = dot(before.astype(jnp.float32).astype(jnp.bfloat16), ones)
    slots = jnp.where(assigned, ranks, -1.0).astype(jnp.bfloat16)
    spread = (
        lax.broadcasted_iota(jnp.int32, (experts, width), 1) // (split * CAP) + base[0]
        == lax.broadcasted_iota(jnp.int32, (experts, width), 0)
    )
    spread = spread.astype(jnp.float32).astype(jnp.bfloat16)
    wanted = lax.broadcasted_iota(jnp.int32, (tokens, width), 1) % CAP
    hit = dot(slots, spread).astype(jnp.int32) == wanted
    share_high = share.astype(jnp.bfloat16)
    share_low = (share - share_high.astype(jnp.float32)).astype(jnp.bfloat16)
    high[...] = jnp.where(hit, dot(share_high, spread), 0.0).astype(jnp.bfloat16)
    low[...] = jnp.where(hit, dot(share_low, spread), 0.0).astype(jnp.bfloat16)


def front_kernel(
    meta, table, hidden, parents, path, spectrum, gain, w_qkv, w_out, pool,
    queries, fresh, reach, compact, staying, cache, sems,
):
    stay = 1 - meta[0]
    page = pool.shape[1]
    copies = []
    for i in range(table.shape[1]):
        copies.append(
            pltpu.make_async_copy(
                pool.at[table[stay, i]], cache.at[pl.ds(i * page, page)], sems.at[i]
            )
        )
    for copy in copies:
        copy.start()
    requests = meta.shape[0] - 1
    draft = hidden.shape[0] // requests
    query_width = queries.shape[1]
    key_width = KEY_VALUE_HEADS * HEAD_SIZE
    normed = rms_scale(hidden[...], gain[...])
    projected = dot(normed, w_qkv[...])
    names = lax.broadcasted_iota(jnp.int32, (draft, draft), 1)
    itself = names == lax.broadcasted_iota(jnp.int32, (draft, draft), 0)
    turned = lax.broadcasted_iota(jnp.int32, (1, HEAD_SIZE), 1) < HEAD_SIZE // 2
    for r in range(requests):
        rows = slice(r * draft, (r + 1) * draft)
        linked = parents[rows, :] == names
        reached = jnp.where(linked | itself, 1.0, 0.0)
        for _ in range(max(1, (draft - 1).bit_length())):
            half = reached.astype(jnp.bfloat16)
            reached = jnp.minimum(dot(half, half), 1.0)
        depth = jnp.sum(reached, axis=-1, keepdims=True) - 1.0
        angles = (depth + meta[1 + r].astype(jnp.float32)) * spectrum[...]
        cosine = jnp.cos(angles)
        sine = jnp.sin(angles)
        sine = jnp.where(turned, -sine, sine)
        for h in range(QUERY_HEADS + KEY_VALUE_HEADS):
            part = projected[rows, h * HEAD_SIZE : (h + 1) * HEAD_SIZE]
            swapped = jnp.concatenate(
                [part[:, HEAD_SIZE // 2 :], part[:, : HEAD_SIZE // 2]], axis=1
            )
            rotated = (part * cosine + swapped * sine).astype(jnp.bfloat16)
            if h < QUERY_HEADS:
                queries[rows, h * HEAD_SIZE : (h + 1) * HEAD_SIZE] = rotated
            else:
                at = (h - QUERY_HEADS) * HEAD_SIZE
                fresh[rows, at : at + HEAD_SIZE] = rotated
        fresh[rows, key_width:] = projected[rows, query_width + key_width :].astype(jnp.bfloat16)
        reach[rows, :] = reached
        picked = jnp.where(path[rows, :] == names, 1.0, 0.0).astype(jnp.bfloat16)
        compact[rows, :] = dot(picked, fresh[rows, :]).astype(jnp.bfloat16)
    for copy in copies:
        copy.wait()
    own = pl.ds(pl.multiple_of(stay * draft, draft), draft)
    attended = attend(queries[own, :], cache, fresh[own, :], reach[own, :], meta[1 + stay])
    projected_out = dot(attended, w_out[...])
    staying[...] = (hidden[own, :].astype(jnp.float32) + projected_out).astype(jnp.bfloat16)


def arrival_kernel(
    meta, select, hidden, queries, fresh, reach, staying, gain, routes, w_out, *rest,
):
    sources = rest[:-8]
    residual, normed, packed, cache, weights, sem, weight_sem, _ = rest[-8:]
    load = pltpu.make_async_copy(w_out, weights, weight_sem)
    load.start()
    for i, source in enumerate(sources):

        @pl.when(select[0] == i)
        def _(source=source):
            copy = pltpu.make_async_copy(source, cache, sem)
            copy.start()
            copy.wait()

    slot = meta[0]
    draft = staying.shape[0]
    own = pl.ds(pl.multiple_of(slot * draft, draft), draft)
    other = pl.ds(pl.multiple_of((1 - slot) * draft, draft), draft)
    attended = attend(queries[own, :], cache, fresh[own, :], reach[own, :], meta[1 + slot])
    load.wait()
    projected_out = dot(attended, weights[...])
    residual[own, :] = (hidden[own, :].astype(jnp.float32) + projected_out).astype(jnp.bfloat16)
    residual[other, :] = staying[...]
    scaled = rms_scale(residual[...], gain[...])
    normed[...] = scaled
    packed[...] = dot(routes[...], scaled).astype(jnp.bfloat16)


def pack_kernel(routes, normed, packed):
    packed[...] = dot(routes[...], normed[...]).astype(jnp.bfloat16)


def expert_kernel(rows, w_gate, w_up, w_down, out, total):
    step = pl.program_id(0)
    gated = dot(rows[...], w_gate[0])
    upped = dot(rows[...], w_up[0])
    activated = (jnp.maximum(gated, 0.0) * upped).astype(jnp.bfloat16)
    piece = dot(activated, w_down[0])

    @pl.when(step == 0)
    def _():
        total[...] = piece

    @pl.when(step > 0)
    def _():
        total[...] += piece

    @pl.when(step == pl.num_programs(0) - 1)
    def _():
        out[...] = total[...].astype(jnp.bfloat16)


def partial_kernel(high, low, rows, out):
    values = rows[...]
    out[...] = (dot(high[...], values) + dot(low[...], values)).astype(jnp.bfloat16)


def final_kernel(residual, high, low, rows, far, out):
    values = rows[...]
    total = dot(high[...], values) + dot(low[...], values) + far[...].astype(jnp.float32)
    out[...] = (residual[...].astype(jnp.float32) + total).astype(jnp.bfloat16)


def params(mib):
    return pltpu.CompilerParams(vmem_limit_bytes=mib * MIB)


def cost(flops, moved):
    return pl.CostEstimate(flops=int(flops), bytes_accessed=int(moved), transcendentals=0)


def run_experts(rows, w_gate, w_up, w_down):
    count, model = rows.shape
    hidden_units = w_gate.shape[2]
    chunk = 256 if hidden_units % 256 == 0 else hidden_units
    return pl.pallas_call(
        expert_kernel,
        grid=(hidden_units // chunk,),
        in_specs=[
            pl.BlockSpec((count, model), lambda f: (0, 0)),
            pl.BlockSpec((1, model, chunk), lambda f: (0, 0, f)),
            pl.BlockSpec((1, model, chunk), lambda f: (0, 0, f)),
            pl.BlockSpec((1, chunk, model), lambda f: (0, f, 0)),
        ],
        out_specs=pl.BlockSpec((count, model), lambda f: (0, 0)),
        out_shape=jax.ShapeDtypeStruct((count, model), jnp.bfloat16),
        scratch_shapes=[pltpu.VMEM((count, model), jnp.float32)],
        compiler_params=params(50),
        cost_estimate=cost(6 * count * model * hidden_units, 6 * model * hidden_units),
        name="experts",
    )(rows, w_gate, w_up, w_down)


def per_device(
    hidden, parents, path, cache_len, page_table, kv_pool, mig_slot, mig_dest,
    attn_gain, w_qkv, w_out, moe_gain, w_router, expert_ids, w_gate, w_up, w_down,
):
    bf16 = jnp.bfloat16
    requests, draft = parents.shape
    tokens, model = hidden.shape
    req_count = lax.axis_size("req")
    ep_count = lax.axis_size("ep")
    device_count = req_count * ep_count
    half_count = device_count // 2
    experts = w_router.shape[1]
    split = device_count // experts
    pages = page_table.shape[1]
    page, kv_width = kv_pool.shape[1:]
    context = pages * page
    query_width = w_out.shape[0]
    slot_rows = half_count * CAP
    req_index = lax.axis_index("req")
    ep_index = lax.axis_index("ep")
    groups = [[h * half_count + i for i in range(half_count)] for h in range(2)]
    swap = [(i, (i + req_count // 2) % req_count) for i in range(req_count)]
    base = (req_index // (req_count // 2) * (experts // 2)).astype(jnp.int32).reshape(1)

    def within_half(rows):
        return lax.all_to_all(rows, AXES, 0, 0, tiled=True, axis_index_groups=groups)

    leave_len = lax.dynamic_index_in_dim(cache_len, mig_slot[0], 0, keepdims=False)
    note = jnp.stack([mig_dest[0], leave_len])
    notes = lax.all_to_all(
        jnp.broadcast_to(note[None], (ep_count, 2)), "ep", 0, 0, tiled=True
    )
    leaving = pl.pallas_call(
        leaving_kernel,
        in_specs=[SMEM, SMEM, ANY],
        out_specs=ANY,
        out_shape=jax.ShapeDtypeStruct((context, kv_width), bf16),
        scratch_shapes=[pltpu.SemaphoreType.DMA((pages,))],
        cost_estimate=cost(0, 4 * context * kv_width),
        name="leaving",
    )(mig_slot, page_table, kv_pool)
    sibling = lax.ppermute(leaving, "ep", [(i, i ^ 1) for i in range(ep_count)])
    far_ids = lax.ppermute(expert_ids, "req", swap)
    chips = ep_count // 2
    chip = ep_index // 2
    core = ep_index % 2
    arrivals = []
    for k in range(1, chips):
        target = (chip + k) % chips * 2 + core
        payload = jnp.where(mig_dest[0] == target, leaving, sibling)
        moves = [(i, ((i // 2 + k) % chips) * 2 + i % 2) for i in range(ep_count)]
        arrivals.append(lax.ppermute(payload, "ep", moves))
    ep_ids = jnp.arange(ep_count, dtype=jnp.int32)
    for_me = notes[:, 0] == ep_index
    sender = jnp.sum(jnp.where(for_me, ep_ids, 0))
    arrived_len = jnp.sum(jnp.where(for_me, notes[:, 1], 0))
    lengths = jnp.where(jnp.arange(requests) == mig_slot[0], arrived_len, cache_len)
    meta = jnp.concatenate([mig_slot, lengths]).astype(jnp.int32)
    hop = (chip - sender // 2) % chips
    select = jnp.where(
        hop > 0, hop + 1, jnp.where(sender == ep_index, 0, 1)
    ).astype(jnp.int32).reshape(1)

    def routes_of(ids):
        return pl.pallas_call(
            lambda b, i, o: routes_kernel(b, split, i, o),
            in_specs=[SMEM, VMEM],
            out_specs=VMEM,
            out_shape=jax.ShapeDtypeStruct((slot_rows, tokens), bf16),
            name="routes",
        )(base, ids.T)

    routes = routes_of(expert_ids)
    far_routes = routes_of(far_ids)

    frequencies = ROPE_BASE ** (-2.0 * np.arange(HEAD_SIZE // 2) / HEAD_SIZE)
    spectrum = jnp.asarray(np.concatenate([frequencies] * 2)[None].astype(np.float32))
    queries, fresh, reach, compact, staying = pl.pallas_call(
        front_kernel,
        in_specs=[SMEM, SMEM] + [VMEM] * 7 + [ANY],
        out_specs=[VMEM] * 5,
        out_shape=[
            jax.ShapeDtypeStruct((tokens, query_width), bf16),
            jax.ShapeDtypeStruct((tokens, kv_width), bf16),
            jax.ShapeDtypeStruct((tokens, draft), jnp.float32),
            jax.ShapeDtypeStruct((tokens, kv_width), bf16),
            jax.ShapeDtypeStruct((draft, model), bf16),
        ],
        scratch_shapes=[
            pltpu.VMEM((context, kv_width), bf16),
            pltpu.SemaphoreType.DMA((pages,)),
        ],
        compiler_params=params(48),
        cost_estimate=cost(12e9, 24e6),
        name="front",
    )(
        meta, page_table, hidden, parents.reshape(tokens, 1), path.reshape(tokens, 1), spectrum,
        attn_gain.reshape(1, model), w_qkv, w_out, kv_pool,
    )
    sources = [leaving, sibling] + arrivals
    residual, normed, packed = pl.pallas_call(
        arrival_kernel,
        in_specs=[SMEM, SMEM] + [VMEM] * 7 + [ANY] * (1 + len(sources)),
        out_specs=[VMEM] * 3,
        out_shape=[
            jax.ShapeDtypeStruct((tokens, model), bf16),
            jax.ShapeDtypeStruct((tokens, model), bf16),
            jax.ShapeDtypeStruct((slot_rows, model), bf16),
        ],
        scratch_shapes=[
            pltpu.VMEM((context, kv_width), bf16),
            pltpu.VMEM(w_out.shape, bf16),
            pltpu.SemaphoreType.DMA,
            pltpu.SemaphoreType.DMA,
            pltpu.SemaphoreType.DMA,
        ],
        compiler_params=params(48),
        cost_estimate=cost(4e9, 8e6),
        name="arrival",
    )(
        meta, select, hidden, queries, fresh, reach, staying, moe_gain.reshape(1, model),
        routes, w_out, *sources,
    )
    far_normed = lax.ppermute(normed, "req", swap)
    near_rows = within_half(packed)
    far_packed = pl.pallas_call(
        pack_kernel,
        in_specs=[VMEM] * 2,
        out_specs=VMEM,
        out_shape=jax.ShapeDtypeStruct((slot_rows, model), bf16),
        name="pack",
    )(far_routes, far_normed)
    far_rows = within_half(far_packed)

    def shares_of(ids, values):
        return pl.pallas_call(
            lambda b, n, w, i, h, l: shares_kernel(b, split, experts, n, w, i, h, l),
            in_specs=[SMEM] + [VMEM] * 3,
            out_specs=[VMEM] * 2,
            out_shape=[jax.ShapeDtypeStruct((tokens, slot_rows), bf16)] * 2,
            name="shares",
        )(base, values, w_router, ids)

    near_high, near_low = shares_of(expert_ids, normed)
    far_high, far_low = shares_of(far_ids, far_normed)
    near_out = run_experts(near_rows, w_gate, w_up, w_down)
    far_out = run_experts(far_rows, w_gate, w_up, w_down)
    far_back = within_half(far_out)
    far_sum = pl.pallas_call(
        partial_kernel,
        in_specs=[VMEM] * 3,
        out_specs=VMEM,
        out_shape=jax.ShapeDtypeStruct((tokens, model), bf16),
        compiler_params=params(40),
        name="partial",
    )(far_high, far_low, far_back)
    own_far = lax.ppermute(far_sum, "req", swap)
    near_back = within_half(near_out)
    layer_out = pl.pallas_call(
        final_kernel,
        in_specs=[VMEM] * 5,
        out_specs=VMEM,
        out_shape=jax.ShapeDtypeStruct((tokens, model), bf16),
        compiler_params=params(40),
        name="final",
    )(residual, near_high, near_low, near_back, own_far)
    return layer_out, compact.reshape(requests, draft, kv_width)


def solution(mesh):
    rows = P(AXES, None)
    blocks = P(AXES, None, None)
    in_specs = (
        rows, rows, rows, P(AXES), rows, blocks, P(AXES), P(AXES),
        P(), P(), P(), P(), P(), rows, blocks, blocks, blocks,
    )
    return jax.shard_map(
        per_device, mesh=mesh, in_specs=in_specs, out_specs=(rows, blocks), check_vma=False
    )
```

time: 290 us -> 226 us (0.78)
  Pallas kernels: 0 us -> 78 us
  blocking collectives: 76.3 us -> 26.4 us
  local copies, waits for them, and re-layouts: 49.3 us -> 12.1 us
  other arithmetic: 36.2 us -> 3.62 us
  matrix products: 31.2 us -> 0 us
  starting transfers between devices: 13.1 us -> 21 us
    pallas_call x0 -> x12, Pallas kernels: none -> 78 us  [the longest x1 33.8 us: per_device(): pl.pallas_call(leaving_kernel, in_specs=[SMEM, SMEM, ANY], out_specs=ANY,...]
    all_to_all x1, blocking collectives: 76.3 us -> 26.4 us  [within_half(): lax.all_to_all(rows, AXES, 0, 0, tiled=True, axis_index_groups=groups)]
    dot_general x16 -> x0, matrix products: 31.2 us -> none  [the longest x1 11.2 us: per_device(): jnp.dot(activated, w_down[0], preferred_element_type=jnp.float32)]
    ppermute x0 -> x5, waiting for transfers between devices: none -> 28.4 us  [the longest x1 16.7 us: per_device(): far_ids = lax.ppermute(expert_ids, 'req', swap)]
    all_to_all x3 -> x4, waiting for transfers between devices: 78.6 us -> 50.3 us  [the longest x3 48.5 us: within_half(): lax.all_to_all(rows, AXES, 0, 0, tiled=True, axis_index_groups=groups)]
    gather x13 -> x0, local copies, waits for them, and re-layouts: 25.6 us -> none  [the longest x2 12.4 us: per_device(): gathered_rows = expert_out[slot_pick]]
    slice x7 -> x0, local copies, waits for them, and re-layouts: 9.53 us -> none  [the longest x2 4.13 us: split_into_heads(): cache_rows[..., :key_width].reshape(head_shape)]
    reduce_sum x8 -> x1, other arithmetic: 8.93 us -> 0.7 us  [per_device(): sender = jnp.sum(jnp.where(for_me, ep_ids, 0))]
  transfers between devices with their start and end apart: 3 -> 9, of which waited for: 2 -> 6; matrix products, arithmetic and copies ran while one was open for 17% -> 3% of each run, Pallas kernels for 0% -> 15%
where the time goes in v1:
time: 226 us; the launch traced here: 225 us
  waiting for transfers between devices  78.7 us (35%)
  Pallas kernels  78 us (35%)
  blocking collectives  26.4 us (12%)
  starting transfers between devices  21 us (9%)
  local copies, waits for them, and re-layouts  12.1 us (5%)
  between operations  5.51 us (2%)
  other arithmetic  3.62 us (2%)
    all_to_all x3, waiting for transfers between devices, within_half(): lax.all_to_all(rows, AXES, 0, 0, tiled=True, axis_index_groups=groups)  48.5 us
    pallas_call x1, Pallas kernels, per_device(): pl.pallas_call(leaving_kernel, in_specs=[SMEM, SMEM, ANY], out_specs=ANY,...  33.8 us
    all_to_all x1, blocking collectives, within_half(): lax.all_to_all(rows, AXES, 0, 0, tiled=True, axis_index_groups=groups)  26.4 us
    ppermute x1, waiting for transfers between devices, per_device(): far_ids = lax.ppermute(expert_ids, 'req', swap)  16.7 us
    pallas_call x2, Pallas kernels, run_experts(): pl.pallas_call(expert_kernel, grid=(hidden_units // chunk,), in_specs=[pl...  13.6 us
    ppermute x1, waiting for transfers between devices, per_device(): arrivals.append(lax.ppermute(payload, 'ep', moves))  11.7 us
    pallas_call x1, Pallas kernels, per_device(): pl.pallas_call(front_kernel, in_specs=[SMEM, SMEM] + [VMEM] * 7 + [ANY],...  11.4 us
    all_to_all x3, starting transfers between devices, within_half(): lax.all_to_all(rows, AXES, 0, 0, tiled=True, axis_index_groups=groups)  11.4 us
  transfers between devices with their start and end apart: 9, of which 6 were waited for; matrix products, arithmetic and copies ran while one was open for 3% of the time, Pallas kernels for 15%

profile of v1, /device:TPU:0, one launch (start us, length us, event | category | flops | bytes accessed | tf_op | source)
XLA Modules:
  0.0 225.4 jit_solution(10517660120083440257)
XLA Ops:
  1.3 33.8 %leaving.1.rest_0_ = bf16[1024,512]{1,0:T(8,128)(2,1)} custom-call(s32[1]{0:T(128)} %copy.33.meta, s32[2,8]{1,0:T(2,128)} %table.3, bf16[16,128,512]{2,1,0:T(8,128)(2,1)} %pool.3), custom_call_target="tpu_custom_call" | custom-call | bytes 2097152 | tf_op jit(solution)/shard_map/leaving/pallas_call | solution.py:322
  38.2 3.9 %all-to-all-start = ((s32[4,1,2]{2,1,0:T(1,128)}), s32[4,1,2]{2,1,0:T(1,128)S(1)}, u32[]{:S(2)}, u32[]{:S(2)}) async-start(s32[4,1,2]{2,1,0:T(1,128)} %broadcast_in_dim.15), calls=%async_computation | async-start | bytes 4096 | tf_op jit(solution)/shard_map/all_to_all | solution.py:319
  42.4 1.5 routes.2
  43.9 1.8 all-to-all-done
  50.6 1.5 broadcast_select_fusion
  52.5 11.4 %front.1 = (bf16[128,1536]{1,0:T(8,128)(2,1)S(1)}, bf16[128,512]{1,0:T(8,128)(2,1)S(1)}, f32[128,64]{1,0:T(8,128)S(1)}, bf16[128,512]{1,0:T(8,128)(2,1)}, bf16[64,1536]{1,0:T(8,128)(2,1)S(1)}) custom-call(s32[3]{0:T(128)S(1)} %pad_add_fusion.1.meta, s32[2,8]{1,0:T(2,128)S(1)} %copy-done.12, bf16[128,1536]{1,0:T(8,128)(2,1)S(1)} %copy-done.13, ...), custom_call_target="tpu_custom_call" | custom-call | flops 12000000000 | bytes 24000000 | tf_op jit(solution)/shard_map/front/pallas_call | solution.py:367
  63.9 11.7 %collective-permute-done.1.rest_2_ = bf16[1024,512]{1,0:T(8,128)(2,1)S(1)} collective-permute-done((bf16[1024,512]{1,0:T(8,128)(2,1)S(1)}, bf16[1024,512]{1,0:T(8,128)(2,1)S(1)}, u32[]{:S(2)}, u32[]{:S(2)}) %collective-permute-start.1) | collective-permute-done | bytes 1048608 | tf_op jit(solution)/shard_map/ppermute | solution.py:341
  75.7 6.1 %arrival.1 = (bf16[128,1536]{1,0:T(8,128)(2,1)S(1)}, bf16[128,1536]{1,0:T(8,128)(2,1)S(1)}, bf16[512,1536]{1,0:T(8,128)(2,1)}) custom-call(s32[3]{0:T(128)S(1)} %pad_add_fusion.1.meta, s32[1]{0:T(128)} %bitcast.4.select, bf16[128,1536]{1,0:T(8,128)(2,1)S(1)} %copy-done.13, bf16[128,1536]{1,0:T(8,128)(2,1)S(1)} %get-tuple-element.14.queries, ...), custom_call_target="tpu_custom_call" | custom-call | flops 4000000000 | bytes 8000000 | tf_op jit(solution)/shard_map/arrival/pallas_call | solution.py:390
  82.5 2.9 %collective-permute-start.2 = (bf16[128,1536]{1,0:T(8,128)(2,1)S(1)}, bf16[128,1536]{1,0:T(8,128)(2,1)S(1)}, u32[]{:S(2)}, u32[]{:S(2)}) collective-permute-start(bf16[128,1536]{1,0:T(8,128)(2,1)S(1)} %get-tuple-element.19.n), channel_id=1, source_target_pairs={{0,16},{4,20},{8,24},{12,28},{16,0},{20,4},{24,8},{28,12},{1,17},{... | collective-permute-start | bytes 1179656 | tf_op jit(solution)/shard_map/ppermute | solution.py:413
  85.4 16.7 %collective-permute-done.3 = s32[128,4]{0,1:T(4,128)S(1)} collective-permute-done((s32[128,4]{0,1:T(4,128)S(1)}, s32[128,4]{0,1:T(4,128)S(1)}, u32[]{:S(2)}, u32[]{:S(2)}) %collective-permute-start.3) | collective-permute-done | bytes 2080 | tf_op jit(solution)/shard_map/ppermute | solution.py:332
  102.7 1.5 routes.3
  104.9 2.8 %pack.1 = bf16[512,1536]{1,0:T(8,128)(2,1)} custom-call(bf16[512,128]{1,0:T(8,128)(2,1)} %routes.3, bf16[128,1536]{1,0:T(8,128)(2,1)} %copy-done.15), custom_call_target="tpu_custom_call" | custom-call | tf_op jit(solution)/shard_map/pack/pallas_call | solution.py:415
  107.7 26.4 %all_to_all.53 = bf16[16,32,1536]{2,1,0:T(8,128)(2,1)S(1)} all-to-all(bf16[16,32,1536]{2,1,0:T(8,128)(2,1)} %bitcast.36), channel_id=1, replica_groups={{0,1,2,3,4,5,6,7,8,9,10,11,12,13,14,15},{16,17,18,19,20,21,22,23,24,25,..., dimensions={0} | all-to-all | bytes 3145728 | tf_op jit(solution)/shard_map/all_to_all | solution.py:315
  134.1 3.7 %all-to-all-start.1 = ((bf16[16,32,1536]{2,1,0:T(8,128)(2,1)}), bf16[16,32,1536]{2,1,0:T(8,128)(2,1)S(1)}, u32[]{:S(2)}, u32[]{:S(2)}) async-start(bf16[16,32,1536]{2,1,0:T(8,128)(2,1)} %bitcast.37), calls=%async_computation.1 | async-start | bytes 3145728 | tf_op jit(solution)/shard_map/all_to_all | solution.py:315
  137.8 6.8 %experts.3 = bf16[512,1536]{1,0:T(8,128)(2,1)S(1)} custom-call(bf16[512,1536]{1,0:T(8,128)(2,1)S(1)} %bitcast.35, bf16[1,1536,768]{2,1,0:T(8,128)(2,1)} %w_gate.3, bf16[1,1536,768]{2,1,0:T(8,128)(2,1)} %w_up.3, bf16[1,768,1536]{2,1,0:T(8,128)(2,1)} %w_down.3), custom_call_target="tpu_custom_call" | custom-call | flops 3623878656 | bytes 7077888 | tf_op jit(solution)/shard_map/experts/pallas_call | solution.py:272
  144.6 1.1 copy-done.3
  145.8 15.0 %all-to-all-done.1 = bf16[16,32,1536]{2,1,0:T(8,128)(2,1)S(1)} async-done(((bf16[16,32,1536]{2,1,0:T(8,128)(2,1)}), bf16[16,32,1536]{2,1,0:T(8,128)(2,1)S(1)}, u32[]{:S(2)}, u32[]{:S(2)}) %all-to-all-start.1) | async-done | bytes 1572896 | tf_op jit(solution)/shard_map/all_to_all | solution.py:315
  160.8 3.9 %all-to-all-start.4 = ((bf16[16,32,1536]{2,1,0:T(8,128)(2,1)}), bf16[16,32,1536]{2,1,0:T(8,128)(2,1)S(1)}, u32[]{:S(2)}, u32[]{:S(2)}) async-start(bf16[16,32,1536]{2,1,0:T(8,128)(2,1)} %bitcast.34), calls=%async_computation.4 | async-start | bytes 3145728 | tf_op jit(solution)/shard_map/all_to_all | solution.py:315
  164.7 6.8 %experts.2 = bf16[512,1536]{1,0:T(8,128)(2,1)S(1)} custom-call(bf16[512,1536]{1,0:T(8,128)(2,1)S(1)} %bitcast.33, bf16[1,1536,768]{2,1,0:T(8,128)(2,1)} %w_gate.3, bf16[1,1536,768]{2,1,0:T(8,128)(2,1)} %w_up.3, bf16[1,768,1536]{2,1,0:T(8,128)(2,1)} %w_down.3), custom_call_target="tpu_custom_call" | custom-call | flops 3623878656 | bytes 7077888 | tf_op jit(solution)/shard_map/experts/pallas_call | solution.py:272
  171.5 1.2 copy-done.2
  172.7 14.8 %all-to-all-done.4 = bf16[16,32,1536]{2,1,0:T(8,128)(2,1)S(1)} async-done(((bf16[16,32,1536]{2,1,0:T(8,128)(2,1)}), bf16[16,32,1536]{2,1,0:T(8,128)(2,1)S(1)}, u32[]{:S(2)}, u32[]{:S(2)}) %all-to-all-start.4) | async-done | bytes 1572896 | tf_op jit(solution)/shard_map/all_to_all | solution.py:315
  187.5 3.8 %all-to-all-start.2 = ((bf16[16,32,1536]{2,1,0:T(8,128)(2,1)}), bf16[16,32,1536]{2,1,0:T(8,128)(2,1)S(1)}, u32[]{:S(2)}, u32[]{:S(2)}) async-start(bf16[16,32,1536]{2,1,0:T(8,128)(2,1)} %bitcast.32), calls=%async_computation.2 | async-start | bytes 3145728 | tf_op jit(solution)/shard_map/all_to_all | solution.py:315
  191.4 0.9 copy.29.w
  193.0 2.3 %shares.3 = (bf16[128,512]{1,0:T(8,128)(2,1)}, bf16[128,512]{1,0:T(8,128)(2,1)}) custom-call(s32[1]{0:T(128)} %bitcast.5.b, bf16[128,1536]{1,0:T(8,128)(2,1)} %copy-done.15, bf16[1536,32]{1,0:T(8,128)(2,1)} %copy.29.w, s32[128,4]{1,0:T(8,128)} %copy.32.i), custom_call_target="tpu_custom_call" | custom-call | tf_op jit(solution)/shard_map/shares/pallas_call | solution.py:425
  195.4 0.9 copy-done.9
  196.3 0.9 copy-done.10
  197.2 1.3 partial.1
  198.5 2.0 collective-permute-start.4
  201.2 2.3 %shares.2 = (bf16[128,512]{1,0:T(8,128)(2,1)}, bf16[128,512]{1,0:T(8,128)(2,1)}) custom-call(s32[1]{0:T(128)} %bitcast.5.b, bf16[128,1536]{1,0:T(8,128)(2,1)} %copy-done.4, bf16[1536,32]{1,0:T(8,128)(2,1)} %copy.29.w, s32[128,4]{1,0:T(8,128)} %copy.30.i), custom_call_target="tpu_custom_call" | custom-call | tf_op jit(solution)/shard_map/shares/pallas_call | solution.py:425
  203.5 18.7 %all-to-all-done.2 = bf16[16,32,1536]{2,1,0:T(8,128)(2,1)S(1)} async-done(((bf16[16,32,1536]{2,1,0:T(8,128)(2,1)}), bf16[16,32,1536]{2,1,0:T(8,128)(2,1)S(1)}, u32[]{:S(2)}, u32[]{:S(2)}) %all-to-all-start.2) | async-done | bytes 1572896 | tf_op jit(solution)/shard_map/all_to_all | solution.py:315
  223.1 0.9 copy-done.8
  224.0 1.3 final.1
  (64 shorter events, 9.2 us)
Async XLA Ops:
  1.3 35.0 %copy-start.24 = (s32[2]{0:T(128)S(1)}, s32[2]{0:T(128)}, u32[]{:S(2)}) copy-start(s32[2]{0:T(128)} %param.21) | copy-start | bytes 28
  1.3 40.8 %copy-start.22 = (s32[2,64]{1,0:T(2,128)S(1)}, s32[2,64]{1,0:T(2,128)}, u32[]{:S(2)}) copy-start(s32[2,64]{1,0:T(2,128)} %param.19) | copy-start | bytes 1540
  1.3 40.9 %copy-start.23 = (s32[2,64]{1,0:T(2,128)S(1)}, s32[2,64]{1,0:T(2,128)}, u32[]{:S(2)}) copy-start(s32[2,64]{1,0:T(2,128)} %param.20) | copy-start | bytes 1540
  1.3 41.1 %copy-start.20 = (bf16[1536]{0:T(1024)(128)(2,1)S(1)}, bf16[1536]{0:T(1024)(128)(2,1)}, u32[]{:S(2)}) copy-start(bf16[1536]{0:T(1024)(128)(2,1)} %param.26) | copy-start | bytes 9220
  1.3 41.1 %copy-start.21 = (bf16[1536]{0:T(1024)(128)(2,1)S(1)}, bf16[1536]{0:T(1024)(128)(2,1)}, u32[]{:S(2)}) copy-start(bf16[1536]{0:T(1024)(128)(2,1)} %param.29) | copy-start | bytes 9220
  35.1 15.5 %collective-permute-start = (bf16[1024,512]{1,0:T(8,128)(2,1)}, bf16[1024,512]{1,0:T(8,128)(2,1)S(1)}, u32[]{:S(2)}, u32[]{:S(2)}) collective-permute-start(bf16[1024,512]{1,0:T(8,128)(2,1)} %leaving.1.rest_0_), channel_id=1, source_target_pairs={{0,1},{1,0},{2,3},{3,2},{4,5},{5,4},{6,7},{7,6},{8,9},{9,8},{10,11... | collective-permute-start | bytes 3145736 | tf_op jit(solution)/shard_map/ppermute | solution.py:331
  38.2 7.6 %all-to-all-start = ((s32[4,1,2]{2,1,0:T(1,128)}), s32[4,1,2]{2,1,0:T(1,128)S(1)}, u32[]{:S(2)}, u32[]{:S(2)}) async-start(s32[4,1,2]{2,1,0:T(1,128)} %broadcast_in_dim.15), calls=%async_computation | async-start | bytes 4096 | tf_op jit(solution)/shard_map/all_to_all | solution.py:319
  50.5 1.9 copy-start.1
  50.5 1.9 copy-start.12
  50.5 2.0 copy-start.13
  50.5 2.0 copy-start.14
  52.1 23.6 %copy-start = (bf16[1024,512]{1,0:T(8,128)(2,1)S(1)}, bf16[1024,512]{1,0:T(8,128)(2,1)}, u32[]{:S(2)}) copy-start(bf16[1024,512]{1,0:T(8,128)(2,1)} %leaving.1.rest_0_) | copy-start | bytes 3145732
  52.1 23.6 %copy-start.11 = (bf16[512,128]{1,0:T(8,128)(2,1)S(1)}, bf16[512,128]{1,0:T(8,128)(2,1)}, u32[]{:S(2)}) copy-start(bf16[512,128]{1,0:T(8,128)(2,1)} %routes.2) | copy-start | bytes 393220
  52.1 23.6 %collective-permute-start.1 = (bf16[1024,512]{1,0:T(8,128)(2,1)S(1)}, bf16[1024,512]{1,0:T(8,128)(2,1)S(1)}, u32[]{:S(2)}, u32[]{:S(2)}) collective-permute-start(bf16[1024,512]{1,0:T(8,128)(2,1)S(1)} %broadcast_select_fusion), channel_id=1, source_target_pairs={{0,2},{1,3},{2,0},{3,1},{4,6},{5,7},{6,4},{7,5},{8,10},{9,11},{10,... | collective-permute-start | bytes 3145736 | tf_op jit(solution)/shard_map/ppermute | solution.py:341
  75.7 9.7 %copy-start.17 = (s32[128,4]{0,1:T(4,128)S(1)}, s32[128,4]{0,1:T(4,128)}, u32[]{:S(2)}) copy-start(s32[128,4]{0,1:T(4,128)} %param.31) | copy-start | bytes 6148
  81.7 0.7 copy-start.5
  82.5 51.6 %copy-start.4 = (bf16[128,1536]{1,0:T(8,128)(2,1)}, bf16[128,1536]{1,0:T(8,128)(2,1)S(1)}, u32[]{:S(2)}) copy-start(bf16[128,1536]{1,0:T(8,128)(2,1)S(1)} %get-tuple-element.19.n) | copy-start | bytes 1179652
  82.5 21.7 %collective-permute-start.2 = (bf16[128,1536]{1,0:T(8,128)(2,1)S(1)}, bf16[128,1536]{1,0:T(8,128)(2,1)S(1)}, u32[]{:S(2)}, u32[]{:S(2)}) collective-permute-start(bf16[128,1536]{1,0:T(8,128)(2,1)S(1)} %get-tuple-element.19.n), channel_id=1, source_target_pairs={{0,16},{4,20},{8,24},{12,28},{16,0},{20,4},{24,8},{28,12},{1,17},{... | collective-permute-start | bytes 1179656 | tf_op jit(solution)/shard_map/ppermute | solution.py:413
  85.4 16.7 %collective-permute-start.3 = (s32[128,4]{0,1:T(4,128)S(1)}, s32[128,4]{0,1:T(4,128)S(1)}, u32[]{:S(2)}, u32[]{:S(2)}) collective-permute-start(s32[128,4]{0,1:T(4,128)S(1)} %copy-done.17), channel_id=1, source_target_pairs={{0,16},{4,20},{8,24},{12,28},{16,0},{20,4},{24,8},{28,12},{1,17},{... | collective-permute-start | bytes 6152 | tf_op jit(solution)/shard_map/ppermute | solution.py:332
  134.1 26.7 %all-to-all-start.1 = ((bf16[16,32,1536]{2,1,0:T(8,128)(2,1)}), bf16[16,32,1536]{2,1,0:T(8,128)(2,1)S(1)}, u32[]{:S(2)}, u32[]{:S(2)}) async-start(bf16[16,32,1536]{2,1,0:T(8,128)(2,1)} %bitcast.37), calls=%async_computation.1 | async-start | bytes 3145728 | tf_op jit(solution)/shard_map/all_to_all | solution.py:315
  144.6 1.2 copy-start.3
  160.8 26.7 %all-to-all-start.4 = ((bf16[16,32,1536]{2,1,0:T(8,128)(2,1)}), bf16[16,32,1536]{2,1,0:T(8,128)(2,1)S(1)}, u32[]{:S(2)}, u32[]{:S(2)}) async-start(bf16[16,32,1536]{2,1,0:T(8,128)(2,1)} %bitcast.34), calls=%async_computation.4 | async-start | bytes 3145728 | tf_op jit(solution)/shard_map/all_to_all | solution.py:315
  171.5 1.2 copy-start.2
  187.5 3.9 %copy-start.16 = (bf16[1536,32]{0,1:T(8,128)(2,1)S(1)}, bf16[1536,32]{0,1:T(8,128)(2,1)}, u32[]{:S(2)}) copy-start(bf16[1536,32]{0,1:T(8,128)(2,1)} %param.30) | copy-start | bytes 294916
  187.5 4.8 %copy-start.19 = (s32[128,4]{0,1:T(4,128)S(1)}, s32[128,4]{0,1:T(4,128)}, u32[]{:S(2)}) copy-start(s32[128,4]{0,1:T(4,128)} %copy-done.18) | copy-start | bytes 6148
  187.5 34.7 %all-to-all-start.2 = ((bf16[16,32,1536]{2,1,0:T(8,128)(2,1)}), bf16[16,32,1536]{2,1,0:T(8,128)(2,1)S(1)}, u32[]{:S(2)}, u32[]{:S(2)}) async-start(bf16[16,32,1536]{2,1,0:T(8,128)(2,1)} %bitcast.32), calls=%async_computation.2 | async-start | bytes 3145728 | tf_op jit(solution)/shard_map/all_to_all | solution.py:315
  195.4 0.9 copy-start.9
  196.3 0.9 copy-start.10
  197.2 25.1 %copy-start.6 = (bf16[128,1536]{1,0:T(8,128)(2,1)S(1)}, bf16[128,1536]{1,0:T(8,128)(2,1)}, u32[]{:S(2)}) copy-start(bf16[128,1536]{1,0:T(8,128)(2,1)} %copy-done.5) | copy-start | bytes 1179652
  198.5 23.7 %collective-permute-start.4 = (bf16[128,1536]{1,0:T(8,128)(2,1)}, bf16[128,1536]{1,0:T(8,128)(2,1)S(1)}, u32[]{:S(2)}, u32[]{:S(2)}) collective-permute-start(bf16[128,1536]{1,0:T(8,128)(2,1)} %partial.1), channel_id=1, source_target_pairs={{0,16},{4,20},{8,24},{12,28},{16,0},{20,4},{24,8},{28,12},{1,17},{... | collective-permute-start | bytes 1179656 | tf_op jit(solution)/shard_map/ppermute | solution.py:446
  222.2 0.9 copy-start.7
  223.1 0.9 copy-start.8
  (2 other events, 1.3 us)

commit v2 on v1

v2 whole, which is shorter than its diff:
```python
import functools

import jax
import jax.numpy as jnp
import numpy as np
from jax import lax
from jax.experimental import pallas as pl
from jax.experimental.pallas import tpu as pltpu
from jax.sharding import PartitionSpec as P

QUERY_HEADS = 12
KEY_VALUE_HEADS = 2
HEAD_SIZE = 128
GROUP = QUERY_HEADS // KEY_VALUE_HEADS
CAP = 32
EPSILON = 1e-06
ROPE_BASE = 1000000.0
MASKED = -1e30
MIB = 1024 * 1024
NOTE = 16
LIMIT = 60
NOTE_BASE = 32
AXES = ("req", "ep")

VMEM = pl.BlockSpec(memory_space=pltpu.VMEM)
SMEM = pl.BlockSpec(memory_space=pltpu.SMEM)
ANY = pl.BlockSpec(memory_space=pl.ANY)


def dot(a, b, dims=((1,), (0,))):
    return lax.dot_general(a, b, (dims, ((), ())), preferred_element_type=jnp.float32)


def rms_scale(values, scaling):
    widened = values.astype(jnp.float32)
    spread = jnp.mean(widened * widened, axis=-1, keepdims=True)
    return (widened * lax.rsqrt(spread + EPSILON) * scaling.astype(jnp.float32)).astype(
        jnp.bfloat16
    )


def attend(queries, cached, fresh, reach, length):
    scale = HEAD_SIZE ** (-0.5)
    key_width = KEY_VALUE_HEADS * HEAD_SIZE
    context = cached.shape[0]
    rows = queries.shape[0] * GROUP
    in_cache = lax.broadcasted_iota(jnp.int32, (rows, context), 1) < length
    in_tree = jnp.concatenate([reach] * GROUP, axis=0) > 0.5
    outs = []
    for kv in range(KEY_VALUE_HEADS):
        cols = slice(kv * HEAD_SIZE, (kv + 1) * HEAD_SIZE)
        vcols = slice(key_width + kv * HEAD_SIZE, key_width + (kv + 1) * HEAD_SIZE)
        heads = [
            queries[:, (kv * GROUP + g) * HEAD_SIZE : (kv * GROUP + g + 1) * HEAD_SIZE]
            for g in range(GROUP)
        ]
        stacked = jnp.concatenate(heads, axis=0)
        first = dot(stacked, cached[:, cols], ((1,), (1,))) * scale
        first = jnp.where(in_cache, first, MASKED)
        second = dot(stacked, fresh[:, cols], ((1,), (1,))) * scale
        second = jnp.where(in_tree, second, MASKED)
        highest = jnp.maximum(
            jnp.max(first, axis=-1, keepdims=True), jnp.max(second, axis=-1, keepdims=True)
        )
        first = jnp.exp(first - highest)
        second = jnp.exp(second - highest)
        total = jnp.sum(first, axis=-1, keepdims=True) + jnp.sum(second, axis=-1, keepdims=True)
        mixed = dot(first.astype(jnp.bfloat16), cached[:, vcols])
        mixed = mixed + dot(second.astype(jnp.bfloat16), fresh[:, vcols])
        mixed = (mixed / total).astype(jnp.bfloat16)
        step = queries.shape[0]
        outs += [mixed[g * step : (g + 1) * step] for g in range(GROUP)]
    return jnp.concatenate(outs, axis=1)


def load_pages(table, row, pool, target, sems):
    page = pool.shape[1]
    copies = [
        pltpu.make_async_copy(
            pool.at[table[row, i]], target.at[pl.ds(i * page, page)], sems.at[i]
        )
        for i in range(table.shape[1])
    ]
    for copy in copies:
        copy.start()
    return copies


def leaving_kernel(slot, dest, lengths, table, pool, out, sems):
    copies = load_pages(table, slot[0], pool, out, sems)
    length = lengths[slot[0]]
    context = out.shape[0] - NOTE
    note = jnp.zeros((NOTE, 128), jnp.float32)
    for at, value in enumerate((dest[0], length // NOTE_BASE, length % NOTE_BASE)):
        filled = note + value.astype(jnp.float32)
        out[context:, at * 128 : (at + 1) * 128] = filled.astype(jnp.bfloat16)
    out[context:, 3 * 128 :] = jnp.zeros((NOTE, out.shape[1] - 3 * 128), jnp.bfloat16)
    for copy in copies:
        copy.wait()


def slots_of(ids_t, first, shown):
    tokens = ids_t.shape[1]
    names = lax.broadcasted_iota(jnp.int32, (shown, tokens), 0) + first
    assigned = jnp.zeros((shown, tokens), jnp.bool_)
    for k in range(ids_t.shape[0]):
        assigned = assigned | (ids_t[k : k + 1, :] == names)
    before = lax.broadcasted_iota(jnp.int32, (tokens, tokens), 0) < lax.broadcasted_iota(
        jnp.int32, (tokens, tokens), 1
    )
    ranks = dot(one_hot(assigned), one_hot(before))
    return assigned, jnp.where(assigned, ranks, -1.0)


def one_hot(flags):
    return jnp.where(flags, 1.0, 0.0).astype(jnp.bfloat16)


def flipped(values):
    size = values.shape[1]
    same = lax.broadcasted_iota(jnp.int32, (size, size), 0) == lax.broadcasted_iota(
        jnp.int32, (size, size), 1
    )
    if values.shape[0] == 1:
        return jnp.sum(jnp.where(same, values, 0.0), axis=1, keepdims=True)
    return dot(one_hot(same), values.astype(jnp.bfloat16), ((1,), (1,)))


def routes_kernel(split, base, slot, ids_t, table, ordered):
    ids = ids_t[...]
    tokens = ids.shape[1]
    turned = jnp.concatenate([ids[:, tokens // 2 :], ids[:, : tokens // 2]], axis=1)
    ids = jnp.where(slot[0] == 0, turned, ids)
    ordered[...] = ids
    shown = table.shape[0] // (split * CAP)
    _, slots = slots_of(ids, base[0], shown)
    wanted = lax.broadcasted_iota(jnp.int32, (shown, split * CAP, tokens), 1) % CAP
    hot = jnp.where(slots.astype(jnp.int32)[:, None, :] == wanted, 1.0, 0.0)
    table[...] = hot.reshape(table.shape).astype(jnp.bfloat16)


def shares_kernel(split, base, staying, moved, w_router_t, ids_t, high, low):
    tokens = ids_t.shape[1]
    experts = w_router_t.shape[0]
    width = high.shape[1]
    both = jnp.concatenate([staying[...], moved[...]], axis=0)
    logits = dot(both, w_router_t[...], ((1,), (1,)))
    _, slots_t = slots_of(ids_t, 0, experts)
    slots = flipped(slots_t)
    squashed = jnp.where(slots >= 0.0, jax.nn.sigmoid(logits), 0.0)
    share = squashed / jnp.sum(squashed, axis=1, keepdims=True)
    spread = one_hot(
        lax.broadcasted_iota(jnp.int32, (experts, width), 1) // (split * CAP) + base[0]
        == lax.broadcasted_iota(jnp.int32, (experts, width), 0)
    )
    wanted = lax.broadcasted_iota(jnp.int32, (tokens, width), 1) % CAP
    hit = dot(slots.astype(jnp.bfloat16), spread).astype(jnp.int32) == wanted
    share_high = share.astype(jnp.bfloat16)
    share_low = (share - share_high.astype(jnp.float32)).astype(jnp.bfloat16)
    high[...] = jnp.where(hit, dot(share_high, spread), 0.0).astype(jnp.bfloat16)
    low[...] = jnp.where(hit, dot(share_low, spread), 0.0).astype(jnp.bfloat16)


def rotate(projected, depth, length, spectrum, query_width):
    angles = (depth + length) * spectrum
    cosine = jnp.cos(angles)
    sine = jnp.sin(angles)
    first_half = lax.broadcasted_iota(jnp.int32, (1, HEAD_SIZE), 1) < HEAD_SIZE // 2
    sine = jnp.where(first_half, -sine, sine)
    key_width = KEY_VALUE_HEADS * HEAD_SIZE
    turned = []
    for h in range(QUERY_HEADS + KEY_VALUE_HEADS):
        part = projected[:, h * HEAD_SIZE : (h + 1) * HEAD_SIZE]
        swapped = jnp.concatenate([part[:, HEAD_SIZE // 2 :], part[:, : HEAD_SIZE // 2]], axis=1)
        turned.append((part * cosine + swapped * sine).astype(jnp.bfloat16))
    values = projected[:, query_width + key_width :].astype(jnp.bfloat16)
    return (
        jnp.concatenate(turned[:QUERY_HEADS], axis=1),
        jnp.concatenate(turned[QUERY_HEADS:] + [values], axis=1),
    )


def front_kernel(
    slot, lengths, table, hidden, parents, path, spectrum, gain, moe_gain, w_qkv, w_out, pool,
    moved_projected, moved_reach, moved_picked, compact, staying, staying_normed, cache, sems,
):
    stay = 1 - slot[0]
    copies = load_pages(table, stay, pool, cache, sems)
    draft = parents.shape[1]
    query_width = w_out.shape[0]
    rows = [
        hidden[pl.ds(pl.multiple_of(r * draft, draft), draft), :] for r in (stay, slot[0])
    ]
    normed = rms_scale(jnp.concatenate(rows, axis=0), gain[...])
    projected = dot(normed, w_qkv[...])
    names = lax.broadcasted_iota(jnp.int32, (draft, draft), 1)
    itself = names == lax.broadcasted_iota(jnp.int32, (draft, draft), 0)
    trees = []
    for r in (stay, slot[0]):
        above = flipped(parents[pl.ds(r, 1), :].astype(jnp.float32)).astype(jnp.int32)
        reached = jnp.where((above == names) | itself, 1.0, 0.0)
        for _ in range(max(1, (draft - 1).bit_length())):
            half = reached.astype(jnp.bfloat16)
            reached = jnp.minimum(dot(half, half), 1.0)
        trees.append(reached)
    picks = [
        one_hot(flipped(path[pl.ds(r, 1), :].astype(jnp.float32)).astype(jnp.int32) == names)
        for r in (stay, slot[0])
    ]
    moved_projected[...] = projected[draft:]
    moved_reach[...] = trees[1]
    moved_picked[...] = picks[1]
    depth = jnp.sum(trees[0], axis=-1, keepdims=True) - 1.0
    length = lengths[stay]
    queries, fresh = rotate(
        projected[:draft], depth, length.astype(jnp.float32), spectrum[...], query_width
    )
    compact[...] = dot(picks[0], fresh).astype(jnp.bfloat16)
    for copy in copies:
        copy.wait()
    attended = attend(queries, cache, fresh, trees[0], length)
    kept = (rows[0].astype(jnp.float32) + dot(attended, w_out[...])).astype(jnp.bfloat16)
    staying[...] = kept
    staying_normed[...] = rms_scale(kept, moe_gain[...])


def arrival_kernel(
    slot, me, hidden, projected, reach, picked, staying_compact, spectrum, gain, w_out, *rest,
):
    sources = rest[:-7]
    moved, moved_normed, compact, caches, weights, sems, weight_sem = rest[-7:]
    loads = [
        pltpu.make_async_copy(source, caches.at[i], sems.at[i])
        for i, source in enumerate(sources)
    ]
    for load in loads:
        load.start()
    weight_load = pltpu.make_async_copy(w_out, weights, weight_sem)
    weight_load.start()
    draft = projected.shape[0]
    query_width = w_out.shape[0]
    depth = jnp.sum(reach[...], axis=-1, keepdims=True) - 1.0
    for load in loads:
        load.wait()
    context = caches.shape[1] - NOTE

    def noted(i, at):
        values = caches[i, context:, at * 128 : (at + 1) * 128]
        return jnp.max(values.astype(jnp.float32)).astype(jnp.int32)

    chosen = jnp.int32(0)
    length = jnp.int32(0)
    for i in range(len(sources)):
        mine = noted(i, 0) == me[0]
        chosen = jnp.where(mine, i, chosen)
        length = jnp.where(mine, noted(i, 1) * NOTE_BASE + noted(i, 2), length)
    queries, fresh = rotate(
        projected[...], depth, length.astype(jnp.float32), spectrum[...], query_width
    )
    attended = attend(
        queries, caches.at[chosen, pl.ds(0, context)], fresh, reach[...], length
    )
    weight_load.wait()
    own = pl.ds(pl.multiple_of(slot[0] * draft, draft), draft)
    other = pl.ds(pl.multiple_of((1 - slot[0]) * draft, draft), draft)
    kept = hidden[own, :].astype(jnp.float32) + dot(attended, weights[...])
    kept = kept.astype(jnp.bfloat16)
    moved[...] = kept
    moved_normed[...] = rms_scale(kept, gain[...])
    compact[own, :] = dot(picked[...], fresh).astype(jnp.bfloat16)
    compact[other, :] = staying_compact[...]


def pack_kernel(routes, staying, moved, packed):
    both = jnp.concatenate([staying[...], moved[...]], axis=0)
    packed[...] = dot(routes[...], both).astype(jnp.bfloat16)


def expert_kernel(rows, w_gate, w_up, w_down, out, total):
    step = pl.program_id(0)
    gated = dot(rows[...], w_gate[0])
    upped = dot(rows[...], w_up[0])
    activated = (jnp.maximum(gated, 0.0) * upped).astype(jnp.bfloat16)
    piece = dot(activated, w_down[0])

    @pl.when(step == 0)
    def _():
        total[...] = piece

    @pl.when(step > 0)
    def _():
        total[...] += piece

    @pl.when(step == pl.num_programs(0) - 1)
    def _():
        out[...] = total[...].astype(jnp.bfloat16)


def partial_kernel(high, low, rows, out):
    values = rows[...]
    out[...] = (dot(high[...], values) + dot(low[...], values)).astype(jnp.bfloat16)


def final_kernel(slot, staying, moved, high, low, rows, far, out):
    values = rows[...]
    total = dot(high[...], values) + dot(low[...], values) + far[...].astype(jnp.float32)
    draft = staying.shape[0]
    stay = pl.ds(pl.multiple_of((1 - slot[0]) * draft, draft), draft)
    move = pl.ds(pl.multiple_of(slot[0] * draft, draft), draft)
    out[stay, :] = (staying[...].astype(jnp.float32) + total[:draft]).astype(jnp.bfloat16)
    out[move, :] = (moved[...].astype(jnp.float32) + total[draft:]).astype(jnp.bfloat16)


def params(mib):
    return pltpu.CompilerParams(vmem_limit_bytes=mib * MIB)


def cost(flops, moved):
    return pl.CostEstimate(flops=int(flops), bytes_accessed=int(moved), transcendentals=0)


def run_experts(rows, w_gate, w_up, w_down):
    count, model = rows.shape
    hidden_units = w_gate.shape[2]
    chunk = 256 if hidden_units % 256 == 0 else hidden_units
    return pl.pallas_call(
        expert_kernel,
        grid=(hidden_units // chunk,),
        in_specs=[
            pl.BlockSpec((count, model), lambda f: (0, 0)),
            pl.BlockSpec((1, model, chunk), lambda f: (0, 0, f)),
            pl.BlockSpec((1, model, chunk), lambda f: (0, 0, f)),
            pl.BlockSpec((1, chunk, model), lambda f: (0, f, 0)),
        ],
        out_specs=pl.BlockSpec((count, model), lambda f: (0, 0)),
        out_shape=jax.ShapeDtypeStruct((count, model), jnp.bfloat16),
        scratch_shapes=[pltpu.VMEM((count, model), jnp.float32)],
        compiler_params=params(LIMIT),
        cost_estimate=cost(6 * count * model * hidden_units, 6 * model * hidden_units),
        name="experts",
    )(rows, w_gate, w_up, w_down)


def per_device(
    hidden, parents, path, cache_len, page_table, kv_pool, mig_slot, mig_dest,
    attn_gain, w_qkv, w_out, moe_gain, w_router, expert_ids, w_gate, w_up, w_down,
):
    bf16 = jnp.bfloat16
    requests, draft = parents.shape
    tokens, model = hidden.shape
    req_count = lax.axis_size("req")
    ep_count = lax.axis_size("ep")
    device_count = req_count * ep_count
    half_count = device_count // 2
    experts = w_router.shape[1]
    split = device_count // experts
    pages = page_table.shape[1]
    page, kv_width = kv_pool.shape[1:]
    context = pages * page
    query_width = w_out.shape[0]
    slot_rows = half_count * CAP
    req_index = lax.axis_index("req")
    ep_index = lax.axis_index("ep")
    groups = [[h * half_count + i for i in range(half_count)] for h in range(2)]
    inner = req_count // 4
    swap = [(i, (3 - i // inner) * inner + i % inner) for i in range(req_count)]
    base = (req_index // (req_count // 2) * (experts // 2)).astype(jnp.int32).reshape(1)

    def within_half(rows):
        return lax.all_to_all(rows, AXES, 0, 0, tiled=True, axis_index_groups=groups)

    leaving = pl.pallas_call(
        leaving_kernel,
        in_specs=[SMEM] * 4 + [ANY],
        out_specs=VMEM,
        out_shape=jax.ShapeDtypeStruct((context + NOTE, kv_width), bf16),
        scratch_shapes=[pltpu.SemaphoreType.DMA((pages,))],
        compiler_params=params(LIMIT),
        cost_estimate=cost(0, 4 * context * kv_width),
        name="leaving",
    )(mig_slot, mig_dest, cache_len, page_table, kv_pool)
    sibling = lax.ppermute(leaving, "ep", [(i, i ^ 1) for i in range(ep_count)])
    chips = ep_count // 2
    chip = ep_index // 2
    core = ep_index % 2
    arrivals = []
    for k in range(1, chips):
        target = (chip + k) % chips * 2 + core
        payload = jnp.where(mig_dest[0] == target, leaving, sibling)
        moves = [(i, ((i // 2 + k) % chips) * 2 + i % 2) for i in range(ep_count)]
        arrivals.append(lax.ppermute(payload, "ep", moves))
    me = ep_index.astype(jnp.int32).reshape(1)

    def routes_of(slot, names):
        return pl.pallas_call(
            functools.partial(routes_kernel, split),
            in_specs=[SMEM, SMEM, VMEM],
            out_specs=[VMEM] * 2,
            out_shape=[
                jax.ShapeDtypeStruct((slot_rows, tokens), bf16),
                jax.ShapeDtypeStruct(names.shape, jnp.int32),
            ],
            compiler_params=params(LIMIT),
            cost_estimate=cost(1e8, 1e6),
            name="routes",
        )(base, slot, names)

    routes, ids = routes_of(mig_slot, expert_ids.T)
    far_ids = lax.ppermute(ids, "req", swap)
    far_routes, _ = routes_of(jnp.ones((1,), jnp.int32), far_ids)

    frequencies = ROPE_BASE ** (-2.0 * np.arange(HEAD_SIZE // 2) / HEAD_SIZE)
    spectrum = jnp.asarray(np.concatenate([frequencies] * 2)[None].astype(np.float32))
    row_gain = attn_gain.reshape(1, model)
    row_moe_gain = moe_gain.reshape(1, model)
    projected, reach, picked, staying_compact, staying, staying_normed = pl.pallas_call(
        front_kernel,
        in_specs=[SMEM] * 3 + [VMEM] * 8 + [ANY],
        out_specs=[VMEM] * 6,
        out_shape=[
            jax.ShapeDtypeStruct((draft, w_qkv.shape[1]), jnp.float32),
            jax.ShapeDtypeStruct((draft, draft), jnp.float32),
            jax.ShapeDtypeStruct((draft, draft), bf16),
            jax.ShapeDtypeStruct((draft, kv_width), bf16),
            jax.ShapeDtypeStruct((draft, model), bf16),
            jax.ShapeDtypeStruct((draft, model), bf16),
        ],
        scratch_shapes=[
            pltpu.VMEM((context, kv_width), bf16),
            pltpu.SemaphoreType.DMA((pages,)),
        ],
        compiler_params=params(LIMIT),
        cost_estimate=cost(3e9, 3e6),
        name="front",
    )(
        mig_slot, cache_len, page_table, hidden, parents, path, spectrum, row_gain,
        row_moe_gain, w_qkv, w_out, kv_pool,
    )
    far_staying = lax.ppermute(staying_normed, "req", swap)
    projected, routes, far_routes = lax.optimization_barrier((projected, routes, far_routes))
    sources = [leaving, sibling] + arrivals
    moved, moved_normed, compact = pl.pallas_call(
        arrival_kernel,
        in_specs=[SMEM] * 2 + [VMEM] * 7 + [ANY] * (1 + len(sources)),
        out_specs=[VMEM] * 3,
        out_shape=[
            jax.ShapeDtypeStruct((draft, model), bf16),
            jax.ShapeDtypeStruct((draft, model), bf16),
            jax.ShapeDtypeStruct((tokens, kv_width), bf16),
        ],
        scratch_shapes=[
            pltpu.VMEM((len(sources), context + NOTE, kv_width), bf16),
            pltpu.VMEM(w_out.shape, bf16),
            pltpu.SemaphoreType.DMA((len(sources),)),
            pltpu.SemaphoreType.DMA,
        ],
        compiler_params=params(LIMIT),
        cost_estimate=cost(4e9, 8e6),
        name="arrival",
    )(
        mig_slot, me, hidden, projected, reach, picked, staying_compact, spectrum,
        row_moe_gain, w_out, *sources,
    )
    far_moved = lax.ppermute(moved_normed, "req", swap)

    def pack(table, first, second):
        return pl.pallas_call(
            pack_kernel,
            in_specs=[VMEM] * 3,
            out_specs=VMEM,
            out_shape=jax.ShapeDtypeStruct((slot_rows, model), bf16),
            compiler_params=params(LIMIT),
            cost_estimate=cost(3e8, 2e6),
            name="pack",
        )(table, first, second)

    packed = pack(routes, staying_normed, moved_normed)
    far_packed = pack(far_routes, far_staying, far_moved)
    packed, far_packed = lax.optimization_barrier((packed, far_packed))
    far_rows = within_half(far_packed)
    near_rows = within_half(packed)

    def shares_of(names, first, second):
        return pl.pallas_call(
            functools.partial(shares_kernel, split),
            in_specs=[SMEM] + [VMEM] * 4,
            out_specs=[VMEM] * 2,
            out_shape=[jax.ShapeDtypeStruct((tokens, slot_rows), bf16)] * 2,
            compiler_params=params(LIMIT),
            cost_estimate=cost(3e8, 1e6),
            name="shares",
        )(base, first, second, w_router.T, names)

    near_high, near_low = shares_of(ids, staying_normed, moved_normed)
    far_high, far_low = shares_of(far_ids, far_staying, far_moved)
    near_out = run_experts(near_rows, w_gate, w_up, w_down)
    far_out = run_experts(far_rows, w_gate, w_up, w_down)
    far_out, near_high, near_low, far_high, far_low = lax.optimization_barrier(
        (far_out, near_high, near_low, far_high, far_low)
    )
    far_back = within_half(far_out)
    far_sum = pl.pallas_call(
        partial_kernel,
        in_specs=[VMEM] * 3,
        out_specs=VMEM,
        out_shape=jax.ShapeDtypeStruct((tokens, model), bf16),
        compiler_params=params(LIMIT),
        name="partial",
    )(far_high, far_low, far_back)
    own_far = lax.ppermute(far_sum, "req", swap)
    near_back = within_half(near_out)
    layer_out = pl.pallas_call(
        final_kernel,
        in_specs=[SMEM] + [VMEM] * 6,
        out_specs=VMEM,
        out_shape=jax.ShapeDtypeStruct((tokens, model), bf16),
        compiler_params=params(LIMIT),
        name="final",
    )(mig_slot, staying, moved, near_high, near_low, near_back, own_far)
    return layer_out, compact.reshape(requests, draft, kv_width)


def solution(mesh):
    rows = P(AXES, None)
    blocks = P(AXES, None, None)
    in_specs = (
        rows, rows, rows, P(AXES), rows, blocks, P(AXES), P(AXES),
        P(), P(), P(), P(), P(), rows, blocks, blocks, blocks,
    )
    return jax.shard_map(
        per_device, mesh=mesh, in_specs=in_specs, out_specs=(rows, blocks), check_vma=False
    )
```

time: 226 us -> 180 us (0.80)
  waiting for transfers between devices: 78.7 us -> 55.9 us
  Pallas kernels: 78 us -> 58.2 us
  starting transfers between devices: 21 us -> 25.8 us
  local copies, waits for them, and re-layouts: 12.1 us -> 7.39 us
  other arithmetic: 3.62 us -> 0.11 us
  between operations: 5.51 us -> 2 us
  blocking collectives: 26.4 us -> 28.9 us
    pallas_call x9 -> x10, Pallas kernels: 63.1 us -> 37.8 us  [the longest x1 11 us: per_device(): pl.pallas_call(front_kernel, in_specs=[SMEM] * 3 + [VMEM] * 8 + [ANY], ou...]
    ppermute x2 -> x3, waiting for transfers between devices: 16.7 us -> 1.91 us  [the longest x1 1.91 us: per_device(): far_moved = lax.ppermute(moved_normed, 'req', swap)]
    all_to_all x3, waiting for transfers between devices: 48.5 us -> 40.3 us  [within_half(): lax.all_to_all(rows, AXES, 0, 0, tiled=True, axis_index_groups=groups)]
    ppermute x1, waiting for transfers between devices: 11.7 us -> 4.08 us  [per_device(): arrivals.append(lax.ppermute(payload, 'ep', moves))]
    ppermute x1, waiting for transfers between devices: 0.01 us -> 7.02 us  [per_device(): own_far = lax.ppermute(far_sum, 'req', swap)]
    ppermute x2 -> x3, starting transfers between devices: 2.95 us -> 7.78 us  [the longest x1 3.89 us: per_device(): far_moved = lax.ppermute(moved_normed, 'req', swap)]
    all_to_all x1 -> x0, starting transfers between devices: 3.9 us -> none  [per_device(): lax.all_to_all(jnp.broadcast_to(note[None], (ep_count, 2)), 'ep', 0, 0, t...]
    pallas_call x2, Pallas kernels: 13.6 us -> 17.5 us  [run_experts(): pl.pallas_call(expert_kernel, grid=(hidden_units // chunk,), in_specs=[pl...]
  transfers between devices with their start and end apart: 9 -> 9, of which waited for: 6 -> 7; matrix products, arithmetic and copies ran while one was open for 3% -> 1% of each run, Pallas kernels for 15% -> 28%
where the time goes in v2:
time: 180 us; the launch traced here: 178 us
  Pallas kernels  58.2 us (32%)
  waiting for transfers between devices  55.9 us (31%)
  blocking collectives  28.9 us (16%)
  starting transfers between devices  25.8 us (14%)
  local copies, waits for them, and re-layouts  7.39 us (4%)
  between operations  2 us (1%)
    all_to_all x3, waiting for transfers between devices, within_half(): lax.all_to_all(rows, AXES, 0, 0, tiled=True, axis_index_groups=groups)  40.3 us
    all_to_all x1, blocking collectives, within_half(): lax.all_to_all(rows, AXES, 0, 0, tiled=True, axis_index_groups=groups)  28.9 us
    pallas_call x2, Pallas kernels, run_experts(): pl.pallas_call(expert_kernel, grid=(hidden_units // chunk,), in_specs=[pl...  17.5 us
    all_to_all x3, starting transfers between devices, within_half(): lax.all_to_all(rows, AXES, 0, 0, tiled=True, axis_index_groups=groups)  11.3 us
    pallas_call x1, Pallas kernels, per_device(): pl.pallas_call(front_kernel, in_specs=[SMEM] * 3 + [VMEM] * 8 + [ANY], ou...  11 us
    pallas_call x1, Pallas kernels, per_device(): pl.pallas_call(arrival_kernel, in_specs=[SMEM] * 2 + [VMEM] * 7 + [ANY] *...  7.18 us
    ppermute x1, waiting for transfers between devices, per_device(): own_far = lax.ppermute(far_sum, 'req', swap)  7.02 us
    unnamed x22, local copies, waits for them, and re-layouts  6.19 us
  transfers between devices with their start and end apart: 9, of which 7 were waited for; matrix products, arithmetic and copies ran while one was open for 1% of the time, Pallas kernels for 28%

profile of v2, /device:TPU:0, one launch (start us, length us, event | category | flops | bytes accessed | tf_op | source)
XLA Modules:
  0.0 178.3 jit_solution(11947989523522480227)
XLA Ops:
  1.9 3.1 %leaving.1.rest_0_ = bf16[1040,512]{1,0:T(8,128)(2,1)} custom-call(s32[1]{0:T(128)S(6)} %copy.20.slot, s32[1]{0:T(128)} %copy.21.dest, s32[2]{0:T(128)} %lengths.3, s32[2,8]{1,0:T(2,128)} %table.3, bf16[16,128,512]{2,1,0:T(8,128)(2,1)} %pool.3), custom_call_target="tpu_custom_call" | custom-call | bytes 2097152 | tf_op jit(solution)/shard_map/leaving/pallas_call | solution.py:372
  5.5 2.5 %collective-permute-done.1.rest_1_ = bf16[1040,512]{1,0:T(8,128)(2,1)S(1)} collective-permute-done((bf16[1040,512]{1,0:T(8,128)(2,1)}, bf16[1040,512]{1,0:T(8,128)(2,1)S(1)}, u32[]{:S(2)}, u32[]{:S(2)}) %collective-permute-start.1) | collective-permute-done | bytes 1064992 | tf_op jit(solution)/shard_map/ppermute | solution.py:382
  8.2 0.9 copy-done.3
  9.0 2.9 %collective-permute-start.2 = (bf16[1040,512]{1,0:T(8,128)(2,1)S(1)}, bf16[1040,512]{1,0:T(8,128)(2,1)S(1)}, u32[]{:S(2)}, u32[]{:S(2)}) collective-permute-start(bf16[1040,512]{1,0:T(8,128)(2,1)S(1)} %broadcast_select_fusion), channel_id=1, source_target_pairs={{0,2},{1,3},{2,0},{3,1},{4,6},{5,7},{6,4},{7,5},{8,10},{9,11},{10,... | collective-permute-start | bytes 3194888 | tf_op jit(solution)/shard_map/ppermute | solution.py:391
  11.9 1.5 routes.2
  13.4 3.6 %collective-permute-start = (s32[4,128]{1,0:T(4,128)}, s32[4,128]{1,0:T(4,128)S(1)}, u32[]{:S(2)}, u32[]{:S(2)}) collective-permute-start(s32[4,128]{1,0:T(4,128)} %get-tuple-element.31.ids_t), channel_id=1, source_target_pairs={{0,24},{4,28},{8,16},{12,20},{16,8},{20,12},{24,0},{28,4},{1,25},{... | collective-permute-start | bytes 6152 | tf_op jit(solution)/shard_map/ppermute | solution.py:409
  18.2 11.0 %front.1 = (f32[64,2048]{1,0:T(8,128)}, f32[64,64]{1,0:T(8,128)}, bf16[64,64]{1,0:T(8,128)(2,1)}, bf16[64,512]{1,0:T(8,128)(2,1)}, bf16[64,1536]{1,0:T(8,128)(2,1)}, /*index=5*/bf16[64,1536]{1,0:T(8,128)(2,1)}) custom-call(s32[1]{0:T(128)S(6)} %copy.20.slot, s32[2]{0:T(128)} %lengths.3, s32[2,8]{1,0:T(2,128)} %table.3, bf16[128,1536]{1,0:T(8,128)(2,1)} %hidden.3, ...), custom_call_target="tpu_custom_call" | custom-call | flops 3000000000 | bytes 3000000 | tf_op jit(solution)/shard_map/front/pallas_call | solution.py:416
  30.1 1.5 routes.3
  31.6 4.1 %collective-permute-done.2.rest_2_ = bf16[1040,512]{1,0:T(8,128)(2,1)S(1)} collective-permute-done((bf16[1040,512]{1,0:T(8,128)(2,1)S(1)}, bf16[1040,512]{1,0:T(8,128)(2,1)S(1)}, u32[]{:S(2)}, u32[]{:S(2)}) %collective-permute-start.2) | collective-permute-done | bytes 1064992 | tf_op jit(solution)/shard_map/ppermute | solution.py:391
  35.7 1.0 copy-done.9
  36.7 7.2 %arrival.1 = (bf16[64,1536]{1,0:T(8,128)(2,1)}, bf16[64,1536]{1,0:T(8,128)(2,1)}, bf16[128,512]{1,0:T(8,128)(2,1)}) custom-call(s32[1]{0:T(128)S(6)} %copy.20.slot, s32[1]{0:T(128)} %bitcast.me, bf16[128,1536]{1,0:T(8,128)(2,1)} %hidden.3, f32[64,2048]{1,0:T(8,128)} %get-tuple-element.33.projected, f32[64,64]{1,0:T(8,128)} %get-tuple-element.34.reach, ...), custom_call_target="tpu_custom_call" | custom-call | flops 4000000000 | bytes 8000000 | tf_op jit(solution)/shard_map/arrival/pallas_call | solution.py:442
  43.9 3.9 %collective-permute-start.4 = (bf16[64,1536]{1,0:T(8,128)(2,1)}, bf16[64,1536]{1,0:T(8,128)(2,1)S(1)}, u32[]{:S(2)}, u32[]{:S(2)}) collective-permute-start(bf16[64,1536]{1,0:T(8,128)(2,1)} %get-tuple-element.40.moved), channel_id=1, source_target_pairs={{0,24},{4,28},{8,16},{12,20},{16,8},{20,12},{24,0},{28,4},{1,25},{... | collective-permute-start | bytes 589832 | tf_op jit(solution)/shard_map/ppermute | solution.py:464
  47.8 2.8 %pack.2 = bf16[512,1536]{1,0:T(8,128)(2,1)} custom-call(bf16[512,128]{1,0:T(8,128)(2,1)} %get-tuple-element.38.routes, bf16[64,1536]{1,0:T(8,128)(2,1)} %get-tuple-element.39.staying, bf16[64,1536]{1,0:T(8,128)(2,1)} %get-tuple-element.40.moved), custom_call_target="tpu_custom_call" | custom-call | flops 300000000 | bytes 2000000 | tf_op jit(solution)/shard_map/pack/pallas_call | solution.py:467
  50.6 1.9 %collective-permute-done.4.moved = bf16[64,1536]{1,0:T(8,128)(2,1)S(1)} collective-permute-done((bf16[64,1536]{1,0:T(8,128)(2,1)}, bf16[64,1536]{1,0:T(8,128)(2,1)S(1)}, u32[]{:S(2)}, u32[]{:S(2)}) %collective-permute-start.4) | collective-permute-done | bytes 196640 | tf_op jit(solution)/shard_map/ppermute | solution.py:464
  53.2 2.8 %pack.3 = bf16[512,1536]{1,0:T(8,128)(2,1)} custom-call(bf16[512,128]{1,0:T(8,128)(2,1)} %get-tuple-element.41.routes, bf16[64,1536]{1,0:T(8,128)(2,1)} %copy-done.5, bf16[64,1536]{1,0:T(8,128)(2,1)} %copy-done.6), custom_call_target="tpu_custom_call" | custom-call | flops 300000000 | bytes 2000000 | tf_op jit(solution)/shard_map/pack/pallas_call | solution.py:467
  56.0 28.9 %all_to_all.44 = bf16[16,32,1536]{2,1,0:T(8,128)(2,1)} all-to-all(bf16[16,32,1536]{2,1,0:T(8,128)(2,1)} %bitcast.17), channel_id=1, replica_groups={{0,1,2,3,4,5,6,7,8,9,10,11,12,13,14,15},{16,17,18,19,20,21,22,23,24,25,..., dimensions={0} | all-to-all | bytes 3145728 | tf_op jit(solution)/shard_map/all_to_all | solution.py:370
  84.9 3.7 %all-to-all-start.1 = ((bf16[16,32,1536]{2,1,0:T(8,128)(2,1)}), bf16[16,32,1536]{2,1,0:T(8,128)(2,1)S(1)}, u32[]{:S(2)}, u32[]{:S(2)}) async-start(bf16[16,32,1536]{2,1,0:T(8,128)(2,1)} %bitcast.7), calls=%async_computation.1 | async-start | bytes 3145728 | tf_op jit(solution)/shard_map/all_to_all | solution.py:370
  88.6 2.4 %shares.2 = (bf16[128,512]{1,0:T(8,128)(2,1)}, bf16[128,512]{1,0:T(8,128)(2,1)}) custom-call(s32[1]{0:T(128)} %bitcast.1.base, bf16[64,1536]{1,0:T(8,128)(2,1)} %get-tuple-element.39.staying, bf16[64,1536]{1,0:T(8,128)(2,1)} %get-tuple-element.40.moved, bf16[32,1536]{1,0:T(8,128)(2,1)} %bitcast.22, s32[4,128]{1,0:T(4,128)} %get-tuple-element.31.ids_t), custom_call_target="tpu_custom_call" | custom-call | flops 300000000 | bytes 1000000 | tf_op jit(solution)/shard_map/shares/pallas_call | solution.py:484
  91.0 2.4 %shares.3 = (bf16[128,512]{1,0:T(8,128)(2,1)}, bf16[128,512]{1,0:T(8,128)(2,1)}) custom-call(s32[1]{0:T(128)} %bitcast.1.base, bf16[64,1536]{1,0:T(8,128)(2,1)} %copy-done.5, bf16[64,1536]{1,0:T(8,128)(2,1)} %copy-done.6, bf16[32,1536]{1,0:T(8,128)(2,1)} %bitcast.23, s32[4,128]{1,0:T(4,128)} %copy-done.10), custom_call_target="tpu_custom_call" | custom-call | flops 300000000 | bytes 1000000 | tf_op jit(solution)/shard_map/shares/pallas_call | solution.py:484
  93.4 8.7 %experts.2 = bf16[512,1536]{1,0:T(8,128)(2,1)} custom-call(bf16[512,1536]{1,0:T(8,128)(2,1)} %bitcast.19, bf16[1,1536,768]{2,1,0:T(8,128)(2,1)} %w_gate.3, bf16[1,1536,768]{2,1,0:T(8,128)(2,1)} %w_up.3, bf16[1,768,1536]{2,1,0:T(8,128)(2,1)} %w_down.3), custom_call_target="tpu_custom_call" | custom-call | flops 3623878656 | bytes 7077888 | tf_op jit(solution)/shard_map/experts/pallas_call | solution.py:326
  102.2 9.5 %all-to-all-done.1 = bf16[16,32,1536]{2,1,0:T(8,128)(2,1)S(1)} async-done(((bf16[16,32,1536]{2,1,0:T(8,128)(2,1)}), bf16[16,32,1536]{2,1,0:T(8,128)(2,1)S(1)}, u32[]{:S(2)}, u32[]{:S(2)}) %all-to-all-start.1) | async-done | bytes 1572896 | tf_op jit(solution)/shard_map/all_to_all | solution.py:370
  111.7 1.1 copy-done.2
  112.8 3.9 %all-to-all-start.3 = ((bf16[16,32,1536]{2,1,0:T(8,128)(2,1)}), bf16[16,32,1536]{2,1,0:T(8,128)(2,1)S(1)}, u32[]{:S(2)}, u32[]{:S(2)}) async-start(bf16[16,32,1536]{2,1,0:T(8,128)(2,1)} %bitcast.21), calls=%async_computation.3 | async-start | bytes 3145728 | tf_op jit(solution)/shard_map/all_to_all | solution.py:370
  116.7 8.8 %experts.3 = bf16[512,1536]{1,0:T(8,128)(2,1)} custom-call(bf16[512,1536]{1,0:T(8,128)(2,1)} %bitcast.18, bf16[1,1536,768]{2,1,0:T(8,128)(2,1)} %w_gate.3, bf16[1,1536,768]{2,1,0:T(8,128)(2,1)} %w_up.3, bf16[1,768,1536]{2,1,0:T(8,128)(2,1)} %w_down.3), custom_call_target="tpu_custom_call" | custom-call | flops 3623878656 | bytes 7077888 | tf_op jit(solution)/shard_map/experts/pallas_call | solution.py:326
  125.5 14.1 %all-to-all-done.3 = bf16[16,32,1536]{2,1,0:T(8,128)(2,1)S(1)} async-done(((bf16[16,32,1536]{2,1,0:T(8,128)(2,1)}), bf16[16,32,1536]{2,1,0:T(8,128)(2,1)S(1)}, u32[]{:S(2)}, u32[]{:S(2)}) %all-to-all-start.3) | async-done | bytes 1572896 | tf_op jit(solution)/shard_map/all_to_all | solution.py:370
  139.5 1.1 copy-done.1
  140.7 3.7 %all-to-all-start.2 = ((bf16[16,32,1536]{2,1,0:T(8,128)(2,1)}), bf16[16,32,1536]{2,1,0:T(8,128)(2,1)S(1)}, u32[]{:S(2)}, u32[]{:S(2)}) async-start(bf16[16,32,1536]{2,1,0:T(8,128)(2,1)} %bitcast.20), calls=%async_computation.2 | async-start | bytes 3145728 | tf_op jit(solution)/shard_map/all_to_all | solution.py:370
  144.4 2.9 %partial.1 = bf16[128,1536]{1,0:T(8,128)(2,1)} custom-call(bf16[128,512]{1,0:T(8,128)(2,1)} %get-tuple-element.50.high, bf16[128,512]{1,0:T(8,128)(2,1)} %get-tuple-element.51.low, bf16[512,1536]{1,0:T(8,128)(2,1)} %bitcast.16), custom_call_target="tpu_custom_call" | custom-call | tf_op jit(solution)/shard_map/partial/pallas_call | solution.py:502
  147.3 3.3 %collective-permute-start.5 = (bf16[128,1536]{1,0:T(8,128)(2,1)}, bf16[128,1536]{1,0:T(8,128)(2,1)S(1)}, u32[]{:S(2)}, u32[]{:S(2)}) collective-permute-start(bf16[128,1536]{1,0:T(8,128)(2,1)} %partial.1), channel_id=1, source_target_pairs={{0,24},{4,28},{8,16},{12,20},{16,8},{20,12},{24,0},{28,4},{1,25},{... | collective-permute-start | bytes 1179656 | tf_op jit(solution)/shard_map/ppermute | solution.py:510
  150.6 16.8 %all-to-all-done.2 = bf16[16,32,1536]{2,1,0:T(8,128)(2,1)S(1)} async-done(((bf16[16,32,1536]{2,1,0:T(8,128)(2,1)}), bf16[16,32,1536]{2,1,0:T(8,128)(2,1)S(1)}, u32[]{:S(2)}, u32[]{:S(2)}) %all-to-all-start.2) | async-done | bytes 1572896 | tf_op jit(solution)/shard_map/all_to_all | solution.py:370
  167.4 7.0 %collective-permute-done.5.far = bf16[128,1536]{1,0:T(8,128)(2,1)S(1)} collective-permute-done((bf16[128,1536]{1,0:T(8,128)(2,1)}, bf16[128,1536]{1,0:T(8,128)(2,1)S(1)}, u32[]{:S(2)}, u32[]{:S(2)}) %collective-permute-start.5) | collective-permute-done | bytes 393248 | tf_op jit(solution)/shard_map/ppermute | solution.py:510
  175.2 3.1 %final.1 = bf16[128,1536]{1,0:T(8,128)(2,1)} custom-call(s32[1]{0:T(128)S(6)} %copy.20.slot, bf16[64,1536]{1,0:T(8,128)(2,1)} %get-tuple-element.28.staying, bf16[64,1536]{1,0:T(8,128)(2,1)} %get-tuple-element.37.moved, bf16[128,512]{1,0:T(8,128)(2,1)} %get-tuple-element.47.high, bf16[128,512]{1,0:T(8,128)(2,1)} %get-tuple-element.48.low, ...), custom_call_target="tpu_custom_call" | custom-call | tf_op jit(solution)/shard_map/final/pallas_call | solution.py:512
  (25 shorter events, 4.2 us)
Async XLA Ops:
  5.0 3.0 %collective-permute-start.1 = (bf16[1040,512]{1,0:T(8,128)(2,1)}, bf16[1040,512]{1,0:T(8,128)(2,1)S(1)}, u32[]{:S(2)}, u32[]{:S(2)}) collective-permute-start(bf16[1040,512]{1,0:T(8,128)(2,1)} %leaving.1.rest_0_), channel_id=1, source_target_pairs={{0,1},{1,0},{2,3},{3,2},{4,5},{5,4},{6,7},{7,6},{8,9},{9,8},{10,11... | collective-permute-start | bytes 3194888 | tf_op jit(solution)/shard_map/ppermute | solution.py:382
  5.5 11.5 %copy-start.7 = (bf16[1536]{0:T(1024)(128)(2,1)S(1)}, bf16[1536]{0:T(1024)(128)(2,1)}, u32[]{:S(2)}) copy-start(bf16[1536]{0:T(1024)(128)(2,1)} %param.29) | copy-start | bytes 9220
  5.5 12.1 %copy-start.8 = (bf16[1536]{0:T(1024)(128)(2,1)S(1)}, bf16[1536]{0:T(1024)(128)(2,1)}, u32[]{:S(2)}) copy-start(bf16[1536]{0:T(1024)(128)(2,1)} %param.26) | copy-start | bytes 9220
  8.0 1.0 copy-start.3
  9.0 26.7 %collective-permute-start.2 = (bf16[1040,512]{1,0:T(8,128)(2,1)S(1)}, bf16[1040,512]{1,0:T(8,128)(2,1)S(1)}, u32[]{:S(2)}, u32[]{:S(2)}) collective-permute-start(bf16[1040,512]{1,0:T(8,128)(2,1)S(1)} %broadcast_select_fusion), channel_id=1, source_target_pairs={{0,2},{1,3},{2,0},{3,1},{4,6},{5,7},{6,4},{7,5},{8,10},{9,11},{10,... | collective-permute-start | bytes 3194888 | tf_op jit(solution)/shard_map/ppermute | solution.py:391
  13.4 16.1 %collective-permute-start = (s32[4,128]{1,0:T(4,128)}, s32[4,128]{1,0:T(4,128)S(1)}, u32[]{:S(2)}, u32[]{:S(2)}) collective-permute-start(s32[4,128]{1,0:T(4,128)} %get-tuple-element.31.ids_t), channel_id=1, source_target_pairs={{0,24},{4,28},{8,16},{12,20},{16,8},{20,12},{24,0},{28,4},{1,25},{... | collective-permute-start | bytes 6152 | tf_op jit(solution)/shard_map/ppermute | solution.py:409
  29.2 21.4 %collective-permute-start.3 = (bf16[64,1536]{1,0:T(8,128)(2,1)}, bf16[64,1536]{1,0:T(8,128)(2,1)S(1)}, u32[]{:S(2)}, u32[]{:S(2)}) collective-permute-start(bf16[64,1536]{1,0:T(8,128)(2,1)} %get-tuple-element.39.staying), channel_id=1, source_target_pairs={{0,24},{4,28},{8,16},{12,20},{16,8},{20,12},{24,0},{28,4},{1,25},{... | collective-permute-start | bytes 589832 | tf_op jit(solution)/shard_map/ppermute | solution.py:439
  29.5 0.6 copy-start.10
  35.7 1.0 copy-start.9
  43.9 8.6 %collective-permute-start.4 = (bf16[64,1536]{1,0:T(8,128)(2,1)}, bf16[64,1536]{1,0:T(8,128)(2,1)S(1)}, u32[]{:S(2)}, u32[]{:S(2)}) collective-permute-start(bf16[64,1536]{1,0:T(8,128)(2,1)} %get-tuple-element.40.moved), channel_id=1, source_target_pairs={{0,24},{4,28},{8,16},{12,20},{16,8},{20,12},{24,0},{28,4},{1,25},{... | collective-permute-start | bytes 589832 | tf_op jit(solution)/shard_map/ppermute | solution.py:464
  50.6 1.9 %copy-start.5 = (bf16[64,1536]{1,0:T(8,128)(2,1)}, bf16[64,1536]{1,0:T(8,128)(2,1)S(1)}, u32[]{:S(2)}) copy-start(bf16[64,1536]{1,0:T(8,128)(2,1)S(1)} %collective-permute-done.3.staying) | copy-start | bytes 589828
  52.5 0.7 copy-start.6
  84.9 26.7 %all-to-all-start.1 = ((bf16[16,32,1536]{2,1,0:T(8,128)(2,1)}), bf16[16,32,1536]{2,1,0:T(8,128)(2,1)S(1)}, u32[]{:S(2)}, u32[]{:S(2)}) async-start(bf16[16,32,1536]{2,1,0:T(8,128)(2,1)} %bitcast.7), calls=%async_computation.1 | async-start | bytes 3145728 | tf_op jit(solution)/shard_map/all_to_all | solution.py:370
  111.7 1.1 copy-start.2
  112.8 26.7 %all-to-all-start.3 = ((bf16[16,32,1536]{2,1,0:T(8,128)(2,1)}), bf16[16,32,1536]{2,1,0:T(8,128)(2,1)S(1)}, u32[]{:S(2)}, u32[]{:S(2)}) async-start(bf16[16,32,1536]{2,1,0:T(8,128)(2,1)} %bitcast.21), calls=%async_computation.3 | async-start | bytes 3145728 | tf_op jit(solution)/shard_map/all_to_all | solution.py:370
  139.5 1.1 copy-start.1
  140.7 26.7 %all-to-all-start.2 = ((bf16[16,32,1536]{2,1,0:T(8,128)(2,1)}), bf16[16,32,1536]{2,1,0:T(8,128)(2,1)S(1)}, u32[]{:S(2)}, u32[]{:S(2)}) async-start(bf16[16,32,1536]{2,1,0:T(8,128)(2,1)} %bitcast.20), calls=%async_computation.2 | async-start | bytes 3145728 | tf_op jit(solution)/shard_map/all_to_all | solution.py:370
  147.3 27.1 %collective-permute-start.5 = (bf16[128,1536]{1,0:T(8,128)(2,1)}, bf16[128,1536]{1,0:T(8,128)(2,1)S(1)}, u32[]{:S(2)}, u32[]{:S(2)}) collective-permute-start(bf16[128,1536]{1,0:T(8,128)(2,1)} %partial.1), channel_id=1, source_target_pairs={{0,24},{4,28},{8,16},{12,20},{16,8},{20,12},{24,0},{28,4},{1,25},{... | collective-permute-start | bytes 1179656 | tf_op jit(solution)/shard_map/ppermute | solution.py:510
  167.4 7.0 %copy-start = (bf16[16,32,1536]{2,1,0:T(8,128)(2,1)}, bf16[16,32,1536]{2,1,0:T(8,128)(2,1)S(1)}, u32[]{:S(2)}) copy-start(bf16[16,32,1536]{2,1,0:T(8,128)(2,1)S(1)} %all-to-all-done.2) | copy-start | bytes 4718596
  174.4 0.8 copy-start.4

commit v3 on v2

v3 whole, which is shorter than its diff:
```python
import functools

import jax
import jax.numpy as jnp
import numpy as np
from jax import lax
from jax.experimental import pallas as pl
from jax.experimental.pallas import tpu as pltpu
from jax.sharding import PartitionSpec as P

QUERY_HEADS = 12
KEY_VALUE_HEADS = 2
HEAD_SIZE = 128
GROUP = QUERY_HEADS // KEY_VALUE_HEADS
CAP = 32
EPSILON = 1e-06
ROPE_BASE = 1000000.0
MASKED = -1e30
LOG2E = 1.4426950408889634
MIB = 1024 * 1024
NOTE = 16
NOTE_BASE = 32
AXES = ("req", "ep")

VMEM = pl.BlockSpec(memory_space=pltpu.VMEM)
SMEM = pl.BlockSpec(memory_space=pltpu.SMEM)
ANY = pl.BlockSpec(memory_space=pl.ANY)
HBM = pl.BlockSpec(memory_space=pltpu.HBM)


def in_hbm(*values):
    return [pltpu.with_memory_space_constraint(value, pltpu.HBM) for value in values]


def in_vmem(*values):
    return [pltpu.with_memory_space_constraint(value, pltpu.VMEM) for value in values]


def load_all(pairs, sems):
    copies = [
        pltpu.make_async_copy(source, target, sems.at[i])
        for i, (source, target) in enumerate(pairs)
    ]
    for copy in copies:
        copy.start()
    return copies


def finish(copies):
    for copy in copies:
        copy.wait()


def dot(a, b, dims=((1,), (0,))):
    return lax.dot_general(a, b, (dims, ((), ())), preferred_element_type=jnp.float32)


def rms_scale(values, scaling):
    widened = values.astype(jnp.float32)
    spread = jnp.mean(widened * widened, axis=-1, keepdims=True)
    return (widened * lax.rsqrt(spread + EPSILON) * scaling.astype(jnp.float32)).astype(
        jnp.bfloat16
    )


def attend(queries, cached, fresh, reach, length):
    scale = HEAD_SIZE ** (-0.5) * LOG2E
    key_width = KEY_VALUE_HEADS * HEAD_SIZE
    context = cached.shape[0]
    in_cache = lax.broadcasted_iota(jnp.int32, (1, context), 1) < length
    cache_bias = jnp.where(in_cache, 0.0, MASKED)
    tree_bias = jnp.concatenate([jnp.where(reach > 0.5, 0.0, MASKED)] * GROUP, axis=0)
    outs = []
    for kv in range(KEY_VALUE_HEADS):
        cols = slice(kv * HEAD_SIZE, (kv + 1) * HEAD_SIZE)
        vcols = slice(key_width + kv * HEAD_SIZE, key_width + (kv + 1) * HEAD_SIZE)
        heads = [
            queries[:, (kv * GROUP + g) * HEAD_SIZE : (kv * GROUP + g + 1) * HEAD_SIZE]
            for g in range(GROUP)
        ]
        stacked = jnp.concatenate(heads, axis=0)
        first = dot(stacked, cached[:, cols], ((1,), (1,))) * scale + cache_bias
        second = dot(stacked, fresh[:, cols], ((1,), (1,))) * scale + tree_bias
        highest = jnp.maximum(
            jnp.max(first, axis=-1, keepdims=True), jnp.max(second, axis=-1, keepdims=True)
        )
        first = jnp.exp2(first - highest)
        second = jnp.exp2(second - highest)
        total = jnp.sum(first, axis=-1, keepdims=True) + jnp.sum(second, axis=-1, keepdims=True)
        mixed = dot(first.astype(jnp.bfloat16), cached[:, vcols])
        mixed = mixed + dot(second.astype(jnp.bfloat16), fresh[:, vcols])
        mixed = (mixed / total).astype(jnp.bfloat16)
        step = queries.shape[0]
        outs += [mixed[g * step : (g + 1) * step] for g in range(GROUP)]
    return jnp.concatenate(outs, axis=1)


def load_pages(table, row, pool, target, sems):
    page = pool.shape[1]
    copies = [
        pltpu.make_async_copy(
            pool.at[table[row, i]], target.at[pl.ds(i * page, page)], sems.at[i]
        )
        for i in range(table.shape[1])
    ]
    for copy in copies:
        copy.start()
    return copies


def leaving_kernel(slot, dest, lengths, table, pool, first, second, pages, note, sems, out_sems):
    loads = load_pages(table, slot[0], pool, pages, sems)
    length = lengths[slot[0]]
    half = second.shape[0]
    page = 2 * half // len(loads)
    blank = jnp.zeros((NOTE, 128), jnp.float32)
    for at, value in enumerate((dest[0], length // NOTE_BASE, length % NOTE_BASE)):
        filled = blank + value.astype(jnp.float32)
        note[:, at * 128 : (at + 1) * 128] = filled.astype(jnp.bfloat16)
    note[:, 3 * 128 :] = jnp.zeros((NOTE, note.shape[1] - 3 * 128), jnp.bfloat16)
    stores = [pltpu.make_async_copy(note, first.at[pl.ds(half, NOTE)], out_sems.at[len(loads)])]
    stores[0].start()
    for i, load in enumerate(loads):
        load.wait()
        target = first if i * page < half else second
        stores.append(
            pltpu.make_async_copy(
                pages.at[pl.ds(i * page, page)],
                target.at[pl.ds(i * page % half, page)],
                out_sems.at[i],
            )
        )
        stores[-1].start()
    finish(stores)


def slots_of(ids_t, first, shown):
    tokens = ids_t.shape[1]
    names = lax.broadcasted_iota(jnp.int32, (shown, tokens), 0) + first
    assigned = jnp.zeros((shown, tokens), jnp.bool_)
    for k in range(ids_t.shape[0]):
        assigned = assigned | (ids_t[k : k + 1, :] == names)
    before = lax.broadcasted_iota(jnp.int32, (tokens, tokens), 0) < lax.broadcasted_iota(
        jnp.int32, (tokens, tokens), 1
    )
    ranks = dot(one_hot(assigned), one_hot(before))
    return assigned, jnp.where(assigned, ranks, -1.0)


def one_hot(flags):
    return jnp.where(flags, 1.0, 0.0).astype(jnp.bfloat16)


def flipped(values):
    size = values.shape[1]
    same = lax.broadcasted_iota(jnp.int32, (size, size), 0) == lax.broadcasted_iota(
        jnp.int32, (size, size), 1
    )
    if values.shape[0] == 1:
        return jnp.sum(jnp.where(same, values, 0.0), axis=1, keepdims=True)
    return dot(one_hot(same), values.astype(jnp.bfloat16), ((1,), (1,)))


def write_routes(split, first, ids, table):
    shown = table.shape[0] // (split * CAP)
    _, slots = slots_of(ids, first, shown)
    wanted = lax.broadcasted_iota(jnp.int32, (shown, split * CAP, ids.shape[1]), 1) % CAP
    hot = jnp.where(slots.astype(jnp.int32)[:, None, :] == wanted, 1.0, 0.0)
    table[...] = hot.reshape(table.shape).astype(jnp.bfloat16)


def travel_order(slot, ids):
    half = ids.shape[1] // 2
    return jnp.where(slot == 0, jnp.concatenate([ids[:, half:], ids[:, :half]], axis=1), ids)


def routes_kernel(split, base, slot, ids_t, table, ordered, names, sems):
    finish(load_all(((ids_t, names),), sems))
    ids = travel_order(slot[0], names[...])
    ordered[...] = ids
    write_routes(split, base[0], ids, table)


def far_routes_kernel(split, base, parcel, table, ordered):
    draft = parcel.shape[0] - NOTE
    ids = parcel[draft:, : ordered.shape[1]].astype(jnp.float32).astype(jnp.int32)
    ids = ids[: ordered.shape[0]]
    ordered[...] = ids
    write_routes(split, base[0], ids, table)


def shares_kernel(split, base, w_router_t, *rest):
    inputs, out, (weights, names, done, sems, out_sem) = rest[:6], rest[6], rest[7:]
    finish(
        load_all(
            ((w_router_t, weights), (inputs[4], names.at[0]), (inputs[5], names.at[1])), sems
        )
    )
    experts = weights.shape[0]
    tokens, width = done.shape[2:]
    spread = one_hot(
        lax.broadcasted_iota(jnp.int32, (experts, width), 1) // (split * CAP) + base[0]
        == lax.broadcasted_iota(jnp.int32, (experts, width), 0)
    )
    wanted = lax.broadcasted_iota(jnp.int32, (tokens, width), 1) % CAP
    for i in range(2):
        staying, moved = inputs[2 * i : 2 * i + 2]
        rows = jnp.concatenate([staying[: moved.shape[0], :], moved[...]], axis=0)
        logits = dot(rows, weights[...], ((1,), (1,)))
        _, slots_t = slots_of(names.at[i], 0, experts)
        slots = flipped(slots_t)
        squashed = jnp.where(slots >= 0.0, jax.nn.sigmoid(logits), 0.0)
        share = squashed / jnp.sum(squashed, axis=1, keepdims=True)
        hit = dot(slots.astype(jnp.bfloat16), spread).astype(jnp.int32) == wanted
        high = share.astype(jnp.bfloat16)
        low = (share - high.astype(jnp.float32)).astype(jnp.bfloat16)
        done[i, 0] = jnp.where(hit, dot(high, spread), 0.0).astype(jnp.bfloat16)
        done[i, 1] = jnp.where(hit, dot(low, spread), 0.0).astype(jnp.bfloat16)
    finish(load_all(((done, out),), out_sem))


def rotate(projected, depth, length, spectrum, query_width):
    angles = (depth + length) * spectrum
    cosine = jnp.cos(angles)
    sine = jnp.sin(angles)
    first_half = lax.broadcasted_iota(jnp.int32, (1, HEAD_SIZE), 1) < HEAD_SIZE // 2
    sine = jnp.where(first_half, -sine, sine)
    key_width = KEY_VALUE_HEADS * HEAD_SIZE
    turned = []
    for h in range(QUERY_HEADS + KEY_VALUE_HEADS):
        part = projected[:, h * HEAD_SIZE : (h + 1) * HEAD_SIZE]
        swapped = jnp.concatenate([part[:, HEAD_SIZE // 2 :], part[:, : HEAD_SIZE // 2]], axis=1)
        turned.append((part * cosine + swapped * sine).astype(jnp.bfloat16))
    values = projected[:, query_width + key_width :].astype(jnp.bfloat16)
    return (
        jnp.concatenate(turned[:QUERY_HEADS], axis=1),
        jnp.concatenate(turned[QUERY_HEADS:] + [values], axis=1),
    )


def front_kernel(
    slot, lengths, table, hidden, parents, path, spectrum, gain, moe_gain, ids_t, w_qkv, w_out,
    pool, moved_projected, moved_reach, moved_picked, compact, staying, parcel,
    weights, tokens, lines, trees, table_row, gains, names_t, w_in, cache, sems, page_sems,
):
    stay = 1 - slot[0]
    loads = load_all(
        (
            (hidden, tokens), (gain, gains.at[0]), (w_qkv, w_in), (moe_gain, gains.at[1]),
            (parents, lines), (path, trees), (spectrum, table_row),
            (ids_t, names_t), (w_out, weights),
        ),
        sems,
    )
    pages = load_pages(table, stay, pool, cache, page_sems)
    draft = parents.shape[1]
    query_width = w_out.shape[0]
    finish(loads[:3])
    rows = [
        tokens[pl.ds(pl.multiple_of(r * draft, draft), draft), :] for r in (stay, slot[0])
    ]
    normed = rms_scale(jnp.concatenate(rows, axis=0), gains[0])
    projected = dot(normed, w_in[...])
    names = lax.broadcasted_iota(jnp.int32, (draft, draft), 1)
    itself = names == lax.broadcasted_iota(jnp.int32, (draft, draft), 0)
    finish(loads[3:8])
    reaches = []
    for r in (stay, slot[0]):
        above = flipped(lines[pl.ds(r, 1), :].astype(jnp.float32)).astype(jnp.int32)
        reached = jnp.where((above == names) | itself, 1.0, 0.0)
        for _ in range(max(1, (draft - 1).bit_length())):
            half = reached.astype(jnp.bfloat16)
            reached = jnp.minimum(dot(half, half), 1.0)
        reaches.append(reached)
    picks = [
        one_hot(flipped(trees[pl.ds(r, 1), :].astype(jnp.float32)).astype(jnp.int32) == names)
        for r in (stay, slot[0])
    ]
    moved_projected[...] = projected[draft:]
    moved_reach[...] = reaches[1]
    moved_picked[...] = picks[1]
    depth = jnp.sum(reaches[0], axis=-1, keepdims=True) - 1.0
    length = lengths[stay]
    queries, fresh = rotate(
        projected[:draft], depth, length.astype(jnp.float32), table_row[...], query_width
    )
    compact[...] = dot(picks[0], fresh).astype(jnp.bfloat16)
    finish(pages)
    attended = attend(queries, cache, fresh, reaches[0], length)
    finish(loads[8:])
    kept = (rows[0].astype(jnp.float32) + dot(attended, weights[...])).astype(jnp.bfloat16)
    staying[...] = kept
    parcel[:draft, :] = rms_scale(kept, gains[1])
    ids = travel_order(slot[0], names_t[...]).astype(jnp.float32)
    blank = jnp.zeros((NOTE - ids.shape[0], ids.shape[1]), jnp.float32)
    parcel[draft:, :] = jnp.zeros((NOTE, parcel.shape[1]), jnp.bfloat16)
    parcel[draft:, : ids.shape[1]] = jnp.concatenate([ids, blank], axis=0).astype(jnp.bfloat16)


def arrival_kernel(
    slot, me, projected, reach, picked, staying_compact, hidden, spectrum, gain, w_out, *rest,
):
    sources = rest[:-11]
    sources = list(zip(sources[0::2], sources[1::2]))
    moved, moved_normed, compact, cache, notes, weights, rows, table_row, gains, sems, note_sems = (
        rest[-11:]
    )
    half = cache.shape[0] // 2
    draft = projected.shape[0]
    query_width = weights.shape[0]
    note_loads = load_all(
        [(first.at[pl.ds(half, NOTE)], notes.at[i]) for i, (first, _) in enumerate(sources)],
        note_sems,
    )
    own = pl.ds(pl.multiple_of(slot[0] * draft, draft), draft)
    other = pl.ds(pl.multiple_of((1 - slot[0]) * draft, draft), draft)
    loads = load_all(
        ((hidden.at[own], rows), (spectrum, table_row), (gain, gains), (w_out, weights)),
        sems.at[pl.ds(2, 4)],
    )
    depth = jnp.sum(reach[...], axis=-1, keepdims=True) - 1.0
    finish(note_loads)

    def noted(i, at):
        values = notes[i, :, at * 128 : (at + 1) * 128]
        return jnp.max(values.astype(jnp.float32)).astype(jnp.int32)

    def cache_loads(pair):
        return [
            pltpu.make_async_copy(pair[0].at[pl.ds(0, half)], cache.at[pl.ds(0, half)], sems.at[0]),
            pltpu.make_async_copy(pair[1], cache.at[pl.ds(half, half)], sems.at[1]),
        ]

    length = jnp.int32(0)
    for i, pair in enumerate(sources):
        mine = noted(i, 0) == me[0]
        length = jnp.where(mine, noted(i, 1) * NOTE_BASE + noted(i, 2), length)

        @pl.when(mine)
        def _(pair=pair):
            for copy in cache_loads(pair):
                copy.start()

    finish(loads[:3])
    queries, fresh = rotate(
        projected[...], depth, length.astype(jnp.float32), table_row[...], query_width
    )
    finish(cache_loads(sources[0]))
    attended = attend(queries, cache, fresh, reach[...], length)
    finish(loads[3:])
    kept = rows[...].astype(jnp.float32) + dot(attended, weights[...])
    kept = kept.astype(jnp.bfloat16)
    moved[...] = kept
    moved_normed[...] = rms_scale(kept, gains[...])
    compact[own, :] = dot(picked[...], fresh).astype(jnp.bfloat16)
    compact[other, :] = staying_compact[...]


def pack_kernel(routes, staying, moved, out, rows, sems):
    both = jnp.concatenate([staying[: moved.shape[0], :], moved[...]], axis=0)
    group = rows.shape[0] // 2
    stores = []
    for i in range(2):
        span = pl.ds(i * group, group)
        rows[span] = dot(routes[i * group : (i + 1) * group, :], both).astype(jnp.bfloat16)
        stores += load_all(((rows.at[span], out.at[span]),), sems.at[pl.ds(i, 1)])
    finish(stores)


def expert_kernel(arrived, w_gate, w_up, w_down, out, gates, ups, downs, act, done, sems):
    count, model = out.shape
    hidden_units = gates.shape[1]
    chunk = 256 if hidden_units % 256 == 0 else hidden_units
    wide = 512 if model % 512 == 0 else model
    block = 256 if count % 256 == 0 else count
    chunks = [pl.ds(i * chunk, chunk) for i in range(hidden_units // chunk)]
    wides = [pl.ds(i * wide, wide) for i in range(model // wide)]
    loads = []
    for i, cols in enumerate(chunks):
        pairs = ((w_gate.at[0, :, cols], gates.at[:, cols]), (w_up.at[0, :, cols], ups.at[:, cols]))
        loads.append(load_all(pairs, sems.at[i]))
    down_loads = [
        load_all(((w_down.at[0, :, cols], downs.at[:, cols]),), sems.at[len(chunks) + i])
        for i, cols in enumerate(wides)
    ]
    blocks = [slice(i * block, (i + 1) * block) for i in range(count // block)]
    for load, cols in zip(loads, chunks):
        finish(load)
        for span in blocks:
            rows = arrived[span, :]
            gated = dot(rows, gates[:, cols])
            upped = dot(rows, ups[:, cols])
            act[span, cols] = (jnp.maximum(gated, 0.0) * upped).astype(jnp.bfloat16)
    stores = []
    for i, cols in enumerate(wides):
        finish(down_loads[i])
        for span in blocks:
            done[span, cols] = dot(act[span, :], downs[:, cols]).astype(jnp.bfloat16)
        stores += load_all(((done.at[:, cols], out.at[:, cols]),), sems.at[len(chunks) + i])
    finish(stores)


def partial_kernel(shares, rows, out, pair, sems):
    finish(load_all(((shares.at[1], pair),), sems))
    values = rows[...]
    out[...] = (dot(pair[0], values) + dot(pair[1], values)).astype(jnp.bfloat16)


def final_kernel(slot, shares, staying, moved, far, rows, out, pair, sems):
    finish(load_all(((shares.at[0], pair),), sems))
    draft = staying.shape[0]
    values = rows[...]
    total = dot(pair[0], values) + dot(pair[1], values) + far[...].astype(jnp.float32)
    for at, kept, part in (
        (1 - slot[0], staying, total[:draft]), (slot[0], moved, total[draft:])
    ):
        at = pl.ds(pl.multiple_of(at * draft, draft), draft)
        out[at, :] = (kept[...].astype(jnp.float32) + part).astype(jnp.bfloat16)


def params(mib, rows=512):
    return pltpu.CompilerParams(vmem_limit_bytes=min(60, mib * max(rows, 512) // 512) * MIB)


def cost(flops, moved):
    return pl.CostEstimate(flops=int(flops), bytes_accessed=int(moved), transcendentals=0)


def run_experts(arrived, w_gate, w_up, w_down):
    count, model = arrived.shape
    hidden_units = w_gate.shape[2]
    return pl.pallas_call(
        expert_kernel,
        in_specs=[VMEM] + [HBM] * 3,
        out_specs=HBM,
        out_shape=pltpu.HBM((count, model), jnp.bfloat16),
        scratch_shapes=[
            pltpu.VMEM((model, hidden_units), jnp.bfloat16),
            pltpu.VMEM((model, hidden_units), jnp.bfloat16),
            pltpu.VMEM((hidden_units, model), jnp.bfloat16),
            pltpu.VMEM((count, hidden_units), jnp.bfloat16),
            pltpu.VMEM((count, model), jnp.bfloat16),
            pltpu.SemaphoreType.DMA((8, 2)),
        ],
        compiler_params=params(16 + 3 * count * model // MIB),
        cost_estimate=cost(6 * count * model * hidden_units, 6 * model * hidden_units),
        name="experts",
    )(*in_vmem(arrived), *in_hbm(w_gate, w_up, w_down))


def per_device(
    hidden, parents, path, cache_len, page_table, kv_pool, mig_slot, mig_dest,
    attn_gain, w_qkv, w_out, moe_gain, w_router, expert_ids, w_gate, w_up, w_down,
):
    bf16 = jnp.bfloat16
    requests, draft = parents.shape
    tokens, model = hidden.shape
    req_count = lax.axis_size("req")
    ep_count = lax.axis_size("ep")
    device_count = req_count * ep_count
    half_count = device_count // 2
    experts = w_router.shape[1]
    split = device_count // experts
    pages = page_table.shape[1]
    page, kv_width = kv_pool.shape[1:]
    context = pages * page
    query_width = w_out.shape[0]
    slot_rows = half_count * CAP
    req_index = lax.axis_index("req")
    ep_index = lax.axis_index("ep")
    groups = [[h * half_count + i for i in range(half_count)] for h in range(2)]
    inner = req_count // 4
    swap = [(i, (3 - i // inner) * inner + i % inner) for i in range(req_count)]
    base = (req_index // (req_count // 2) * (experts // 2)).astype(jnp.int32).reshape(1)

    def within_half(rows):
        return lax.all_to_all(rows, AXES, 0, 0, tiled=True, axis_index_groups=groups)

    f32 = jnp.float32
    half_cache = context // 2
    leaving = pl.pallas_call(
        leaving_kernel,
        in_specs=[SMEM] * 4 + [HBM],
        out_specs=[HBM] * 2,
        out_shape=[
            pltpu.HBM((half_cache + NOTE, kv_width), bf16),
            pltpu.HBM((half_cache, kv_width), bf16),
        ],
        scratch_shapes=[
            pltpu.VMEM((context, kv_width), bf16),
            pltpu.VMEM((NOTE, kv_width), bf16),
            pltpu.SemaphoreType.DMA((pages,)),
            pltpu.SemaphoreType.DMA((pages + 1,)),
        ],
        compiler_params=params(60),
        cost_estimate=cost(0, 4 * context * kv_width),
        name="leaving",
    )(mig_slot, mig_dest, cache_len, page_table, *in_hbm(kv_pool))
    chips = ep_count // 2
    chip = ep_index // 2
    core = ep_index % 2
    pairs = [(i, i ^ 1) for i in range(ep_count)]
    sibling = [lax.ppermute(part, "ep", pairs) for part in leaving]
    sources = [*leaving, *sibling]
    payloads = []
    for k in range(1, chips):
        target = (chip + k) % chips * 2 + core
        moves = [(i, ((i // 2 + k) % chips) * 2 + i % 2) for i in range(ep_count)]
        for mine, other in zip(leaving, sibling):
            payload = jnp.where(mig_dest[0] == target, mine, other)
            payloads.append(payload)
            sources.append(lax.ppermute(payload, "ep", moves))
    me = ep_index.astype(jnp.int32).reshape(1)

    route_shapes = [
        pltpu.VMEM((slot_rows, tokens), bf16),
        pltpu.HBM((expert_ids.shape[1], tokens), jnp.int32),
    ]
    frequencies = ROPE_BASE ** (-2.0 * np.arange(HEAD_SIZE // 2) / HEAD_SIZE)
    spectrum = jnp.asarray(np.concatenate([frequencies] * 2)[None].astype(np.float32))
    row_gain = attn_gain.reshape(1, model)
    row_moe_gain = moe_gain.reshape(1, model)
    hidden, *_ = lax.optimization_barrier((hidden, *payloads))
    projected, reach, picked, staying_compact, staying, parcel = pl.pallas_call(
        front_kernel,
        in_specs=[SMEM] * 3 + [HBM] * 10,
        out_specs=[VMEM] * 6,
        out_shape=[
            pltpu.VMEM((draft, w_qkv.shape[1]), f32),
            pltpu.VMEM((draft, draft), f32),
            pltpu.VMEM((draft, draft), bf16),
            pltpu.VMEM((draft, kv_width), bf16),
            pltpu.VMEM((draft, model), bf16),
            pltpu.VMEM((draft + NOTE, model), bf16),
        ],
        scratch_shapes=[
            pltpu.VMEM(w_out.shape, bf16),
            pltpu.VMEM((tokens, model), bf16),
            pltpu.VMEM(parents.shape, jnp.int32),
            pltpu.VMEM(path.shape, jnp.int32),
            pltpu.VMEM(spectrum.shape, f32),
            pltpu.VMEM((2, 1, model), bf16),
            pltpu.VMEM((expert_ids.shape[1], tokens), jnp.int32),
            pltpu.VMEM(w_qkv.shape, bf16),
            pltpu.VMEM((context, kv_width), bf16),
            pltpu.SemaphoreType.DMA((9,)),
            pltpu.SemaphoreType.DMA((pages,)),
        ],
        compiler_params=params(36),
        cost_estimate=cost(3e9, 3e6),
        name="front",
    )(
        mig_slot, cache_len, page_table,
        *in_hbm(
            hidden, parents, path, spectrum, row_gain, row_moe_gain, expert_ids.T, w_qkv, w_out,
            kv_pool,
        ),
    )
    far_parcel = lax.ppermute(parcel, "req", swap)
    names_t, _ = lax.optimization_barrier((expert_ids.T, projected))
    routes, ids = pl.pallas_call(
        functools.partial(routes_kernel, split),
        in_specs=[SMEM, SMEM, HBM],
        out_specs=[VMEM] * 2,
        out_shape=route_shapes,
        scratch_shapes=[
            pltpu.VMEM((expert_ids.shape[1], tokens), jnp.int32),
            pltpu.SemaphoreType.DMA((1,)),
        ],
        compiler_params=params(6, slot_rows),
        cost_estimate=cost(1e8, 1e6),
        name="routes",
    )(base, mig_slot, *in_hbm(names_t))
    far_parcel, routes, *sources = lax.optimization_barrier((far_parcel, routes, *sources))
    moved, moved_normed, compact = pl.pallas_call(
        arrival_kernel,
        in_specs=[SMEM] * 2 + [VMEM] * 4 + [HBM] * (4 + len(sources)),
        out_specs=[VMEM] * 3,
        out_shape=[
            pltpu.VMEM((draft, model), bf16),
            pltpu.VMEM((draft, model), bf16),
            jax.ShapeDtypeStruct((tokens, kv_width), bf16),
        ],
        scratch_shapes=[
            pltpu.VMEM((context, kv_width), bf16),
            pltpu.VMEM((len(sources) // 2, NOTE, kv_width), bf16),
            pltpu.VMEM(w_out.shape, bf16),
            pltpu.VMEM((draft, model), bf16),
            pltpu.VMEM(spectrum.shape, f32),
            pltpu.VMEM((1, model), bf16),
            pltpu.SemaphoreType.DMA((6,)),
            pltpu.SemaphoreType.DMA((len(sources) // 2,)),
        ],
        compiler_params=params(24),
        cost_estimate=cost(4e9, 8e6),
        name="arrival",
    )(
        mig_slot, me, *in_vmem(projected, reach, picked, staying_compact),
        *in_hbm(hidden, spectrum, row_moe_gain, w_out, *sources),
    )
    far_moved = lax.ppermute(moved_normed, "req", swap)
    far_routes, far_ids = pl.pallas_call(
        functools.partial(far_routes_kernel, split),
        in_specs=[SMEM, VMEM],
        out_specs=[VMEM] * 2,
        out_shape=route_shapes,
        compiler_params=params(6, slot_rows),
        cost_estimate=cost(1e8, 1e6),
        name="far_routes",
    )(base, *in_vmem(far_parcel))

    def pack(table, first, second):
        return pl.pallas_call(
            pack_kernel,
            in_specs=[VMEM] * 3,
            out_specs=HBM,
            out_shape=pltpu.HBM((slot_rows, model), bf16),
            scratch_shapes=[
                pltpu.VMEM((slot_rows, model), bf16),
                pltpu.SemaphoreType.DMA((2,)),
            ],
            compiler_params=params(10, slot_rows),
            cost_estimate=cost(3e8, 2e6),
            name="pack",
        )(*in_vmem(table, first, second))

    near_packed = pack(routes, parcel, moved_normed)
    far_packed = pack(far_routes, far_parcel, far_moved)
    far_rows = within_half(far_packed)
    near_packed, far_rows = lax.optimization_barrier((near_packed, far_rows))
    near_rows = within_half(near_packed)
    shares = pl.pallas_call(
        functools.partial(shares_kernel, split),
        in_specs=[SMEM, HBM] + [VMEM] * 4 + [HBM] * 2,
        out_specs=HBM,
        out_shape=pltpu.HBM((2, 2, tokens, slot_rows), bf16),
        scratch_shapes=[
            pltpu.VMEM((experts, model), bf16),
            pltpu.VMEM((2,) + ids.shape, jnp.int32),
            pltpu.VMEM((2, 2, tokens, slot_rows), bf16),
            pltpu.SemaphoreType.DMA((3,)),
            pltpu.SemaphoreType.DMA((1,)),
        ],
        compiler_params=params(10, slot_rows),
        cost_estimate=cost(3e8, 1e6),
        name="shares",
    )(
        base, *in_hbm(w_router.T), *in_vmem(parcel, moved_normed, far_parcel, far_moved),
        *in_hbm(ids, far_ids),
    )
    far_out = run_experts(far_rows, w_gate, w_up, w_down)
    far_out, near_rows, shares = lax.optimization_barrier((far_out, near_rows, shares))
    far_back = within_half(far_out)
    near_out = run_experts(near_rows, w_gate, w_up, w_down)
    near_out, far_back = lax.optimization_barrier((near_out, far_back))
    far_sum = pl.pallas_call(
        partial_kernel,
        in_specs=[HBM, VMEM],
        out_specs=VMEM,
        out_shape=pltpu.VMEM((tokens, model), bf16),
        scratch_shapes=[
            pltpu.VMEM((2, tokens, slot_rows), bf16),
            pltpu.SemaphoreType.DMA((1,)),
        ],
        compiler_params=params(8, slot_rows),
        cost_estimate=cost(4e8, 2e6),
        name="partial",
    )(*in_hbm(shares), *in_vmem(far_back))
    own_far = lax.ppermute(far_sum, "req", swap)
    near_back = within_half(near_out)
    layer_out = pl.pallas_call(
        final_kernel,
        in_specs=[SMEM, HBM] + [VMEM] * 4,
        out_specs=VMEM,
        out_shape=jax.ShapeDtypeStruct((tokens, model), bf16),
        scratch_shapes=[
            pltpu.VMEM((2, tokens, slot_rows), bf16),
            pltpu.SemaphoreType.DMA((1,)),
        ],
        compiler_params=params(10, slot_rows),
        cost_estimate=cost(4e8, 2e6),
        name="final",
    )(mig_slot, *in_hbm(shares), *in_vmem(staying, moved, own_far, near_back))
    return layer_out, compact.reshape(requests, draft, kv_width)


def solution(mesh):
    rows = P(AXES, None)
    blocks = P(AXES, None, None)
    in_specs = (
        rows, rows, rows, P(AXES), rows, blocks, P(AXES), P(AXES),
        P(), P(), P(), P(), P(), rows, blocks, blocks, blocks,
    )
    return jax.shard_map(
        per_device, mesh=mesh, in_specs=in_specs, out_specs=(rows, blocks), check_vma=False
    )
```

time: 180 us -> 173 us (0.961)
  blocking collectives: 28.9 us -> 0 us
  waiting for transfers between devices: 55.9 us -> 84.8 us
  Pallas kernels: 58.2 us -> 44.8 us
  starting transfers between devices: 25.8 us -> 33.9 us
  local copies, waits for them, and re-layouts: 7.39 us -> 5.49 us
    all_to_all x1 -> x0, blocking collectives: 28.9 us -> none  [within_half(): lax.all_to_all(rows, AXES, 0, 0, tiled=True, axis_index_groups=groups)]
    ppermute x1, waiting for transfers between devices: 7.02 us -> 25 us  [per_device(): own_far = lax.ppermute(far_sum, 'req', swap)]
    pallas_call x13 -> x12, Pallas kernels: 58.2 us -> 44.8 us  [the longest x2 14.1 us: run_experts(): pl.pallas_call(expert_kernel, in_specs=[VMEM] + [HBM] * 3, out_specs=HBM,...]
    all_to_all x3 -> x4, waiting for transfers between devices: 40.3 us -> 47.3 us  [within_half(): lax.all_to_all(rows, AXES, 0, 0, tiled=True, axis_index_groups=groups)]
    all_to_all x3 -> x4, starting transfers between devices: 11.3 us -> 17.8 us  [within_half(): lax.all_to_all(rows, AXES, 0, 0, tiled=True, axis_index_groups=groups)]
    ppermute x1, waiting for transfers between devices: 1.91 us -> 4.69 us  [per_device(): far_moved = lax.ppermute(moved_normed, 'req', swap)]
    unnamed x22 -> x36, local copies, waits for them, and re-layouts: 6.19 us -> 4.3 us
    ppermute x4 -> x5, waiting for transfers between devices: 6.61 us -> 7.85 us  [the longest x1 5.39 us: per_device(): far_parcel = lax.ppermute(parcel, 'req', swap)]
  transfers between devices with their start and end apart: 9 -> 11, of which waited for: 7 -> 8; matrix products, arithmetic and copies ran while one was open for 1% -> 1% of each run, Pallas kernels for 28% -> 18%
where the time goes in v3:
time: 173 us; the launch traced here: 172 us
  waiting for transfers between devices  84.8 us (49%)
  Pallas kernels  44.8 us (26%)
  starting transfers between devices  33.9 us (20%)
  local copies, waits for them, and re-layouts  5.49 us (3%)
  between operations  2.34 us (1%)
    all_to_all x4, waiting for transfers between devices, within_half(): lax.all_to_all(rows, AXES, 0, 0, tiled=True, axis_index_groups=groups)  47.3 us
    ppermute x1, waiting for transfers between devices, per_device(): own_far = lax.ppermute(far_sum, 'req', swap)  25 us
    all_to_all x4, starting transfers between devices, within_half(): lax.all_to_all(rows, AXES, 0, 0, tiled=True, axis_index_groups=groups)  17.8 us
    pallas_call x2, Pallas kernels, run_experts(): pl.pallas_call(expert_kernel, in_specs=[VMEM] + [HBM] * 3, out_specs=HBM,...  14.1 us
    pallas_call x1, Pallas kernels, per_device(): pl.pallas_call(front_kernel, in_specs=[SMEM] * 3 + [HBM] * 10, out_specs=...  9.24 us
    pallas_call x1, Pallas kernels, per_device(): pl.pallas_call(arrival_kernel, in_specs=[SMEM] * 2 + [VMEM] * 4 + [HBM] *...  6.63 us
    ppermute x1, waiting for transfers between devices, per_device(): far_parcel = lax.ppermute(parcel, 'req', swap)  5.39 us
    ppermute x1, waiting for transfers between devices, per_device(): far_moved = lax.ppermute(moved_normed, 'req', swap)  4.69 us
  transfers between devices with their start and end apart: 11, of which 8 were waited for; matrix products, arithmetic and copies ran while one was open for 1% of the time, Pallas kernels for 18%

profile of v3, /device:TPU:0, one launch (start us, length us, event | category | flops | bytes accessed | tf_op | source)
XLA Modules:
  0.0 172.4 jit_solution(1354194339894189009)
XLA Ops:
  2.0 2.8 %leaving.1 = (bf16[528,512]{1,0:T(8,128)(2,1)}, bf16[512,512]{1,0:T(8,128)(2,1)}) custom-call(s32[1]{0:T(128)S(6)} %copy.20.slot, s32[1]{0:T(128)} %copy.21.dest, s32[2]{0:T(128)} %lengths.3, s32[2,8]{1,0:T(2,128)} %table.3, bf16[16,128,512]{2,1,0:T(8,128)(2,1)} %pool.3), custom_call_target="tpu_custom_call" | custom-call | bytes 2097152 | tf_op jit(solution)/shard_map/leaving/pallas_call | solution.py:481
  7.2 3.0 %collective-permute-start.3 = (bf16[528,512]{1,0:T(8,128)(2,1)S(1)}, bf16[528,512]{1,0:T(8,128)(2,1)}, u32[]{:S(2)}, u32[]{:S(2)}) collective-permute-start(bf16[528,512]{1,0:T(8,128)(2,1)S(1)} %broadcast_select_fusion), channel_id=1, source_target_pairs={{0,2},{1,3},{2,0},{3,1},{4,6},{5,7},{6,4},{7,5},{8,10},{9,11},{10,... | collective-permute-start | bytes 1622024 | tf_op jit(solution)/shard_map/ppermute | solution.py:512
  10.1 0.9 broadcast_select_fusion.1
  11.7 9.2 %front.1 = (f32[64,2048]{1,0:T(8,128)S(1)}, f32[64,64]{1,0:T(8,128)S(1)}, bf16[64,64]{1,0:T(8,128)(2,1)S(1)}, bf16[64,512]{1,0:T(8,128)(2,1)S(1)}, bf16[64,1536]...) custom-call(s32[1]{0:T(128)S(6)} %copy.20.slot, s32[2]{0:T(128)S(1)} %copy-done.11, s32[2,8]{1,0:T(2,128)S(1)} %copy-done.10, ...), custom_call_target="tpu_custom_call" | custom-call | flops 3000000000 | bytes 3000000 | tf_op jit(solution)/shard_map/front/pallas_call | solution.py:524
  21.0 0.7 copy-done.6
  21.6 3.6 %collective-permute-start.2 = (bf16[80,1536]{1,0:T(8,128)(2,1)S(1)}, bf16[80,1536]{1,0:T(8,128)(2,1)S(1)}, u32[]{:S(2)}, u32[]{:S(2)}) collective-permute-start(bf16[80,1536]{1,0:T(8,128)(2,1)S(1)} %get-tuple-element.37.staying.rest_0_), channel_id=1, source_target_pairs={{0,24},{4,28},{8,16},{12,20},{16,8},{20,12},{24,0},{28,4},{1,25},{... | collective-permute-start | bytes 737288 | tf_op jit(solution)/shard_map/ppermute | solution.py:559
  25.2 1.4 routes.1
  26.6 5.4 %collective-permute-done.2.parcel.staying.rest_2_ = bf16[80,1536]{1,0:T(8,128)(2,1)S(1)} collective-permute-done((bf16[80,1536]{1,0:T(8,128)(2,1)S(1)}, bf16[80,1536]{1,0:T(8,128)(2,1)S(1)}, u32[]{:S(2)}, u32[]{:S(2)}) %collective-permute-start.2) | collective-permute-done | bytes 245792 | tf_op jit(solution)/shard_map/ppermute | solution.py:559
  32.0 2.0 %collective-permute-done.4.rest_5_ = bf16[512,512]{1,0:T(8,128)(2,1)S(1)} collective-permute-done((bf16[512,512]{1,0:T(8,128)(2,1)}, bf16[512,512]{1,0:T(8,128)(2,1)S(1)}, u32[]{:S(2)}, u32[]{:S(2)}) %collective-permute-start.4) | collective-permute-done | bytes 524320 | tf_op jit(solution)/shard_map/ppermute | solution.py:512
  33.9 0.8 copy-done.17
  34.7 6.6 %arrival.1 = (bf16[64,1536]{1,0:T(8,128)(2,1)S(1)}, bf16[64,1536]{1,0:T(8,128)(2,1)S(1)}, bf16[128,512]{1,0:T(8,128)(2,1)}) custom-call(s32[1]{0:T(128)S(6)} %copy.20.slot, s32[1]{0:T(128)} %bitcast.3.me, f32[64,2048]{1,0:T(8,128)S(1)} %get-tuple-element.38.projected, f32[64,64]{1,0:T(8,128)S(1)} %get-tuple-element.42.reach, ...), custom_call_target="tpu_custom_call" | custom-call | flops 4000000000 | bytes 8000000 | tf_op jit(solution)/shard_map/arrival/pallas_call | solution.py:575
  41.4 4.5 %collective-permute-start.5 = (bf16[64,1536]{1,0:T(8,128)(2,1)S(1)}, bf16[64,1536]{1,0:T(8,128)(2,1)S(1)}, u32[]{:S(2)}, u32[]{:S(2)}) collective-permute-start(bf16[64,1536]{1,0:T(8,128)(2,1)S(1)} %get-tuple-element.51.moved.rest_1_), channel_id=1, source_target_pairs={{0,24},{4,28},{8,16},{12,20},{16,8},{20,12},{24,0},{28,4},{1,25},{... | collective-permute-start | bytes 589832 | tf_op jit(solution)/shard_map/ppermute | solution.py:601
  46.5 4.7 %collective-permute-done.5.moved.rest_3_ = bf16[64,1536]{1,0:T(8,128)(2,1)S(1)} collective-permute-done((bf16[64,1536]{1,0:T(8,128)(2,1)S(1)}, bf16[64,1536]{1,0:T(8,128)(2,1)S(1)}, u32[]{:S(2)}, u32[]{:S(2)}) %collective-permute-start.5) | collective-permute-done | bytes 196640 | tf_op jit(solution)/shard_map/ppermute | solution.py:601
  51.2 1.5 pack.3
  52.8 6.5 %all-to-all-start = ((bf16[16,32,1536]{2,1,0:T(8,128)(2,1)}), bf16[16,32,1536]{2,1,0:T(8,128)(2,1)S(1)}, u32[]{:S(2)}, u32[]{:S(2)}) async-start(bf16[16,32,1536]{2,1,0:T(8,128)(2,1)} %bitcast.20), calls=%async_computation | async-start | bytes 3145728 | tf_op jit(solution)/shard_map/all_to_all | solution.py:477
  59.3 1.6 pack.2
  60.9 21.5 %all-to-all-done = bf16[16,32,1536]{2,1,0:T(8,128)(2,1)S(1)} async-done(((bf16[16,32,1536]{2,1,0:T(8,128)(2,1)}), bf16[16,32,1536]{2,1,0:T(8,128)(2,1)S(1)}, u32[]{:S(2)}, u32[]{:S(2)}) %all-to-all-start) | async-done | bytes 1572896 | tf_op jit(solution)/shard_map/all_to_all | solution.py:477
  82.4 3.9 %all-to-all-start.1 = ((bf16[16,32,1536]{2,1,0:T(8,128)(2,1)}), bf16[16,32,1536]{2,1,0:T(8,128)(2,1)S(1)}, u32[]{:S(2)}, u32[]{:S(2)}) async-start(bf16[16,32,1536]{2,1,0:T(8,128)(2,1)} %bitcast.19), calls=%async_computation.1 | async-start | bytes 3145728 | tf_op jit(solution)/shard_map/all_to_all | solution.py:477
  86.3 0.9 copy-done.1
  87.2 0.9 copy-done.3
  88.1 0.9 copy-done.5
  89.1 3.1 %shares.1 = bf16[2,2,128,512]{3,2,1,0:T(8,128)(2,1)} custom-call(s32[1]{0:T(128)} %bitcast.2.base, bf16[32,1536]{1,0:T(8,128)(2,1)} %bitcast.23, bf16[80,1536]{1,0:T(8,128)(2,1)S(1)} %get-tuple-element.37.staying.rest_0_, bf16[64,1536]{1,0:T(8,128)(2,1)S(1)} %copy-done.3, bf16[80,1536]{1,0:T(8,128)(2,1)S(1)} %copy-done.1, bf16[64,1536]{1,0:T(8,128)(2,1)S(1)} %copy-done.5, ...), custom_call_target="tpu_custom_call" | custom-call | flops 300000000 | bytes 1000000 | tf_op jit(solution)/shard_map/shares/pallas_call | solution.py:632
  92.2 7.1 %experts.2 = bf16[512,1536]{1,0:T(8,128)(2,1)} custom-call(bf16[512,1536]{1,0:T(8,128)(2,1)S(1)} %bitcast.17, bf16[1,1536,768]{2,1,0:T(8,128)(2,1)} %w_gate.3, bf16[1,1536,768]{2,1,0:T(8,128)(2,1)} %w_up.3, bf16[1,768,1536]{2,1,0:T(8,128)(2,1)} %w_down.3), custom_call_target="tpu_custom_call" | custom-call | flops 3623878656 | bytes 7077888 | tf_op jit(solution)/shard_map/experts/pallas_call | solution.py:432
  99.3 9.8 %all-to-all-done.1 = bf16[16,32,1536]{2,1,0:T(8,128)(2,1)S(1)} async-done(((bf16[16,32,1536]{2,1,0:T(8,128)(2,1)}), bf16[16,32,1536]{2,1,0:T(8,128)(2,1)S(1)}, u32[]{:S(2)}, u32[]{:S(2)}) %all-to-all-start.1) | async-done | bytes 1572896 | tf_op jit(solution)/shard_map/all_to_all | solution.py:477
  109.1 3.7 %all-to-all-start.2 = ((bf16[16,32,1536]{2,1,0:T(8,128)(2,1)}), bf16[16,32,1536]{2,1,0:T(8,128)(2,1)S(1)}, u32[]{:S(2)}, u32[]{:S(2)}) async-start(bf16[16,32,1536]{2,1,0:T(8,128)(2,1)} %bitcast.22), calls=%async_computation.2 | async-start | bytes 3145728 | tf_op jit(solution)/shard_map/all_to_all | solution.py:477
  112.8 7.0 %experts.3 = bf16[512,1536]{1,0:T(8,128)(2,1)} custom-call(bf16[512,1536]{1,0:T(8,128)(2,1)S(1)} %bitcast.18, bf16[1,1536,768]{2,1,0:T(8,128)(2,1)} %w_gate.3, bf16[1,1536,768]{2,1,0:T(8,128)(2,1)} %w_up.3, bf16[1,768,1536]{2,1,0:T(8,128)(2,1)} %w_down.3), custom_call_target="tpu_custom_call" | custom-call | flops 3623878656 | bytes 7077888 | tf_op jit(solution)/shard_map/experts/pallas_call | solution.py:432
  119.8 16.0 %all-to-all-done.2 = bf16[16,32,1536]{2,1,0:T(8,128)(2,1)S(1)} async-done(((bf16[16,32,1536]{2,1,0:T(8,128)(2,1)}), bf16[16,32,1536]{2,1,0:T(8,128)(2,1)S(1)}, u32[]{:S(2)}, u32[]{:S(2)}) %all-to-all-start.2) | async-done | bytes 1572896 | tf_op jit(solution)/shard_map/all_to_all | solution.py:477
  135.8 3.7 %all-to-all-start.3 = ((bf16[16,32,1536]{2,1,0:T(8,128)(2,1)}), bf16[16,32,1536]{2,1,0:T(8,128)(2,1)S(1)}, u32[]{:S(2)}, u32[]{:S(2)}) async-start(bf16[16,32,1536]{2,1,0:T(8,128)(2,1)} %bitcast.21), calls=%async_computation.3 | async-start | bytes 3145728 | tf_op jit(solution)/shard_map/all_to_all | solution.py:477
  139.6 1.6 partial.1
  141.2 3.7 %collective-permute-start.6 = (bf16[128,1536]{1,0:T(8,128)(2,1)S(1)}, bf16[128,1536]{1,0:T(8,128)(2,1)S(1)}, u32[]{:S(2)}, u32[]{:S(2)}) collective-permute-start(bf16[128,1536]{1,0:T(8,128)(2,1)S(1)} %partial.1), channel_id=1, source_target_pairs={{0,24},{4,28},{8,16},{12,20},{16,8},{20,12},{24,0},{28,4},{1,25},{... | collective-permute-start | bytes 1179656 | tf_op jit(solution)/shard_map/ppermute | solution.py:669
  144.9 25.0 %collective-permute-done.6.far = bf16[128,1536]{1,0:T(8,128)(2,1)S(1)} collective-permute-done((bf16[128,1536]{1,0:T(8,128)(2,1)S(1)}, bf16[128,1536]{1,0:T(8,128)(2,1)S(1)}, u32[]{:S(2)}, u32[]{:S(2)}) %collective-permute-start.6) | collective-permute-done | bytes 393248 | tf_op jit(solution)/shard_map/ppermute | solution.py:669
  169.9 2.3 %final.1 = bf16[128,1536]{1,0:T(8,128)(2,1)} custom-call(s32[1]{0:T(128)S(6)} %copy.20.slot, bf16[2,2,128,512]{3,2,1,0:T(8,128)(2,1)} %shares.1, bf16[64,1536]{1,0:T(8,128)(2,1)S(1)} %copy-done.7, bf16[64,1536]{1,0:T(8,128)(2,1)S(1)} %copy-done.9, bf16[128,1536]{1,0:T(8,128)(2,1)S(1)} %collective-permute-done.6.far, bf16[512,1536]{1,0:T(8,128)(2,1)S(1)} %bitcast.16), custom_call_target="tpu_custom_call" | custom-call | flops 400000000 | bytes 2000000 | tf_op jit(solution)/shard_map/final/pallas_call | solution.py:671
  (42 shorter events, 3.6 us)
Async XLA Ops:
  0.6 4.8 %copy-start.15 = (bf16[1536]{0:T(1024)(128)(2,1)S(1)}, bf16[1536]{0:T(1024)(128)(2,1)}, u32[]{:S(2)}) copy-start(bf16[1536]{0:T(1024)(128)(2,1)} %param.29) | copy-start | bytes 9220
  0.6 5.4 %copy-start.16 = (bf16[1536]{0:T(1024)(128)(2,1)S(1)}, bf16[1536]{0:T(1024)(128)(2,1)}, u32[]{:S(2)}) copy-start(bf16[1536]{0:T(1024)(128)(2,1)} %param.26) | copy-start | bytes 9220
  4.8 5.3 %copy-start.13 = (bf16[512,512]{1,0:T(8,128)(2,1)S(1)}, bf16[512,512]{1,0:T(8,128)(2,1)}, u32[]{:S(2)}) copy-start(bf16[512,512]{1,0:T(8,128)(2,1)} %get-tuple-element.46.rest_1_) | copy-start | bytes 1572868
  4.8 2.3 %collective-permute-start = (bf16[528,512]{1,0:T(8,128)(2,1)}, bf16[528,512]{1,0:T(8,128)(2,1)S(1)}, u32[]{:S(2)}, u32[]{:S(2)}) collective-permute-start(bf16[528,512]{1,0:T(8,128)(2,1)} %get-tuple-element.45.rest_0_), channel_id=1, source_target_pairs={{0,1},{1,0},{2,3},{3,2},{4,5},{5,4},{6,7},{7,6},{8,9},{9,8},{10,11... | collective-permute-start | bytes 1622024 | tf_op jit(solution)/shard_map/ppermute | solution.py:503
  5.3 4.8 %collective-permute-start.1 = (bf16[512,512]{1,0:T(8,128)(2,1)}, bf16[512,512]{1,0:T(8,128)(2,1)S(1)}, u32[]{:S(2)}, u32[]{:S(2)}) collective-permute-start(bf16[512,512]{1,0:T(8,128)(2,1)} %get-tuple-element.46.rest_1_), channel_id=1, source_target_pairs={{0,1},{1,0},{2,3},{3,2},{4,5},{5,4},{6,7},{7,6},{8,9},{9,8},{10,11... | collective-permute-start | bytes 1572872 | tf_op jit(solution)/shard_map/ppermute | solution.py:503
  6.6 5.1 %copy-start.10 = (s32[2,8]{1,0:T(2,128)S(1)}, s32[2,8]{1,0:T(2,128)}, u32[]{:S(2)}) copy-start(s32[2,8]{1,0:T(2,128)} %table.3) | copy-start | bytes 196
  6.6 5.1 %copy-start.11 = (s32[2]{0:T(128)S(1)}, s32[2]{0:T(128)}, u32[]{:S(2)}) copy-start(s32[2]{0:T(128)} %lengths.3) | copy-start | bytes 28
  7.1 4.0 %copy-start.12 = (bf16[528,512]{1,0:T(8,128)(2,1)}, bf16[528,512]{1,0:T(8,128)(2,1)S(1)}, u32[]{:S(2)}) copy-start(bf16[528,512]{1,0:T(8,128)(2,1)S(1)} %collective-permute-done.rest_2_) | copy-start | bytes 1622020
  7.2 26.8 %collective-permute-start.3 = (bf16[528,512]{1,0:T(8,128)(2,1)S(1)}, bf16[528,512]{1,0:T(8,128)(2,1)}, u32[]{:S(2)}, u32[]{:S(2)}) collective-permute-start(bf16[528,512]{1,0:T(8,128)(2,1)S(1)} %broadcast_select_fusion), channel_id=1, source_target_pairs={{0,2},{1,3},{2,0},{3,1},{4,6},{5,7},{6,4},{7,5},{8,10},{9,11},{10,... | collective-permute-start | bytes 1622024 | tf_op jit(solution)/shard_map/ppermute | solution.py:512
  10.1 1.6 copy-start.14
  11.1 22.9 %collective-permute-start.4 = (bf16[512,512]{1,0:T(8,128)(2,1)}, bf16[512,512]{1,0:T(8,128)(2,1)S(1)}, u32[]{:S(2)}, u32[]{:S(2)}) collective-permute-start(bf16[512,512]{1,0:T(8,128)(2,1)} %broadcast_select_fusion.1), channel_id=1, source_target_pairs={{0,2},{1,3},{2,0},{3,1},{4,6},{5,7},{6,4},{7,5},{8,10},{9,11},{10,... | collective-permute-start | bytes 1572872 | tf_op jit(solution)/shard_map/ppermute | solution.py:512
  20.9 0.7 copy-start.6
  21.6 10.4 %collective-permute-start.2 = (bf16[80,1536]{1,0:T(8,128)(2,1)S(1)}, bf16[80,1536]{1,0:T(8,128)(2,1)S(1)}, u32[]{:S(2)}, u32[]{:S(2)}) collective-permute-start(bf16[80,1536]{1,0:T(8,128)(2,1)S(1)} %get-tuple-element.37.staying.rest_0_), channel_id=1, source_target_pairs={{0,24},{4,28},{8,16},{12,20},{16,8},{20,12},{24,0},{28,4},{1,25},{... | collective-permute-start | bytes 737288 | tf_op jit(solution)/shard_map/ppermute | solution.py:559
  32.0 19.2 %copy-start = (bf16[80,1536]{1,0:T(8,128)(2,1)}, bf16[80,1536]{1,0:T(8,128)(2,1)S(1)}, u32[]{:S(2)}) copy-start(bf16[80,1536]{1,0:T(8,128)(2,1)S(1)} %collective-permute-done.2.parcel.staying.rest_2_) | copy-start | bytes 737284
  33.9 0.8 copy-start.17
  41.4 11.4 %copy-start.8 = (bf16[64,1536]{1,0:T(8,128)(2,1)}, bf16[64,1536]{1,0:T(8,128)(2,1)S(1)}, u32[]{:S(2)}) copy-start(bf16[64,1536]{1,0:T(8,128)(2,1)S(1)} %get-tuple-element.60.moved) | copy-start | bytes 589828
  41.4 17.9 %copy-start.2 = (bf16[64,1536]{1,0:T(8,128)(2,1)}, bf16[64,1536]{1,0:T(8,128)(2,1)S(1)}, u32[]{:S(2)}) copy-start(bf16[64,1536]{1,0:T(8,128)(2,1)S(1)} %get-tuple-element.51.moved.rest_1_) | copy-start | bytes 589828
  41.4 9.8 %collective-permute-start.5 = (bf16[64,1536]{1,0:T(8,128)(2,1)S(1)}, bf16[64,1536]{1,0:T(8,128)(2,1)S(1)}, u32[]{:S(2)}, u32[]{:S(2)}) collective-permute-start(bf16[64,1536]{1,0:T(8,128)(2,1)S(1)} %get-tuple-element.51.moved.rest_1_), channel_id=1, source_target_pairs={{0,24},{4,28},{8,16},{12,20},{16,8},{20,12},{24,0},{28,4},{1,25},{... | collective-permute-start | bytes 589832 | tf_op jit(solution)/shard_map/ppermute | solution.py:601
  51.2 1.5 copy-start.4
  52.8 29.6 %all-to-all-start = ((bf16[16,32,1536]{2,1,0:T(8,128)(2,1)}), bf16[16,32,1536]{2,1,0:T(8,128)(2,1)S(1)}, u32[]{:S(2)}, u32[]{:S(2)}) async-start(bf16[16,32,1536]{2,1,0:T(8,128)(2,1)} %bitcast.20), calls=%async_computation | async-start | bytes 3145728 | tf_op jit(solution)/shard_map/all_to_all | solution.py:477
  82.4 26.7 %all-to-all-start.1 = ((bf16[16,32,1536]{2,1,0:T(8,128)(2,1)}), bf16[16,32,1536]{2,1,0:T(8,128)(2,1)S(1)}, u32[]{:S(2)}, u32[]{:S(2)}) async-start(bf16[16,32,1536]{2,1,0:T(8,128)(2,1)} %bitcast.19), calls=%async_computation.1 | async-start | bytes 3145728 | tf_op jit(solution)/shard_map/all_to_all | solution.py:477
  86.3 0.9 copy-start.1
  87.2 0.9 copy-start.3
  88.1 0.9 copy-start.5
  109.1 26.7 %all-to-all-start.2 = ((bf16[16,32,1536]{2,1,0:T(8,128)(2,1)}), bf16[16,32,1536]{2,1,0:T(8,128)(2,1)S(1)}, u32[]{:S(2)}, u32[]{:S(2)}) async-start(bf16[16,32,1536]{2,1,0:T(8,128)(2,1)} %bitcast.22), calls=%async_computation.2 | async-start | bytes 3145728 | tf_op jit(solution)/shard_map/all_to_all | solution.py:477
  135.8 34.1 %all-to-all-start.3 = ((bf16[16,32,1536]{2,1,0:T(8,128)(2,1)}), bf16[16,32,1536]{2,1,0:T(8,128)(2,1)S(1)}, u32[]{:S(2)}, u32[]{:S(2)}) async-start(bf16[16,32,1536]{2,1,0:T(8,128)(2,1)} %bitcast.21), calls=%async_computation.3 | async-start | bytes 3145728 | tf_op jit(solution)/shard_map/all_to_all | solution.py:477
  139.5 30.4 %copy-start.7 = (bf16[64,1536]{1,0:T(8,128)(2,1)S(1)}, bf16[64,1536]{1,0:T(8,128)(2,1)}, u32[]{:S(2)}) copy-start(bf16[64,1536]{1,0:T(8,128)(2,1)} %copy-done.6) | copy-start | bytes 589828
  139.5 30.4 %copy-start.9 = (bf16[64,1536]{1,0:T(8,128)(2,1)S(1)}, bf16[64,1536]{1,0:T(8,128)(2,1)}, u32[]{:S(2)}) copy-start(bf16[64,1536]{1,0:T(8,128)(2,1)} %copy-done.8) | copy-start | bytes 589828
  141.2 28.7 %collective-permute-start.6 = (bf16[128,1536]{1,0:T(8,128)(2,1)S(1)}, bf16[128,1536]{1,0:T(8,128)(2,1)S(1)}, u32[]{:S(2)}, u32[]{:S(2)}) collective-permute-start(bf16[128,1536]{1,0:T(8,128)(2,1)S(1)} %partial.1), channel_id=1, source_target_pairs={{0,24},{4,28},{8,16},{12,20},{16,8},{20,12},{24,0},{28,4},{1,25},{... | collective-permute-start | bytes 1179656 | tf_op jit(solution)/shard_map/ppermute | solution.py:669

commit v4 on v3

--- a/solution.py
+++ b/solution.py
@@ -108,30 +108,25 @@
     return copies
 
 
-def leaving_kernel(slot, dest, lengths, table, pool, first, second, pages, note, sems, out_sems):
-    loads = load_pages(table, slot[0], pool, pages, sems)
+def leaving_kernel(slot, dest, lengths, table, pool, first, second, sems):
+    half, page = second.shape[0], pool.shape[1]
+    loads = []
+    for i in range(table.shape[1]):
+        target = first if i * page < half else second
+        span = pl.ds(i * page % half, page)
+        loads.append(
+            pltpu.make_async_copy(pool.at[table[slot[0], i]], target.at[span], sems.at[i])
+        )
+        loads[-1].start()
     length = lengths[slot[0]]
-    half = second.shape[0]
-    page = 2 * half // len(loads)
-    blank = jnp.zeros((NOTE, 128), jnp.float32)
-    for at, value in enumerate((dest[0], length // NOTE_BASE, length % NOTE_BASE)):
-        filled = blank + value.astype(jnp.float32)
-        note[:, at * 128 : (at + 1) * 128] = filled.astype(jnp.bfloat16)
-    note[:, 3 * 128 :] = jnp.zeros((NOTE, note.shape[1] - 3 * 128), jnp.bfloat16)
-    stores = [pltpu.make_async_copy(note, first.at[pl.ds(half, NOTE)], out_sems.at[len(loads)])]
-    stores[0].start()
-    for i, load in enumerate(loads):
-        load.wait()
-        target = first if i * page < half else second
-        stores.append(
-            pltpu.make_async_copy(
-                pages.at[pl.ds(i * page, page)],
-                target.at[pl.ds(i * page % half, page)],
-                out_sems.at[i],
-            )
-        )
-        stores[-1].start()
-    finish(stores)
+    row = lax.broadcasted_iota(jnp.int32, (NOTE, first.shape[1]), 0)
+    lane = lax.broadcasted_iota(jnp.int32, (NOTE, first.shape[1]), 1)
+    note = jnp.zeros((NOTE, first.shape[1]), jnp.int32)
+    parts = (dest[0] * 4 * half, length // NOTE_BASE * NOTE_BASE, length % NOTE_BASE)
+    for at, value in enumerate(parts):
+        note = jnp.where((row == 0) & (lane == at), value, note)
+    first[half:, :] = note.astype(jnp.float32).astype(jnp.bfloat16)
+    finish(loads)
 
 
 def slots_of(ids_t, first, shown):
@@ -241,7 +236,8 @@
 def front_kernel(
     slot, lengths, table, hidden, parents, path, spectrum, gain, moe_gain, ids_t, w_qkv, w_out,
     pool, moved_projected, moved_reach, moved_picked, compact, staying, parcel,
-    weights, tokens, lines, trees, table_row, gains, names_t, w_in, cache, sems, page_sems,
+    weights, tokens, lines, trees, table_row, gains, names_t, w_in, cache, kept_lines, sems,
+    page_sems, out_sem,
 ):
     stay = 1 - slot[0]
     loads = load_all(
@@ -276,7 +272,8 @@
         one_hot(flipped(trees[pl.ds(r, 1), :].astype(jnp.float32)).astype(jnp.int32) == names)
         for r in (stay, slot[0])
     ]
-    moved_projected[...] = projected[draft:]
+    kept_lines[...] = projected[draft:]
+    store = load_all(((kept_lines, moved_projected),), out_sem)
     moved_reach[...] = reaches[1]
     moved_picked[...] = picks[1]
     depth = jnp.sum(reaches[0], axis=-1, keepdims=True) - 1.0
@@ -291,69 +288,126 @@
     kept = (rows[0].astype(jnp.float32) + dot(attended, weights[...])).astype(jnp.bfloat16)
     staying[...] = kept
     parcel[:draft, :] = rms_scale(kept, gains[1])
+    finish(store)
     ids = travel_order(slot[0], names_t[...]).astype(jnp.float32)
     blank = jnp.zeros((NOTE - ids.shape[0], ids.shape[1]), jnp.float32)
     parcel[draft:, :] = jnp.zeros((NOTE, parcel.shape[1]), jnp.bfloat16)
     parcel[draft:, : ids.shape[1]] = jnp.concatenate([ids, blank], axis=0).astype(jnp.bfloat16)
 
 
-def arrival_kernel(
-    slot, me, projected, reach, picked, staying_compact, hidden, spectrum, gain, w_out, *rest,
+def early_kernel(
+    slot, me, reach, picked, staying_compact, projected, spectrum, *rest,
 ):
-    sources = rest[:-11]
-    sources = list(zip(sources[0::2], sources[1::2]))
-    moved, moved_normed, compact, cache, notes, weights, rows, table_row, gains, sems, note_sems = (
-        rest[-11:]
-    )
-    half = cache.shape[0] // 2
+    sources = rest[:-14]
+    (
+        pick, stacked, mixed, tops, totals, compact,
+        cache, notes, lines, table_row, fresh, note_sems, sems, cache_sem,
+    ) = rest[-14:]
+    half = cache.shape[0]
     draft = projected.shape[0]
-    query_width = weights.shape[0]
     note_loads = load_all(
-        [(first.at[pl.ds(half, NOTE)], notes.at[i]) for i, (first, _) in enumerate(sources)],
+        [
+            (first.at[pl.ds(half, NOTE), pl.ds(0, 128)], notes.at[i])
+            for i, first in enumerate(sources)
+        ],
         note_sems,
     )
+    loads = load_all(((projected, lines), (spectrum, table_row)), sems)
+    depth = jnp.sum(reach[...], axis=-1, keepdims=True) - 1.0
+    finish(note_loads)
+    chosen = jnp.int32(0)
+    length = jnp.int32(0)
+    for i, source in enumerate(sources):
+        code = jnp.sum(notes[i].astype(jnp.float32)).astype(jnp.int32)
+        mine = code // (4 * half) == me[0]
+        chosen = jnp.where(mine, i, chosen)
+        length = jnp.where(mine, code % (4 * half), length)
+
+        @pl.when(mine)
+        def _(source=source):
+            pltpu.make_async_copy(source.at[pl.ds(0, half)], cache, cache_sem).start()
+
+    pick[0] = chosen
+    pick[1] = length
+    finish(loads)
+    query_width = QUERY_HEADS * HEAD_SIZE
+    queries, rows = rotate(
+        lines[...], depth, length.astype(jnp.float32), table_row[...], query_width
+    )
+    fresh[...] = rows
     own = pl.ds(pl.multiple_of(slot[0] * draft, draft), draft)
     other = pl.ds(pl.multiple_of((1 - slot[0]) * draft, draft), draft)
-    loads = load_all(
-        ((hidden.at[own], rows), (spectrum, table_row), (gain, gains), (w_out, weights)),
-        sems.at[pl.ds(2, 4)],
-    )
-    depth = jnp.sum(reach[...], axis=-1, keepdims=True) - 1.0
-    finish(note_loads)
-
-    def noted(i, at):
-        values = notes[i, :, at * 128 : (at + 1) * 128]
-        return jnp.max(values.astype(jnp.float32)).astype(jnp.int32)
-
-    def cache_loads(pair):
-        return [
-            pltpu.make_async_copy(pair[0].at[pl.ds(0, half)], cache.at[pl.ds(0, half)], sems.at[0]),
-            pltpu.make_async_copy(pair[1], cache.at[pl.ds(half, half)], sems.at[1]),
+    compact[own, :] = dot(picked[...], rows).astype(jnp.bfloat16)
+    compact[other, :] = staying_compact[...]
+    pltpu.make_async_copy(sources[0].at[pl.ds(0, half)], cache, cache_sem).wait()
+    scale = HEAD_SIZE ** (-0.5) * LOG2E
+    key_width = KEY_VALUE_HEADS * HEAD_SIZE
+    in_cache = lax.broadcasted_iota(jnp.int32, (1, half), 1) < length
+    cache_bias = jnp.where(in_cache, 0.0, MASKED)
+    tree_bias = jnp.concatenate([jnp.where(reach[...] > 0.5, 0.0, MASKED)] * GROUP, axis=0)
+    for kv in range(KEY_VALUE_HEADS):
+        cols = slice(kv * HEAD_SIZE, (kv + 1) * HEAD_SIZE)
+        vcols = slice(key_width + kv * HEAD_SIZE, key_width + (kv + 1) * HEAD_SIZE)
+        heads = [
+            queries[:, (kv * GROUP + g) * HEAD_SIZE : (kv * GROUP + g + 1) * HEAD_SIZE]
+            for g in range(GROUP)
         ]
-
-    length = jnp.int32(0)
-    for i, pair in enumerate(sources):
-        mine = noted(i, 0) == me[0]
-        length = jnp.where(mine, noted(i, 1) * NOTE_BASE + noted(i, 2), length)
-
-        @pl.when(mine)
-        def _(pair=pair):
-            for copy in cache_loads(pair):
-                copy.start()
-
-    finish(loads[:3])
-    queries, fresh = rotate(
-        projected[...], depth, length.astype(jnp.float32), table_row[...], query_width
-    )
-    finish(cache_loads(sources[0]))
-    attended = attend(queries, cache, fresh, reach[...], length)
-    finish(loads[3:])
+        asked = jnp.concatenate(heads, axis=0)
+        stacked[kv] = asked
+        first = dot(asked, cache[:, cols], ((1,), (1,))) * scale + cache_bias
+        second = dot(asked, fresh[:, cols], ((1,), (1,))) * scale + tree_bias
+        top = jnp.maximum(
+            jnp.max(first, axis=-1, keepdims=True), jnp.max(second, axis=-1, keepdims=True)
+        )
+        first = jnp.exp2(first - top)
+        second = jnp.exp2(second - top)
+        tops[kv] = top
+        totals[kv] = jnp.sum(first, axis=-1, keepdims=True) + jnp.sum(
+            second, axis=-1, keepdims=True
+        )
+        mixed[kv] = dot(first.astype(jnp.bfloat16), cache[:, vcols]) + dot(
+            second.astype(jnp.bfloat16), fresh[:, vcols]
+        )
+
+
+def arrival_kernel(
+    slot, pick, stacked, mixed, tops, totals, hidden, gain, w_out, *rest,
+):
+    sources = rest[:-8]
+    moved, moved_normed, cache, weights, rows, gains, sems, cache_sem = rest[-8:]
+    half = cache.shape[0]
+    draft = rows.shape[0]
+    for i, source in enumerate(sources):
+
+        @pl.when(pick[0] == i)
+        def _(source=source):
+            pltpu.make_async_copy(source, cache, cache_sem).start()
+
+    own = pl.ds(pl.multiple_of(slot[0] * draft, draft), draft)
+    loads = load_all(((hidden.at[own], rows), (gain, gains), (w_out, weights)), sems)
+    scale = HEAD_SIZE ** (-0.5) * LOG2E
+    key_width = KEY_VALUE_HEADS * HEAD_SIZE
+    in_cache = lax.broadcasted_iota(jnp.int32, (1, half), 1) + half < pick[1]
+    bias = jnp.where(in_cache, 0.0, MASKED)
+    pltpu.make_async_copy(sources[0], cache, cache_sem).wait()
+    outs = []
+    for kv in range(KEY_VALUE_HEADS):
+        cols = slice(kv * HEAD_SIZE, (kv + 1) * HEAD_SIZE)
+        vcols = slice(key_width + kv * HEAD_SIZE, key_width + (kv + 1) * HEAD_SIZE)
+        scores = dot(stacked[kv], cache[:, cols], ((1,), (1,))) * scale + bias
+        top = jnp.maximum(jnp.max(scores, axis=-1, keepdims=True), tops[kv])
+        weight = jnp.exp2(scores - top)
+        factor = jnp.exp2(tops[kv] - top)
+        total = totals[kv] * factor + jnp.sum(weight, axis=-1, keepdims=True)
+        blend = mixed[kv] * factor + dot(weight.astype(jnp.bfloat16), cache[:, vcols])
+        blend = (blend / total).astype(jnp.bfloat16)
+        outs += [blend[g * draft : (g + 1) * draft] for g in range(GROUP)]
+    attended = jnp.concatenate(outs, axis=1)
+    finish(loads)
     kept = rows[...].astype(jnp.float32) + dot(attended, weights[...])
     kept = kept.astype(jnp.bfloat16)
     moved[...] = kept
     moved_normed[...] = rms_scale(kept, gains[...])
-    compact[own, :] = dot(picked[...], fresh).astype(jnp.bfloat16)
-    compact[other, :] = staying_compact[...]
 
 
 def pack_kernel(routes, staying, moved, out, rows, sems):
@@ -481,18 +535,13 @@
     leaving = pl.pallas_call(
         leaving_kernel,
         in_specs=[SMEM] * 4 + [HBM],
-        out_specs=[HBM] * 2,
+        out_specs=[VMEM] * 2,
         out_shape=[
-            pltpu.HBM((half_cache + NOTE, kv_width), bf16),
-            pltpu.HBM((half_cache, kv_width), bf16),
-        ],
-        scratch_shapes=[
-            pltpu.VMEM((context, kv_width), bf16),
-            pltpu.VMEM((NOTE, kv_width), bf16),
-            pltpu.SemaphoreType.DMA((pages,)),
-            pltpu.SemaphoreType.DMA((pages + 1,)),
-        ],
-        compiler_params=params(60),
+            pltpu.VMEM((half_cache + NOTE, kv_width), bf16),
+            pltpu.VMEM((half_cache, kv_width), bf16),
+        ],
+        scratch_shapes=[pltpu.SemaphoreType.DMA((pages,))],
+        compiler_params=params(58),
         cost_estimate=cost(0, 4 * context * kv_width),
         name="leaving",
     )(mig_slot, mig_dest, cache_len, page_table, *in_hbm(kv_pool))
@@ -524,9 +573,9 @@
     projected, reach, picked, staying_compact, staying, parcel = pl.pallas_call(
         front_kernel,
         in_specs=[SMEM] * 3 + [HBM] * 10,
-        out_specs=[VMEM] * 6,
+        out_specs=[HBM] + [VMEM] * 5,
         out_shape=[
-            pltpu.VMEM((draft, w_qkv.shape[1]), f32),
+            pltpu.HBM((draft, w_qkv.shape[1]), f32),
             pltpu.VMEM((draft, draft), f32),
             pltpu.VMEM((draft, draft), bf16),
             pltpu.VMEM((draft, kv_width), bf16),
@@ -543,8 +592,10 @@
             pltpu.VMEM((expert_ids.shape[1], tokens), jnp.int32),
             pltpu.VMEM(w_qkv.shape, bf16),
             pltpu.VMEM((context, kv_width), bf16),
+            pltpu.VMEM((draft, w_qkv.shape[1]), f32),
             pltpu.SemaphoreType.DMA((9,)),
             pltpu.SemaphoreType.DMA((pages,)),
+            pltpu.SemaphoreType.DMA((1,)),
         ],
         compiler_params=params(36),
         cost_estimate=cost(3e9, 3e6),
@@ -571,32 +622,57 @@
         cost_estimate=cost(1e8, 1e6),
         name="routes",
     )(base, mig_slot, *in_hbm(names_t))
-    far_parcel, routes, *sources = lax.optimization_barrier((far_parcel, routes, *sources))
-    moved, moved_normed, compact = pl.pallas_call(
+    early, late = sources[0::2], sources[1::2]
+    rows = GROUP * draft
+    pick, stacked, mixed, tops, totals, compact = pl.pallas_call(
+        early_kernel,
+        in_specs=[SMEM] * 2 + [VMEM] * 3 + [HBM] * 2 + [ANY] * len(early),
+        out_specs=[SMEM] + [VMEM] * 5,
+        out_shape=[
+            jax.ShapeDtypeStruct((2,), jnp.int32),
+            pltpu.VMEM((KEY_VALUE_HEADS, rows, HEAD_SIZE), bf16),
+            pltpu.VMEM((KEY_VALUE_HEADS, rows, HEAD_SIZE), f32),
+            pltpu.VMEM((KEY_VALUE_HEADS, rows, 1), f32),
+            pltpu.VMEM((KEY_VALUE_HEADS, rows, 1), f32),
+            jax.ShapeDtypeStruct((tokens, kv_width), bf16),
+        ],
+        scratch_shapes=[
+            pltpu.VMEM((half_cache, kv_width), bf16),
+            pltpu.VMEM((len(early), NOTE, 128), bf16),
+            pltpu.VMEM(projected.shape, f32),
+            pltpu.VMEM(spectrum.shape, f32),
+            pltpu.VMEM((draft, kv_width), bf16),
+            pltpu.SemaphoreType.DMA((len(early),)),
+            pltpu.SemaphoreType.DMA((2,)),
+            pltpu.SemaphoreType.DMA,
+        ],
+        compiler_params=params(16),
+        cost_estimate=cost(1e9, 2e6),
+        name="early",
+    )(
+        mig_slot, me, *in_vmem(reach, picked, staying_compact), *in_hbm(projected, spectrum),
+        *early,
+    )
+    far_parcel, routes, pick, *late = lax.optimization_barrier((far_parcel, routes, pick, *late))
+    moved, moved_normed = pl.pallas_call(
         arrival_kernel,
-        in_specs=[SMEM] * 2 + [VMEM] * 4 + [HBM] * (4 + len(sources)),
-        out_specs=[VMEM] * 3,
-        out_shape=[
-            pltpu.VMEM((draft, model), bf16),
-            pltpu.VMEM((draft, model), bf16),
-            jax.ShapeDtypeStruct((tokens, kv_width), bf16),
-        ],
+        in_specs=[SMEM] * 2 + [VMEM] * 4 + [HBM] * 3 + [ANY] * len(late),
+        out_specs=[VMEM] * 2,
+        out_shape=[pltpu.VMEM((draft, model), bf16)] * 2,
         scratch_shapes=[
-            pltpu.VMEM((context, kv_width), bf16),
-            pltpu.VMEM((len(sources) // 2, NOTE, kv_width), bf16),
+            pltpu.VMEM((half_cache, kv_width), bf16),
             pltpu.VMEM(w_out.shape, bf16),
             pltpu.VMEM((draft, model), bf16),
-            pltpu.VMEM(spectrum.shape, f32),
             pltpu.VMEM((1, model), bf16),
-            pltpu.SemaphoreType.DMA((6,)),
-            pltpu.SemaphoreType.DMA((len(sources) // 2,)),
-        ],
-        compiler_params=params(24),
-        cost_estimate=cost(4e9, 8e6),
+            pltpu.SemaphoreType.DMA((3,)),
+            pltpu.SemaphoreType.DMA,
+        ],
+        compiler_params=params(16),
+        cost_estimate=cost(2e9, 8e6),
         name="arrival",
     )(
-        mig_slot, me, *in_vmem(projected, reach, picked, staying_compact),
-        *in_hbm(hidden, spectrum, row_moe_gain, w_out, *sources),
+        mig_slot, pick, *in_vmem(stacked, mixed, tops, totals),
+        *in_hbm(hidden, row_moe_gain, w_out), *late,
     )
     far_moved = lax.ppermute(moved_normed, "req", swap)
     far_routes, far_ids = pl.pallas_call(

time: 173 us -> 168 us (0.971)
  waiting for transfers between devices: 84.8 us -> 80.6 us
    ppermute x1, waiting for transfers between devices: 5.39 us -> 0.83 us  [per_device(): far_parcel = lax.ppermute(parcel, 'req', swap)]
    pallas_call x1 -> x2, Pallas kernels: 2.83 us -> 5.68 us  [the longest x1 3.62 us: per_device(): pl.pallas_call(early_kernel, in_specs=[SMEM] * 2 + [VMEM] * 3 + [HBM] * 2...]
    pallas_call x1, Pallas kernels: 6.63 us -> 4.16 us  [per_device(): pl.pallas_call(arrival_kernel, in_specs=[SMEM] * 2 + [VMEM] * 4 + [HBM] *...]
    unnamed x36 -> x28, local copies, waits for them, and re-layouts: 4.3 us -> 3.49 us
  transfers between devices with their start and end apart: 11 -> 11, of which waited for: 8 -> 8; matrix products, arithmetic and copies ran while one was open for 1% -> 2% of each run, Pallas kernels for 18% -> 21%
where the time goes in v4:
time: 168 us; the launch traced here: 167 us
  waiting for transfers between devices  80.6 us (48%)
  Pallas kernels  45.2 us (27%)
  starting transfers between devices  32.8 us (20%)
  local copies, waits for them, and re-layouts  4.68 us (3%)
  between operations  2.34 us (1%)
  other arithmetic  1.69 us (1%)
    all_to_all x4, waiting for transfers between devices, within_half(): lax.all_to_all(rows, AXES, 0, 0, tiled=True, axis_index_groups=groups)  47.3 us
    ppermute x1, waiting for transfers between devices, per_device(): own_far = lax.ppermute(far_sum, 'req', swap)  25 us
    all_to_all x4, starting transfers between devices, within_half(): lax.all_to_all(rows, AXES, 0, 0, tiled=True, axis_index_groups=groups)  18.4 us
    pallas_call x2, Pallas kernels, run_experts(): pl.pallas_call(expert_kernel, in_specs=[VMEM] + [HBM] * 3, out_specs=HBM,...  14.1 us
    pallas_call x1, Pallas kernels, per_device(): pl.pallas_call(front_kernel, in_specs=[SMEM] * 3 + [HBM] * 10, out_specs=...  9.33 us
    pallas_call x1, Pallas kernels, per_device(): pl.pallas_call(arrival_kernel, in_specs=[SMEM] * 2 + [VMEM] * 4 + [HBM] *...  4.16 us
    ppermute x1, starting transfers between devices, per_device(): far_parcel = lax.ppermute(parcel, 'req', swap)  4.08 us
    ppermute x1, waiting for transfers between devices, per_device(): far_moved = lax.ppermute(moved_normed, 'req', swap)  3.93 us
  transfers between devices with their start and end apart: 11, of which 8 were waited for; matrix products, arithmetic and copies ran while one was open for 2% of the time, Pallas kernels for 21%

profile of v4, /device:TPU:0, one launch (start us, length us, event | category | flops | bytes accessed | tf_op | source)
XLA Modules:
  0.0 167.3 jit_solution(1435553070435821456)
XLA Ops:
  2.0 2.1 %leaving.1 = (bf16[528,512]{1,0:T(8,128)(2,1)S(1)}, bf16[512,512]{1,0:T(8,128)(2,1)S(1)}) custom-call(s32[1]{0:T(128)S(6)} %copy.20.slot, s32[1]{0:T(128)} %copy.21.dest, s32[2]{0:T(128)} %lengths.3, s32[2,8]{1,0:T(2,128)} %table.3, bf16[16,128,512]{2,1,0:T(8,128)(2,1)} %pool.3), custom_call_target="tpu_custom_call" | custom-call | bytes 2097152 | tf_op jit(solution)/shard_map/leaving/pallas_call | solution.py:535
  6.1 0.9 broadcast_select_fusion
  7.0 2.9 %collective-permute-start.3 = (bf16[528,512]{1,0:T(8,128)(2,1)}, bf16[528,512]{1,0:T(8,128)(2,1)}, u32[]{:S(2)}, u32[]{:S(2)}) collective-permute-start(bf16[528,512]{1,0:T(8,128)(2,1)} %broadcast_select_fusion), channel_id=1, source_target_pairs={{0,2},{1,3},{2,0},{3,1},{4,6},{5,7},{6,4},{7,5},{8,10},{9,11},{10,... | collective-permute-start | bytes 1622024 | tf_op jit(solution)/shard_map/ppermute | solution.py:561
  9.8 0.8 broadcast_select_fusion.1
  10.7 9.3 %front.1 = (f32[64,2048]{1,0:T(8,128)}, f32[64,64]{1,0:T(8,128)S(1)}, bf16[64,64]{1,0:T(8,128)(2,1)S(1)}, bf16[64,512]{1,0:T(8,128)(2,1)S(1)}, bf16[64,1536]{1,0...) custom-call(s32[1]{0:T(128)S(6)} %copy.20.slot, s32[2]{0:T(128)S(1)} %copy-done.11, s32[2,8]{1,0:T(2,128)S(1)} %copy-done.10, ...), custom_call_target="tpu_custom_call" | custom-call | flops 3000000000 | bytes 3000000 | tf_op jit(solution)/shard_map/front/pallas_call | solution.py:573
  20.7 4.1 %collective-permute-start.2 = (bf16[80,1536]{1,0:T(8,128)(2,1)S(1)}, bf16[80,1536]{1,0:T(8,128)(2,1)S(1)}, u32[]{:S(2)}, u32[]{:S(2)}) collective-permute-start(bf16[80,1536]{1,0:T(8,128)(2,1)S(1)} %get-tuple-element.40.staying.rest_0_), channel_id=1, source_target_pairs={{0,24},{4,28},{8,16},{12,20},{16,8},{20,12},{24,0},{28,4},{1,25},{... | collective-permute-start | bytes 737288 | tf_op jit(solution)/shard_map/ppermute | solution.py:610
  24.8 1.3 routes.1
  26.1 3.6 %early.1 = (s32[2]{0:T(128)S(1)}, bf16[2,384,128]{2,1,0:T(8,128)(2,1)S(1)}, f32[2,384,128]{2,1,0:T(8,128)S(1)}, f32[2,384,1]{2,1,0:T(8,128)S(1)}, f32[2,384,1]{2,1,0:T(8,128)S(1)}, /*index=5*/bf16[128,512]{1,0:T(8,128)(2,1)}) custom-call(s32[1]{0:T(128)S(6)} %copy.20.slot, s32[1]{0:T(128)} %bitcast.3.me, f32[64,64]{1,0:T(8,128)S(1)} %get-tuple-element.44.reach, ...), custom_call_target="tpu_custom_call" | custom-call | flops 1000000000 | bytes 2000000 | tf_op jit(solution)/shard_map/early/pallas_call | solution.py:627
  29.8 0.8 collective-permute-done.2.parcel.staying.rest_2_
  30.6 3.3 %collective-permute-done.4.rest_2_ = bf16[512,512]{1,0:T(8,128)(2,1)S(1)} collective-permute-done((bf16[512,512]{1,0:T(8,128)(2,1)}, bf16[512,512]{1,0:T(8,128)(2,1)S(1)}, u32[]{:S(2)}, u32[]{:S(2)}) %collective-permute-start.4) | collective-permute-done | bytes 524320 | tf_op jit(solution)/shard_map/ppermute | solution.py:561
  33.9 4.2 %arrival.1 = (bf16[64,1536]{1,0:T(8,128)(2,1)S(1)}, bf16[64,1536]{1,0:T(8,128)(2,1)S(1)}) custom-call(s32[1]{0:T(128)S(6)} %copy.20.slot, s32[2]{0:T(128)S(1)} %get-tuple-element.49.pick, bf16[2,384,128]{2,1,0:T(8,128)(2,1)S(1)} %get-tuple-element.50.stacked, f32[2,384,128]{2,1,0:T(8,128)S(1)} %get-tuple-element.51.mixed, ...), custom_call_target="tpu_custom_call" | custom-call | flops 2000000000 | bytes 8000000 | tf_op jit(solution)/shard_map/arrival/pallas_call | solution.py:657
  38.0 3.9 %collective-permute-start.5 = (bf16[64,1536]{1,0:T(8,128)(2,1)S(1)}, bf16[64,1536]{1,0:T(8,128)(2,1)S(1)}, u32[]{:S(2)}, u32[]{:S(2)}) collective-permute-start(bf16[64,1536]{1,0:T(8,128)(2,1)S(1)} %get-tuple-element.57.moved.rest_1_), channel_id=1, source_target_pairs={{0,24},{4,28},{8,16},{12,20},{16,8},{20,12},{24,0},{28,4},{1,25},{... | collective-permute-start | bytes 589832 | tf_op jit(solution)/shard_map/ppermute | solution.py:677
  42.5 3.9 %collective-permute-done.5.moved.rest_3_ = bf16[64,1536]{1,0:T(8,128)(2,1)S(1)} collective-permute-done((bf16[64,1536]{1,0:T(8,128)(2,1)S(1)}, bf16[64,1536]{1,0:T(8,128)(2,1)S(1)}, u32[]{:S(2)}, u32[]{:S(2)}) %collective-permute-start.5) | collective-permute-done | bytes 196640 | tf_op jit(solution)/shard_map/ppermute | solution.py:677
  46.5 1.5 pack.3
  48.0 7.1 %all-to-all-start = ((bf16[16,32,1536]{2,1,0:T(8,128)(2,1)}), bf16[16,32,1536]{2,1,0:T(8,128)(2,1)S(1)}, u32[]{:S(2)}, u32[]{:S(2)}) async-start(bf16[16,32,1536]{2,1,0:T(8,128)(2,1)} %bitcast.20), calls=%async_computation | async-start | bytes 3145728 | tf_op jit(solution)/shard_map/all_to_all | solution.py:531
  55.1 1.5 pack.2
  56.6 21.5 %all-to-all-done = bf16[16,32,1536]{2,1,0:T(8,128)(2,1)S(1)} async-done(((bf16[16,32,1536]{2,1,0:T(8,128)(2,1)}), bf16[16,32,1536]{2,1,0:T(8,128)(2,1)S(1)}, u32[]{:S(2)}, u32[]{:S(2)}) %all-to-all-start) | async-done | bytes 1572896 | tf_op jit(solution)/shard_map/all_to_all | solution.py:531
  78.1 3.9 %all-to-all-start.1 = ((bf16[16,32,1536]{2,1,0:T(8,128)(2,1)}), bf16[16,32,1536]{2,1,0:T(8,128)(2,1)S(1)}, u32[]{:S(2)}, u32[]{:S(2)}) async-start(bf16[16,32,1536]{2,1,0:T(8,128)(2,1)} %bitcast.19), calls=%async_computation.1 | async-start | bytes 3145728 | tf_op jit(solution)/shard_map/all_to_all | solution.py:531
  82.0 0.9 copy-done.1
  83.0 0.9 copy-done.3
  83.9 0.9 copy-done.5
  84.8 3.1 %shares.1 = bf16[2,2,128,512]{3,2,1,0:T(8,128)(2,1)} custom-call(s32[1]{0:T(128)} %bitcast.2.base, bf16[32,1536]{1,0:T(8,128)(2,1)} %bitcast.23, bf16[80,1536]{1,0:T(8,128)(2,1)S(1)} %get-tuple-element.40.staying.rest_0_, bf16[64,1536]{1,0:T(8,128)(2,1)S(1)} %copy-done.3, bf16[80,1536]{1,0:T(8,128)(2,1)S(1)} %copy-done.1, bf16[64,1536]{1,0:T(8,128)(2,1)S(1)} %copy-done.5, ...), custom_call_target="tpu_custom_call" | custom-call | flops 300000000 | bytes 1000000 | tf_op jit(solution)/shard_map/shares/pallas_call | solution.py:708
  88.0 7.1 %experts.2 = bf16[512,1536]{1,0:T(8,128)(2,1)} custom-call(bf16[512,1536]{1,0:T(8,128)(2,1)S(1)} %bitcast.17, bf16[1,1536,768]{2,1,0:T(8,128)(2,1)} %w_gate.3, bf16[1,1536,768]{2,1,0:T(8,128)(2,1)} %w_up.3, bf16[1,768,1536]{2,1,0:T(8,128)(2,1)} %w_down.3), custom_call_target="tpu_custom_call" | custom-call | flops 3623878656 | bytes 7077888 | tf_op jit(solution)/shard_map/experts/pallas_call | solution.py:486
  95.0 9.8 %all-to-all-done.1 = bf16[16,32,1536]{2,1,0:T(8,128)(2,1)S(1)} async-done(((bf16[16,32,1536]{2,1,0:T(8,128)(2,1)}), bf16[16,32,1536]{2,1,0:T(8,128)(2,1)S(1)}, u32[]{:S(2)}, u32[]{:S(2)}) %all-to-all-start.1) | async-done | bytes 1572896 | tf_op jit(solution)/shard_map/all_to_all | solution.py:531
  104.9 3.7 %all-to-all-start.2 = ((bf16[16,32,1536]{2,1,0:T(8,128)(2,1)}), bf16[16,32,1536]{2,1,0:T(8,128)(2,1)S(1)}, u32[]{:S(2)}, u32[]{:S(2)}) async-start(bf16[16,32,1536]{2,1,0:T(8,128)(2,1)} %bitcast.22), calls=%async_computation.2 | async-start | bytes 3145728 | tf_op jit(solution)/shard_map/all_to_all | solution.py:531
  108.6 7.0 %experts.3 = bf16[512,1536]{1,0:T(8,128)(2,1)} custom-call(bf16[512,1536]{1,0:T(8,128)(2,1)S(1)} %bitcast.18, bf16[1,1536,768]{2,1,0:T(8,128)(2,1)} %w_gate.3, bf16[1,1536,768]{2,1,0:T(8,128)(2,1)} %w_up.3, bf16[1,768,1536]{2,1,0:T(8,128)(2,1)} %w_down.3), custom_call_target="tpu_custom_call" | custom-call | flops 3623878656 | bytes 7077888 | tf_op jit(solution)/shard_map/experts/pallas_call | solution.py:486
  115.6 16.0 %all-to-all-done.2 = bf16[16,32,1536]{2,1,0:T(8,128)(2,1)S(1)} async-done(((bf16[16,32,1536]{2,1,0:T(8,128)(2,1)}), bf16[16,32,1536]{2,1,0:T(8,128)(2,1)S(1)}, u32[]{:S(2)}, u32[]{:S(2)}) %all-to-all-start.2) | async-done | bytes 1572896 | tf_op jit(solution)/shard_map/all_to_all | solution.py:531
  131.6 3.7 %all-to-all-start.3 = ((bf16[16,32,1536]{2,1,0:T(8,128)(2,1)}), bf16[16,32,1536]{2,1,0:T(8,128)(2,1)S(1)}, u32[]{:S(2)}, u32[]{:S(2)}) async-start(bf16[16,32,1536]{2,1,0:T(8,128)(2,1)} %bitcast.21), calls=%async_computation.3 | async-start | bytes 3145728 | tf_op jit(solution)/shard_map/all_to_all | solution.py:531
  135.3 1.6 partial.1
  136.9 2.9 %collective-permute-start.6 = (bf16[128,1536]{1,0:T(8,128)(2,1)S(1)}, bf16[128,1536]{1,0:T(8,128)(2,1)S(1)}, u32[]{:S(2)}, u32[]{:S(2)}) collective-permute-start(bf16[128,1536]{1,0:T(8,128)(2,1)S(1)} %partial.1), channel_id=1, source_target_pairs={{0,24},{4,28},{8,16},{12,20},{16,8},{20,12},{24,0},{28,4},{1,25},{... | collective-permute-start | bytes 1179656 | tf_op jit(solution)/shard_map/ppermute | solution.py:745
  139.8 25.0 %collective-permute-done.6.far = bf16[128,1536]{1,0:T(8,128)(2,1)S(1)} collective-permute-done((bf16[128,1536]{1,0:T(8,128)(2,1)S(1)}, bf16[128,1536]{1,0:T(8,128)(2,1)S(1)}, u32[]{:S(2)}, u32[]{:S(2)}) %collective-permute-start.6) | collective-permute-done | bytes 393248 | tf_op jit(solution)/shard_map/ppermute | solution.py:745
  164.9 2.3 %final.1 = bf16[128,1536]{1,0:T(8,128)(2,1)} custom-call(s32[1]{0:T(128)S(6)} %copy.20.slot, bf16[2,2,128,512]{3,2,1,0:T(8,128)(2,1)} %shares.1, bf16[64,1536]{1,0:T(8,128)(2,1)S(1)} %copy-done.7, bf16[64,1536]{1,0:T(8,128)(2,1)S(1)} %copy-done.9, bf16[128,1536]{1,0:T(8,128)(2,1)S(1)} %collective-permute-done.6.far, bf16[512,1536]{1,0:T(8,128)(2,1)S(1)} %bitcast.16), custom_call_target="tpu_custom_call" | custom-call | flops 400000000 | bytes 2000000 | tf_op jit(solution)/shard_map/final/pallas_call | solution.py:747
  (35 shorter events, 3.4 us)
Async XLA Ops:
  0.6 4.0 %copy-start.12 = (bf16[1536]{0:T(1024)(128)(2,1)S(1)}, bf16[1536]{0:T(1024)(128)(2,1)}, u32[]{:S(2)}) copy-start(bf16[1536]{0:T(1024)(128)(2,1)} %param.29) | copy-start | bytes 9220
  0.6 4.6 %copy-start.13 = (bf16[1536]{0:T(1024)(128)(2,1)S(1)}, bf16[1536]{0:T(1024)(128)(2,1)}, u32[]{:S(2)}) copy-start(bf16[1536]{0:T(1024)(128)(2,1)} %param.26) | copy-start | bytes 9220
  4.0 2.1 %collective-permute-start = (bf16[528,512]{1,0:T(8,128)(2,1)S(1)}, bf16[528,512]{1,0:T(8,128)(2,1)S(1)}, u32[]{:S(2)}, u32[]{:S(2)}) collective-permute-start(bf16[528,512]{1,0:T(8,128)(2,1)S(1)} %get-tuple-element.37.rest_0_), channel_id=1, source_target_pairs={{0,1},{1,0},{2,3},{3,2},{4,5},{5,4},{6,7},{7,6},{8,9},{9,8},{10,11... | collective-permute-start | bytes 1622024 | tf_op jit(solution)/shard_map/ppermute | solution.py:552
  4.5 5.3 %collective-permute-start.1 = (bf16[512,512]{1,0:T(8,128)(2,1)S(1)}, bf16[512,512]{1,0:T(8,128)(2,1)S(1)}, u32[]{:S(2)}, u32[]{:S(2)}) collective-permute-start(bf16[512,512]{1,0:T(8,128)(2,1)S(1)} %get-tuple-element.54.rest_0_), channel_id=1, source_target_pairs={{0,1},{1,0},{2,3},{3,2},{4,5},{5,4},{6,7},{7,6},{8,9},{9,8},{10,11... | collective-permute-start | bytes 1572872 | tf_op jit(solution)/shard_map/ppermute | solution.py:552
  5.8 4.9 %copy-start.10 = (s32[2,8]{1,0:T(2,128)S(1)}, s32[2,8]{1,0:T(2,128)}, u32[]{:S(2)}) copy-start(s32[2,8]{1,0:T(2,128)} %table.3) | copy-start | bytes 196
  5.8 4.9 %copy-start.11 = (s32[2]{0:T(128)S(1)}, s32[2]{0:T(128)}, u32[]{:S(2)}) copy-start(s32[2]{0:T(128)} %lengths.3) | copy-start | bytes 28
  7.0 19.2 %collective-permute-start.3 = (bf16[528,512]{1,0:T(8,128)(2,1)}, bf16[528,512]{1,0:T(8,128)(2,1)}, u32[]{:S(2)}, u32[]{:S(2)}) collective-permute-start(bf16[528,512]{1,0:T(8,128)(2,1)} %broadcast_select_fusion), channel_id=1, source_target_pairs={{0,2},{1,3},{2,0},{3,1},{4,6},{5,7},{6,4},{7,5},{8,10},{9,11},{10,... | collective-permute-start | bytes 1622024 | tf_op jit(solution)/shard_map/ppermute | solution.py:561
  10.7 23.2 %collective-permute-start.4 = (bf16[512,512]{1,0:T(8,128)(2,1)}, bf16[512,512]{1,0:T(8,128)(2,1)S(1)}, u32[]{:S(2)}, u32[]{:S(2)}) collective-permute-start(bf16[512,512]{1,0:T(8,128)(2,1)} %broadcast_select_fusion.1), channel_id=1, source_target_pairs={{0,2},{1,3},{2,0},{3,1},{4,6},{5,7},{6,4},{7,5},{8,10},{9,11},{10,... | collective-permute-start | bytes 1572872 | tf_op jit(solution)/shard_map/ppermute | solution.py:561
  20.0 0.7 copy-start.6
  20.7 9.9 %collective-permute-start.2 = (bf16[80,1536]{1,0:T(8,128)(2,1)S(1)}, bf16[80,1536]{1,0:T(8,128)(2,1)S(1)}, u32[]{:S(2)}, u32[]{:S(2)}) collective-permute-start(bf16[80,1536]{1,0:T(8,128)(2,1)S(1)} %get-tuple-element.40.staying.rest_0_), channel_id=1, source_target_pairs={{0,24},{4,28},{8,16},{12,20},{16,8},{20,12},{24,0},{28,4},{1,25},{... | collective-permute-start | bytes 737288 | tf_op jit(solution)/shard_map/ppermute | solution.py:610
  30.6 15.9 %copy-start = (bf16[80,1536]{1,0:T(8,128)(2,1)}, bf16[80,1536]{1,0:T(8,128)(2,1)S(1)}, u32[]{:S(2)}) copy-start(bf16[80,1536]{1,0:T(8,128)(2,1)S(1)} %collective-permute-done.2.parcel.staying.rest_2_) | copy-start | bytes 737284
  38.0 10.0 %copy-start.8 = (bf16[64,1536]{1,0:T(8,128)(2,1)}, bf16[64,1536]{1,0:T(8,128)(2,1)S(1)}, u32[]{:S(2)}) copy-start(bf16[64,1536]{1,0:T(8,128)(2,1)S(1)} %get-tuple-element.66.moved) | copy-start | bytes 589828
  38.0 17.0 %copy-start.2 = (bf16[64,1536]{1,0:T(8,128)(2,1)}, bf16[64,1536]{1,0:T(8,128)(2,1)S(1)}, u32[]{:S(2)}) copy-start(bf16[64,1536]{1,0:T(8,128)(2,1)S(1)} %get-tuple-element.57.moved.rest_1_) | copy-start | bytes 589828
  38.0 8.4 %collective-permute-start.5 = (bf16[64,1536]{1,0:T(8,128)(2,1)S(1)}, bf16[64,1536]{1,0:T(8,128)(2,1)S(1)}, u32[]{:S(2)}, u32[]{:S(2)}) collective-permute-start(bf16[64,1536]{1,0:T(8,128)(2,1)S(1)} %get-tuple-element.57.moved.rest_1_), channel_id=1, source_target_pairs={{0,24},{4,28},{8,16},{12,20},{16,8},{20,12},{24,0},{28,4},{1,25},{... | collective-permute-start | bytes 589832 | tf_op jit(solution)/shard_map/ppermute | solution.py:677
  46.5 1.5 copy-start.4
  48.0 30.1 %all-to-all-start = ((bf16[16,32,1536]{2,1,0:T(8,128)(2,1)}), bf16[16,32,1536]{2,1,0:T(8,128)(2,1)S(1)}, u32[]{:S(2)}, u32[]{:S(2)}) async-start(bf16[16,32,1536]{2,1,0:T(8,128)(2,1)} %bitcast.20), calls=%async_computation | async-start | bytes 3145728 | tf_op jit(solution)/shard_map/all_to_all | solution.py:531
  78.1 26.7 %all-to-all-start.1 = ((bf16[16,32,1536]{2,1,0:T(8,128)(2,1)}), bf16[16,32,1536]{2,1,0:T(8,128)(2,1)S(1)}, u32[]{:S(2)}, u32[]{:S(2)}) async-start(bf16[16,32,1536]{2,1,0:T(8,128)(2,1)} %bitcast.19), calls=%async_computation.1 | async-start | bytes 3145728 | tf_op jit(solution)/shard_map/all_to_all | solution.py:531
  82.0 0.9 copy-start.1
  83.0 0.9 copy-start.3
  83.9 0.9 copy-start.5
  104.9 26.7 %all-to-all-start.2 = ((bf16[16,32,1536]{2,1,0:T(8,128)(2,1)}), bf16[16,32,1536]{2,1,0:T(8,128)(2,1)S(1)}, u32[]{:S(2)}, u32[]{:S(2)}) async-start(bf16[16,32,1536]{2,1,0:T(8,128)(2,1)} %bitcast.22), calls=%async_computation.2 | async-start | bytes 3145728 | tf_op jit(solution)/shard_map/all_to_all | solution.py:531
  131.6 33.3 %all-to-all-start.3 = ((bf16[16,32,1536]{2,1,0:T(8,128)(2,1)}), bf16[16,32,1536]{2,1,0:T(8,128)(2,1)S(1)}, u32[]{:S(2)}, u32[]{:S(2)}) async-start(bf16[16,32,1536]{2,1,0:T(8,128)(2,1)} %bitcast.21), calls=%async_computation.3 | async-start | bytes 3145728 | tf_op jit(solution)/shard_map/all_to_all | solution.py:531
  135.3 29.6 %copy-start.7 = (bf16[64,1536]{1,0:T(8,128)(2,1)S(1)}, bf16[64,1536]{1,0:T(8,128)(2,1)}, u32[]{:S(2)}) copy-start(bf16[64,1536]{1,0:T(8,128)(2,1)} %copy-done.6) | copy-start | bytes 589828
  135.3 29.6 %copy-start.9 = (bf16[64,1536]{1,0:T(8,128)(2,1)S(1)}, bf16[64,1536]{1,0:T(8,128)(2,1)}, u32[]{:S(2)}) copy-start(bf16[64,1536]{1,0:T(8,128)(2,1)} %copy-done.8) | copy-start | bytes 589828
  136.9 27.9 %collective-permute-start.6 = (bf16[128,1536]{1,0:T(8,128)(2,1)S(1)}, bf16[128,1536]{1,0:T(8,128)(2,1)S(1)}, u32[]{:S(2)}, u32[]{:S(2)}) collective-permute-start(bf16[128,1536]{1,0:T(8,128)(2,1)S(1)} %partial.1), channel_id=1, source_target_pairs={{0,24},{4,28},{8,16},{12,20},{16,8},{20,12},{24,0},{28,4},{1,25},{... | collective-permute-start | bytes 1179656 | tf_op jit(solution)/shard_map/ppermute | solution.py:745

commit v5 on v4

--- a/solution.py
+++ b/solution.py
@@ -460,16 +460,24 @@
     out[...] = (dot(pair[0], values) + dot(pair[1], values)).astype(jnp.bfloat16)
 
 
-def final_kernel(slot, shares, staying, moved, far, rows, out, pair, sems):
-    finish(load_all(((shares.at[0], pair),), sems))
+def near_kernel(shares, staying, moved, arrived, total, pair, kept, rows, sems):
+    pairs = (
+        (shares.at[0], pair), (staying, kept.at[0]), (moved, kept.at[1]), (arrived, rows),
+    )
+    finish(load_all(pairs, sems))
     draft = staying.shape[0]
     values = rows[...]
-    total = dot(pair[0], values) + dot(pair[1], values) + far[...].astype(jnp.float32)
-    for at, kept, part in (
-        (1 - slot[0], staying, total[:draft]), (slot[0], moved, total[draft:])
-    ):
+    near = dot(pair[0], values) + dot(pair[1], values)
+    total[:draft, :] = kept[0].astype(jnp.float32) + near[:draft]
+    total[draft:, :] = kept[1].astype(jnp.float32) + near[draft:]
+
+
+def final_kernel(slot, total, far, out):
+    draft = out.shape[0] // 2
+    for i, at in enumerate((1 - slot[0], slot[0])):
         at = pl.ds(pl.multiple_of(at * draft, draft), draft)
-        out[at, :] = (kept[...].astype(jnp.float32) + part).astype(jnp.bfloat16)
+        span = slice(i * draft, (i + 1) * draft)
+        out[at, :] = (total[span, :] + far[span, :].astype(jnp.float32)).astype(jnp.bfloat16)
 
 
 def params(mib, rows=512):
@@ -744,19 +752,30 @@
     )(*in_hbm(shares), *in_vmem(far_back))
     own_far = lax.ppermute(far_sum, "req", swap)
     near_back = within_half(near_out)
+    total = pl.pallas_call(
+        near_kernel,
+        in_specs=[HBM] * 3 + [ANY],
+        out_specs=VMEM,
+        out_shape=pltpu.VMEM((tokens, model), f32),
+        scratch_shapes=[
+            pltpu.VMEM((2, tokens, slot_rows), bf16),
+            pltpu.VMEM((2, draft, model), bf16),
+            pltpu.VMEM((slot_rows, model), bf16),
+            pltpu.SemaphoreType.DMA((4,)),
+        ],
+        compiler_params=params(56),
+        cost_estimate=cost(4e8, 2e6),
+        name="near",
+    )(*in_hbm(shares, staying, moved), near_back)
     layer_out = pl.pallas_call(
         final_kernel,
-        in_specs=[SMEM, HBM] + [VMEM] * 4,
+        in_specs=[SMEM] + [VMEM] * 2,
         out_specs=VMEM,
         out_shape=jax.ShapeDtypeStruct((tokens, model), bf16),
-        scratch_shapes=[
-            pltpu.VMEM((2, tokens, slot_rows), bf16),
-            pltpu.SemaphoreType.DMA((1,)),
-        ],
-        compiler_params=params(10, slot_rows),
-        cost_estimate=cost(4e8, 2e6),
+        compiler_params=params(8),
+        cost_estimate=cost(1e6, 2e6),
         name="final",
-    )(mig_slot, *in_hbm(shares), *in_vmem(staying, moved, own_far, near_back))
+    )(mig_slot, *in_vmem(total, own_far))
     return layer_out, compact.reshape(requests, draft, kv_width)
 
 

time: 168 us -> 166 us (0.988)
  waiting for transfers between devices: 80.6 us -> 77.1 us
    ppermute x1, waiting for transfers between devices: 25 us -> 3.03 us  [per_device(): own_far = lax.ppermute(far_sum, 'req', swap)]
    all_to_all x4, waiting for transfers between devices: 47.3 us -> 65.7 us  [within_half(): lax.all_to_all(rows, AXES, 0, 0, tiled=True, axis_index_groups=groups)]
    unnamed x28 -> x26, local copies, waits for them, and re-layouts: 3.49 us -> 4.66 us
  transfers between devices with their start and end apart: 11 -> 11, of which waited for: 8 -> 9; matrix products, arithmetic and copies ran while one was open for 2% -> 2% of each run, Pallas kernels for 21% -> 23%
where the time goes in v5:
time: 166 us
  waiting for transfers between devices  77.1 us (46%)
  Pallas kernels  46 us (28%)
  starting transfers between devices  32.8 us (20%)
  local copies, waits for them, and re-layouts  5.86 us (4%)
  between operations  2.17 us (1%)
  other arithmetic  1.7 us (1%)
    all_to_all x4, waiting for transfers between devices, within_half(): lax.all_to_all(rows, AXES, 0, 0, tiled=True, axis_index_groups=groups)  65.7 us
    all_to_all x4, starting transfers between devices, within_half(): lax.all_to_all(rows, AXES, 0, 0, tiled=True, axis_index_groups=groups)  18.4 us
    pallas_call x2, Pallas kernels, run_experts(): pl.pallas_call(expert_kernel, in_specs=[VMEM] + [HBM] * 3, out_specs=HBM,...  14.1 us
    pallas_call x1, Pallas kernels, per_device(): pl.pallas_call(front_kernel, in_specs=[SMEM] * 3 + [HBM] * 10, out_specs=...  9.33 us
    unnamed x26, local copies, waits for them, and re-layouts  4.66 us
    pallas_call x1, Pallas kernels, per_device(): pl.pallas_call(arrival_kernel, in_specs=[SMEM] * 2 + [VMEM] * 4 + [HBM] *...  4.16 us
    ppermute x1, starting transfers between devices, per_device(): far_parcel = lax.ppermute(parcel, 'req', swap)  4.08 us
    ppermute x1, waiting for transfers between devices, per_device(): far_moved = lax.ppermute(moved_normed, 'req', swap)  3.95 us
  transfers between devices with their start and end apart: 11, of which 9 were waited for; matrix products, arithmetic and copies ran while one was open for 2% of the time, Pallas kernels for 23%

profile of v5, /device:TPU:0, one launch (start us, length us, event | category | flops | bytes accessed | tf_op | source)
XLA Modules:
  0.0 165.6 jit_solution(18414155587497962886)
XLA Ops:
  2.0 2.1 %leaving.1 = (bf16[528,512]{1,0:T(8,128)(2,1)S(1)}, bf16[512,512]{1,0:T(8,128)(2,1)S(1)}) custom-call(s32[1]{0:T(128)S(6)} %copy.20.slot, s32[1]{0:T(128)} %copy.21.dest, s32[2]{0:T(128)} %lengths.3, s32[2,8]{1,0:T(2,128)} %table.3, bf16[16,128,512]{2,1,0:T(8,128)(2,1)} %pool.3), custom_call_target="tpu_custom_call" | custom-call | bytes 2097152 | tf_op jit(solution)/shard_map/leaving/pallas_call | solution.py:543
  6.1 0.9 broadcast_select_fusion
  7.0 2.9 %collective-permute-start.3 = (bf16[528,512]{1,0:T(8,128)(2,1)}, bf16[528,512]{1,0:T(8,128)(2,1)}, u32[]{:S(2)}, u32[]{:S(2)}) collective-permute-start(bf16[528,512]{1,0:T(8,128)(2,1)} %broadcast_select_fusion), channel_id=1, source_target_pairs={{0,2},{1,3},{2,0},{3,1},{4,6},{5,7},{6,4},{7,5},{8,10},{9,11},{10,... | collective-permute-start | bytes 1622024 | tf_op jit(solution)/shard_map/ppermute | solution.py:569
  10.7 9.3 %front.1 = (f32[64,2048]{1,0:T(8,128)}, f32[64,64]{1,0:T(8,128)S(1)}, bf16[64,64]{1,0:T(8,128)(2,1)S(1)}, bf16[64,512]{1,0:T(8,128)(2,1)S(1)}, bf16[64,1536]{1,0...) custom-call(s32[1]{0:T(128)S(6)} %copy.20.slot, s32[2]{0:T(128)S(1)} %copy-done.9, s32[2,8]{1,0:T(2,128)S(1)} %copy-done.8, ...), custom_call_target="tpu_custom_call" | custom-call | flops 3000000000 | bytes 3000000 | tf_op jit(solution)/shard_map/front/pallas_call | solution.py:581
  20.7 4.1 %collective-permute-start.2 = (bf16[80,1536]{1,0:T(8,128)(2,1)S(1)}, bf16[80,1536]{1,0:T(8,128)(2,1)S(1)}, u32[]{:S(2)}, u32[]{:S(2)}) collective-permute-start(bf16[80,1536]{1,0:T(8,128)(2,1)S(1)} %get-tuple-element.40.staying.rest_0_), channel_id=1, source_target_pairs={{0,24},{4,28},{8,16},{12,20},{16,8},{20,12},{24,0},{28,4},{1,25},{... | collective-permute-start | bytes 737288 | tf_op jit(solution)/shard_map/ppermute | solution.py:618
  24.8 1.3 routes.1
  26.1 3.6 %early.1 = (s32[2]{0:T(128)S(1)}, bf16[2,384,128]{2,1,0:T(8,128)(2,1)S(1)}, f32[2,384,128]{2,1,0:T(8,128)S(1)}, f32[2,384,1]{2,1,0:T(8,128)S(1)}, f32[2,384,1]{2,1,0:T(8,128)S(1)}, /*index=5*/bf16[128,512]{1,0:T(8,128)(2,1)}) custom-call(s32[1]{0:T(128)S(6)} %copy.20.slot, s32[1]{0:T(128)} %bitcast.3.me, f32[64,64]{1,0:T(8,128)S(1)} %get-tuple-element.44.reach, ...), custom_call_target="tpu_custom_call" | custom-call | flops 1000000000 | bytes 2000000 | tf_op jit(solution)/shard_map/early/pallas_call | solution.py:635
  30.6 3.3 %collective-permute-done.4.rest_2_ = bf16[512,512]{1,0:T(8,128)(2,1)S(1)} collective-permute-done((bf16[512,512]{1,0:T(8,128)(2,1)}, bf16[512,512]{1,0:T(8,128)(2,1)S(1)}, u32[]{:S(2)}, u32[]{:S(2)}) %collective-permute-start.4) | collective-permute-done | bytes 524320 | tf_op jit(solution)/shard_map/ppermute | solution.py:569
  33.9 4.2 %arrival.1 = (bf16[64,1536]{1,0:T(8,128)(2,1)S(1)}, bf16[64,1536]{1,0:T(8,128)(2,1)S(1)}) custom-call(s32[1]{0:T(128)S(6)} %copy.20.slot, s32[2]{0:T(128)S(1)} %get-tuple-element.49.pick, bf16[2,384,128]{2,1,0:T(8,128)(2,1)S(1)} %get-tuple-element.50.stacked, f32[2,384,128]{2,1,0:T(8,128)S(1)} %get-tuple-element.51.mixed, ...), custom_call_target="tpu_custom_call" | custom-call | flops 2000000000 | bytes 8000000 | tf_op jit(solution)/shard_map/arrival/pallas_call | solution.py:665
  38.1 3.9 %collective-permute-start.5 = (bf16[64,1536]{1,0:T(8,128)(2,1)S(1)}, bf16[64,1536]{1,0:T(8,128)(2,1)S(1)}, u32[]{:S(2)}, u32[]{:S(2)}) collective-permute-start(bf16[64,1536]{1,0:T(8,128)(2,1)S(1)} %get-tuple-element.57.moved.rest_1_), channel_id=1, source_target_pairs={{0,24},{4,28},{8,16},{12,20},{16,8},{20,12},{24,0},{28,4},{1,25},{... | collective-permute-start | bytes 589832 | tf_op jit(solution)/shard_map/ppermute | solution.py:685
  42.5 3.9 %collective-permute-done.5.moved.rest_3_ = bf16[64,1536]{1,0:T(8,128)(2,1)S(1)} collective-permute-done((bf16[64,1536]{1,0:T(8,128)(2,1)S(1)}, bf16[64,1536]{1,0:T(8,128)(2,1)S(1)}, u32[]{:S(2)}, u32[]{:S(2)}) %collective-permute-start.5) | collective-permute-done | bytes 196640 | tf_op jit(solution)/shard_map/ppermute | solution.py:685
  46.5 1.5 pack.3
  48.0 7.1 %all-to-all-start = ((bf16[16,32,1536]{2,1,0:T(8,128)(2,1)}), bf16[16,32,1536]{2,1,0:T(8,128)(2,1)S(1)}, u32[]{:S(2)}, u32[]{:S(2)}) async-start(bf16[16,32,1536]{2,1,0:T(8,128)(2,1)} %bitcast.20), calls=%async_computation | async-start | bytes 3145728 | tf_op jit(solution)/shard_map/all_to_all | solution.py:539
  55.1 1.6 pack.2
  56.6 21.5 %all-to-all-done = bf16[16,32,1536]{2,1,0:T(8,128)(2,1)S(1)} async-done(((bf16[16,32,1536]{2,1,0:T(8,128)(2,1)}), bf16[16,32,1536]{2,1,0:T(8,128)(2,1)S(1)}, u32[]{:S(2)}, u32[]{:S(2)}) %all-to-all-start) | async-done | bytes 1572896 | tf_op jit(solution)/shard_map/all_to_all | solution.py:539
  78.1 3.9 %all-to-all-start.1 = ((bf16[16,32,1536]{2,1,0:T(8,128)(2,1)}), bf16[16,32,1536]{2,1,0:T(8,128)(2,1)S(1)}, u32[]{:S(2)}, u32[]{:S(2)}) async-start(bf16[16,32,1536]{2,1,0:T(8,128)(2,1)} %bitcast.18), calls=%async_computation.1 | async-start | bytes 3145728 | tf_op jit(solution)/shard_map/all_to_all | solution.py:539
  82.0 0.9 copy-done.1
  83.0 0.9 copy-done.3
  83.9 0.9 copy-done.5
  84.8 3.1 %shares.1 = bf16[2,2,128,512]{3,2,1,0:T(8,128)(2,1)} custom-call(s32[1]{0:T(128)} %bitcast.2.base, bf16[32,1536]{1,0:T(8,128)(2,1)} %bitcast.23, bf16[80,1536]{1,0:T(8,128)(2,1)S(1)} %get-tuple-element.40.staying.rest_0_, bf16[64,1536]{1,0:T(8,128)(2,1)S(1)} %copy-done.3, bf16[80,1536]{1,0:T(8,128)(2,1)S(1)} %copy-done.1, bf16[64,1536]{1,0:T(8,128)(2,1)S(1)} %copy-done.5, ...), custom_call_target="tpu_custom_call" | custom-call | flops 300000000 | bytes 1000000 | tf_op jit(solution)/shard_map/shares/pallas_call | solution.py:716
  88.0 7.0 %experts.2 = bf16[512,1536]{1,0:T(8,128)(2,1)} custom-call(bf16[512,1536]{1,0:T(8,128)(2,1)S(1)} %bitcast.16, bf16[1,1536,768]{2,1,0:T(8,128)(2,1)} %w_gate.3, bf16[1,1536,768]{2,1,0:T(8,128)(2,1)} %w_up.3, bf16[1,768,1536]{2,1,0:T(8,128)(2,1)} %w_down.3), custom_call_target="tpu_custom_call" | custom-call | flops 3623878656 | bytes 7077888 | tf_op jit(solution)/shard_map/experts/pallas_call | solution.py:494
  95.0 9.9 %all-to-all-done.1 = bf16[16,32,1536]{2,1,0:T(8,128)(2,1)S(1)} async-done(((bf16[16,32,1536]{2,1,0:T(8,128)(2,1)}), bf16[16,32,1536]{2,1,0:T(8,128)(2,1)S(1)}, u32[]{:S(2)}, u32[]{:S(2)}) %all-to-all-start.1) | async-done | bytes 1572896 | tf_op jit(solution)/shard_map/all_to_all | solution.py:539
  104.8 3.7 %all-to-all-start.2 = ((bf16[16,32,1536]{2,1,0:T(8,128)(2,1)}), bf16[16,32,1536]{2,1,0:T(8,128)(2,1)S(1)}, u32[]{:S(2)}, u32[]{:S(2)}) async-start(bf16[16,32,1536]{2,1,0:T(8,128)(2,1)} %bitcast.22), calls=%async_computation.2 | async-start | bytes 3145728 | tf_op jit(solution)/shard_map/all_to_all | solution.py:539
  108.6 7.1 %experts.3 = bf16[512,1536]{1,0:T(8,128)(2,1)} custom-call(bf16[512,1536]{1,0:T(8,128)(2,1)S(1)} %bitcast.17, bf16[1,1536,768]{2,1,0:T(8,128)(2,1)} %w_gate.3, bf16[1,1536,768]{2,1,0:T(8,128)(2,1)} %w_up.3, bf16[1,768,1536]{2,1,0:T(8,128)(2,1)} %w_down.3), custom_call_target="tpu_custom_call" | custom-call | flops 3623878656 | bytes 7077888 | tf_op jit(solution)/shard_map/experts/pallas_call | solution.py:494
  115.7 15.9 %all-to-all-done.2 = bf16[16,32,1536]{2,1,0:T(8,128)(2,1)S(1)} async-done(((bf16[16,32,1536]{2,1,0:T(8,128)(2,1)}), bf16[16,32,1536]{2,1,0:T(8,128)(2,1)S(1)}, u32[]{:S(2)}, u32[]{:S(2)}) %all-to-all-start.2) | async-done | bytes 1572896 | tf_op jit(solution)/shard_map/all_to_all | solution.py:539
  131.6 3.7 %all-to-all-start.3 = ((bf16[16,32,1536]{2,1,0:T(8,128)(2,1)}), bf16[16,32,1536]{2,1,0:T(8,128)(2,1)S(1)}, u32[]{:S(2)}, u32[]{:S(2)}) async-start(bf16[16,32,1536]{2,1,0:T(8,128)(2,1)} %bitcast.21), calls=%async_computation.3 | async-start | bytes 3145728 | tf_op jit(solution)/shard_map/all_to_all | solution.py:539
  135.3 1.5 partial.1
  136.8 2.9 %collective-permute-start.6 = (bf16[128,1536]{1,0:T(8,128)(2,1)S(1)}, bf16[128,1536]{1,0:T(8,128)(2,1)S(1)}, u32[]{:S(2)}, u32[]{:S(2)}) collective-permute-start(bf16[128,1536]{1,0:T(8,128)(2,1)S(1)} %partial.1), channel_id=1, source_target_pairs={{0,24},{4,28},{8,16},{12,20},{16,8},{20,12},{24,0},{28,4},{1,25},{... | collective-permute-start | bytes 1179656 | tf_op jit(solution)/shard_map/ppermute | solution.py:753
  139.8 18.5 %all-to-all-done.3 = bf16[16,32,1536]{2,1,0:T(8,128)(2,1)S(1)} async-done(((bf16[16,32,1536]{2,1,0:T(8,128)(2,1)}), bf16[16,32,1536]{2,1,0:T(8,128)(2,1)S(1)}, u32[]{:S(2)}, u32[]{:S(2)}) %all-to-all-start.3) | async-done | bytes 1572896 | tf_op jit(solution)/shard_map/all_to_all | solution.py:539
  158.3 1.2 copy-done.10
  159.5 2.3 %near.1.total = f32[128,1536]{1,0:T(8,128)S(1)} custom-call(bf16[2,2,128,512]{3,2,1,0:T(8,128)(2,1)} %shares.1, bf16[64,1536]{1,0:T(8,128)(2,1)} %copy-done.6, bf16[64,1536]{1,0:T(8,128)(2,1)} %copy-done.7, bf16[512,1536]{1,0:T(8,128)(2,1)} %bitcast.19), custom_call_target="tpu_custom_call" | custom-call | flops 400000000 | bytes 2000000 | tf_op jit(solution)/shard_map/near/pallas_call | solution.py:755
  161.8 3.0 %collective-permute-done.6.far = bf16[128,1536]{1,0:T(8,128)(2,1)S(1)} collective-permute-done((bf16[128,1536]{1,0:T(8,128)(2,1)S(1)}, bf16[128,1536]{1,0:T(8,128)(2,1)S(1)}, u32[]{:S(2)}, u32[]{:S(2)}) %collective-permute-start.6) | collective-permute-done | bytes 393248 | tf_op jit(solution)/shard_map/ppermute | solution.py:753
  (34 shorter events, 5.8 us)
Async XLA Ops:
  0.6 4.0 %copy-start.11 = (bf16[1536]{0:T(1024)(128)(2,1)S(1)}, bf16[1536]{0:T(1024)(128)(2,1)}, u32[]{:S(2)}) copy-start(bf16[1536]{0:T(1024)(128)(2,1)} %param.29) | copy-start | bytes 9220
  0.6 4.6 %copy-start.12 = (bf16[1536]{0:T(1024)(128)(2,1)S(1)}, bf16[1536]{0:T(1024)(128)(2,1)}, u32[]{:S(2)}) copy-start(bf16[1536]{0:T(1024)(128)(2,1)} %param.26) | copy-start | bytes 9220
  4.0 2.1 %collective-permute-start = (bf16[528,512]{1,0:T(8,128)(2,1)S(1)}, bf16[528,512]{1,0:T(8,128)(2,1)S(1)}, u32[]{:S(2)}, u32[]{:S(2)}) collective-permute-start(bf16[528,512]{1,0:T(8,128)(2,1)S(1)} %get-tuple-element.37.rest_0_), channel_id=1, source_target_pairs={{0,1},{1,0},{2,3},{3,2},{4,5},{5,4},{6,7},{7,6},{8,9},{9,8},{10,11... | collective-permute-start | bytes 1622024 | tf_op jit(solution)/shard_map/ppermute | solution.py:560
  4.5 5.3 %collective-permute-start.1 = (bf16[512,512]{1,0:T(8,128)(2,1)S(1)}, bf16[512,512]{1,0:T(8,128)(2,1)S(1)}, u32[]{:S(2)}, u32[]{:S(2)}) collective-permute-start(bf16[512,512]{1,0:T(8,128)(2,1)S(1)} %get-tuple-element.54.rest_0_), channel_id=1, source_target_pairs={{0,1},{1,0},{2,3},{3,2},{4,5},{5,4},{6,7},{7,6},{8,9},{9,8},{10,11... | collective-permute-start | bytes 1572872 | tf_op jit(solution)/shard_map/ppermute | solution.py:560
  5.8 4.9 %copy-start.8 = (s32[2,8]{1,0:T(2,128)S(1)}, s32[2,8]{1,0:T(2,128)}, u32[]{:S(2)}) copy-start(s32[2,8]{1,0:T(2,128)} %table.3) | copy-start | bytes 196
  5.8 4.9 %copy-start.9 = (s32[2]{0:T(128)S(1)}, s32[2]{0:T(128)}, u32[]{:S(2)}) copy-start(s32[2]{0:T(128)} %lengths.3) | copy-start | bytes 28
  7.0 19.2 %collective-permute-start.3 = (bf16[528,512]{1,0:T(8,128)(2,1)}, bf16[528,512]{1,0:T(8,128)(2,1)}, u32[]{:S(2)}, u32[]{:S(2)}) collective-permute-start(bf16[528,512]{1,0:T(8,128)(2,1)} %broadcast_select_fusion), channel_id=1, source_target_pairs={{0,2},{1,3},{2,0},{3,1},{4,6},{5,7},{6,4},{7,5},{8,10},{9,11},{10,... | collective-permute-start | bytes 1622024 | tf_op jit(solution)/shard_map/ppermute | solution.py:569
  10.7 23.2 %collective-permute-start.4 = (bf16[512,512]{1,0:T(8,128)(2,1)}, bf16[512,512]{1,0:T(8,128)(2,1)S(1)}, u32[]{:S(2)}, u32[]{:S(2)}) collective-permute-start(bf16[512,512]{1,0:T(8,128)(2,1)} %broadcast_select_fusion.1), channel_id=1, source_target_pairs={{0,2},{1,3},{2,0},{3,1},{4,6},{5,7},{6,4},{7,5},{8,10},{9,11},{10,... | collective-permute-start | bytes 1572872 | tf_op jit(solution)/shard_map/ppermute | solution.py:569
  20.0 0.7 copy-start.6
  20.7 9.9 %collective-permute-start.2 = (bf16[80,1536]{1,0:T(8,128)(2,1)S(1)}, bf16[80,1536]{1,0:T(8,128)(2,1)S(1)}, u32[]{:S(2)}, u32[]{:S(2)}) collective-permute-start(bf16[80,1536]{1,0:T(8,128)(2,1)S(1)} %get-tuple-element.40.staying.rest_0_), channel_id=1, source_target_pairs={{0,24},{4,28},{8,16},{12,20},{16,8},{20,12},{24,0},{28,4},{1,25},{... | collective-permute-start | bytes 737288 | tf_op jit(solution)/shard_map/ppermute | solution.py:618
  30.6 15.9 %copy-start = (bf16[80,1536]{1,0:T(8,128)(2,1)}, bf16[80,1536]{1,0:T(8,128)(2,1)S(1)}, u32[]{:S(2)}) copy-start(bf16[80,1536]{1,0:T(8,128)(2,1)S(1)} %collective-permute-done.2.parcel.staying.rest_2_) | copy-start | bytes 737284
  38.0 10.0 %copy-start.7 = (bf16[64,1536]{1,0:T(8,128)(2,1)}, bf16[64,1536]{1,0:T(8,128)(2,1)S(1)}, u32[]{:S(2)}) copy-start(bf16[64,1536]{1,0:T(8,128)(2,1)S(1)} %get-tuple-element.66.moved) | copy-start | bytes 589828
  38.0 17.0 %copy-start.2 = (bf16[64,1536]{1,0:T(8,128)(2,1)}, bf16[64,1536]{1,0:T(8,128)(2,1)S(1)}, u32[]{:S(2)}) copy-start(bf16[64,1536]{1,0:T(8,128)(2,1)S(1)} %get-tuple-element.57.moved.rest_1_) | copy-start | bytes 589828
  38.1 8.4 %collective-permute-start.5 = (bf16[64,1536]{1,0:T(8,128)(2,1)S(1)}, bf16[64,1536]{1,0:T(8,128)(2,1)S(1)}, u32[]{:S(2)}, u32[]{:S(2)}) collective-permute-start(bf16[64,1536]{1,0:T(8,128)(2,1)S(1)} %get-tuple-element.57.moved.rest_1_), channel_id=1, source_target_pairs={{0,24},{4,28},{8,16},{12,20},{16,8},{20,12},{24,0},{28,4},{1,25},{... | collective-permute-start | bytes 589832 | tf_op jit(solution)/shard_map/ppermute | solution.py:685
  46.5 1.5 copy-start.4
  48.0 30.1 %all-to-all-start = ((bf16[16,32,1536]{2,1,0:T(8,128)(2,1)}), bf16[16,32,1536]{2,1,0:T(8,128)(2,1)S(1)}, u32[]{:S(2)}, u32[]{:S(2)}) async-start(bf16[16,32,1536]{2,1,0:T(8,128)(2,1)} %bitcast.20), calls=%async_computation | async-start | bytes 3145728 | tf_op jit(solution)/shard_map/all_to_all | solution.py:539
  78.1 26.7 %all-to-all-start.1 = ((bf16[16,32,1536]{2,1,0:T(8,128)(2,1)}), bf16[16,32,1536]{2,1,0:T(8,128)(2,1)S(1)}, u32[]{:S(2)}, u32[]{:S(2)}) async-start(bf16[16,32,1536]{2,1,0:T(8,128)(2,1)} %bitcast.18), calls=%async_computation.1 | async-start | bytes 3145728 | tf_op jit(solution)/shard_map/all_to_all | solution.py:539
  82.0 0.9 copy-start.1
  83.0 0.9 copy-start.3
  83.9 0.9 copy-start.5
  104.8 26.7 %all-to-all-start.2 = ((bf16[16,32,1536]{2,1,0:T(8,128)(2,1)}), bf16[16,32,1536]{2,1,0:T(8,128)(2,1)S(1)}, u32[]{:S(2)}, u32[]{:S(2)}) async-start(bf16[16,32,1536]{2,1,0:T(8,128)(2,1)} %bitcast.22), calls=%async_computation.2 | async-start | bytes 3145728 | tf_op jit(solution)/shard_map/all_to_all | solution.py:539
  131.6 26.7 %all-to-all-start.3 = ((bf16[16,32,1536]{2,1,0:T(8,128)(2,1)}), bf16[16,32,1536]{2,1,0:T(8,128)(2,1)S(1)}, u32[]{:S(2)}, u32[]{:S(2)}) async-start(bf16[16,32,1536]{2,1,0:T(8,128)(2,1)} %bitcast.21), calls=%async_computation.3 | async-start | bytes 3145728 | tf_op jit(solution)/shard_map/all_to_all | solution.py:539
  136.8 28.0 %collective-permute-start.6 = (bf16[128,1536]{1,0:T(8,128)(2,1)S(1)}, bf16[128,1536]{1,0:T(8,128)(2,1)S(1)}, u32[]{:S(2)}, u32[]{:S(2)}) collective-permute-start(bf16[128,1536]{1,0:T(8,128)(2,1)S(1)} %partial.1), channel_id=1, source_target_pairs={{0,24},{4,28},{8,16},{12,20},{16,8},{20,12},{24,0},{28,4},{1,25},{... | collective-permute-start | bytes 1179656 | tf_op jit(solution)/shard_map/ppermute | solution.py:753
  158.3 1.2 copy-start.10

commit v6 on v5

--- a/solution.py
+++ b/solution.py
@@ -20,6 +20,7 @@
 MIB = 1024 * 1024
 NOTE = 16
 NOTE_BASE = 32
+NOTE_SPAN = 2048
 AXES = ("req", "ep")
 
 VMEM = pl.BlockSpec(memory_space=pltpu.VMEM)
@@ -109,11 +110,11 @@
 
 
 def leaving_kernel(slot, dest, lengths, table, pool, first, second, sems):
-    half, page = second.shape[0], pool.shape[1]
+    half, page = first.shape[0] - NOTE, pool.shape[1]
     loads = []
     for i in range(table.shape[1]):
         target = first if i * page < half else second
-        span = pl.ds(i * page % half, page)
+        span = pl.ds(i * page if i * page < half else i * page - half, page)
         loads.append(
             pltpu.make_async_copy(pool.at[table[slot[0], i]], target.at[span], sems.at[i])
         )
@@ -122,7 +123,7 @@
     row = lax.broadcasted_iota(jnp.int32, (NOTE, first.shape[1]), 0)
     lane = lax.broadcasted_iota(jnp.int32, (NOTE, first.shape[1]), 1)
     note = jnp.zeros((NOTE, first.shape[1]), jnp.int32)
-    parts = (dest[0] * 4 * half, length // NOTE_BASE * NOTE_BASE, length % NOTE_BASE)
+    parts = (dest[0] * NOTE_SPAN, length // NOTE_BASE * NOTE_BASE, length % NOTE_BASE)
     for at, value in enumerate(parts):
         note = jnp.where((row == 0) & (lane == at), value, note)
     first[half:, :] = note.astype(jnp.float32).astype(jnp.bfloat16)
@@ -319,9 +320,9 @@
     length = jnp.int32(0)
     for i, source in enumerate(sources):
         code = jnp.sum(notes[i].astype(jnp.float32)).astype(jnp.int32)
-        mine = code // (4 * half) == me[0]
+        mine = code // NOTE_SPAN == me[0]
         chosen = jnp.where(mine, i, chosen)
-        length = jnp.where(mine, code % (4 * half), length)
+        length = jnp.where(mine, code % NOTE_SPAN, length)
 
         @pl.when(mine)
         def _(source=source):
@@ -371,7 +372,7 @@
 
 
 def arrival_kernel(
-    slot, pick, stacked, mixed, tops, totals, hidden, gain, w_out, *rest,
+    first_rows, slot, pick, stacked, mixed, tops, totals, hidden, gain, w_out, *rest,
 ):
     sources = rest[:-8]
     moved, moved_normed, cache, weights, rows, gains, sems, cache_sem = rest[-8:]
@@ -387,7 +388,7 @@
     loads = load_all(((hidden.at[own], rows), (gain, gains), (w_out, weights)), sems)
     scale = HEAD_SIZE ** (-0.5) * LOG2E
     key_width = KEY_VALUE_HEADS * HEAD_SIZE
-    in_cache = lax.broadcasted_iota(jnp.int32, (1, half), 1) + half < pick[1]
+    in_cache = lax.broadcasted_iota(jnp.int32, (1, half), 1) + first_rows < pick[1]
     bias = jnp.where(in_cache, 0.0, MASKED)
     pltpu.make_async_copy(sources[0], cache, cache_sem).wait()
     outs = []
@@ -539,14 +540,15 @@
         return lax.all_to_all(rows, AXES, 0, 0, tiled=True, axis_index_groups=groups)
 
     f32 = jnp.float32
-    half_cache = context // 2
+    first_rows = pages * 3 // 8 * page
+    last_rows = context - first_rows
     leaving = pl.pallas_call(
         leaving_kernel,
         in_specs=[SMEM] * 4 + [HBM],
         out_specs=[VMEM] * 2,
         out_shape=[
-            pltpu.VMEM((half_cache + NOTE, kv_width), bf16),
-            pltpu.VMEM((half_cache, kv_width), bf16),
+            pltpu.VMEM((first_rows + NOTE, kv_width), bf16),
+            pltpu.VMEM((last_rows, kv_width), bf16),
         ],
         scratch_shapes=[pltpu.SemaphoreType.DMA((pages,))],
         compiler_params=params(58),
@@ -645,7 +647,7 @@
             jax.ShapeDtypeStruct((tokens, kv_width), bf16),
         ],
         scratch_shapes=[
-            pltpu.VMEM((half_cache, kv_width), bf16),
+            pltpu.VMEM((first_rows, kv_width), bf16),
             pltpu.VMEM((len(early), NOTE, 128), bf16),
             pltpu.VMEM(projected.shape, f32),
             pltpu.VMEM(spectrum.shape, f32),
@@ -663,12 +665,12 @@
     )
     far_parcel, routes, pick, *late = lax.optimization_barrier((far_parcel, routes, pick, *late))
     moved, moved_normed = pl.pallas_call(
-        arrival_kernel,
+        functools.partial(arrival_kernel, first_rows),
         in_specs=[SMEM] * 2 + [VMEM] * 4 + [HBM] * 3 + [ANY] * len(late),
         out_specs=[VMEM] * 2,
         out_shape=[pltpu.VMEM((draft, model), bf16)] * 2,
         scratch_shapes=[
-            pltpu.VMEM((half_cache, kv_width), bf16),
+            pltpu.VMEM((last_rows, kv_width), bf16),
             pltpu.VMEM(w_out.shape, bf16),
             pltpu.VMEM((draft, model), bf16),
             pltpu.VMEM((1, model), bf16),

time: 166 us -> 172 us (1.036)
  waiting for transfers between devices: 77.1 us -> 82.3 us
    ppermute x2, waiting for transfers between devices: 3.28 us -> 8.4 us  [per_device(): sources.append(lax.ppermute(payload, 'ep', moves))]
    unnamed x26 -> x28, local copies, waits for them, and re-layouts: 4.66 us -> 3.84 us
  transfers between devices with their start and end apart: 11 -> 11, of which waited for: 9 -> 8; matrix products, arithmetic and copies ran while one was open for 2% -> 2% of each run, Pallas kernels for 23% -> 22%
where the time goes in v6:
time: 172 us; the launch traced here: 171 us
  waiting for transfers between devices  82.3 us (48%)
  Pallas kernels  46 us (27%)
  starting transfers between devices  34 us (20%)
  local copies, waits for them, and re-layouts  5.04 us (3%)
  between operations  2.2 us (1%)
  other arithmetic  1.75 us (1%)
    all_to_all x4, waiting for transfers between devices, within_half(): lax.all_to_all(rows, AXES, 0, 0, tiled=True, axis_index_groups=groups)  65.8 us
    all_to_all x4, starting transfers between devices, within_half(): lax.all_to_all(rows, AXES, 0, 0, tiled=True, axis_index_groups=groups)  19.4 us
    pallas_call x2, Pallas kernels, run_experts(): pl.pallas_call(expert_kernel, in_specs=[VMEM] + [HBM] * 3, out_specs=HBM,...  14.1 us
    pallas_call x1, Pallas kernels, per_device(): pl.pallas_call(front_kernel, in_specs=[SMEM] * 3 + [HBM] * 10, out_specs=...  9.32 us
    ppermute x2, waiting for transfers between devices, per_device(): sources.append(lax.ppermute(payload, 'ep', moves))  8.4 us
    pallas_call x1, Pallas kernels, per_device(): pl.pallas_call(functools.partial(arrival_kernel, first_rows), in_specs=[S...  4.33 us
    ppermute x1, waiting for transfers between devices, per_device(): own_far = lax.ppermute(far_sum, 'req', swap)  4.28 us
    ppermute x1, starting transfers between devices, per_device(): far_parcel = lax.ppermute(parcel, 'req', swap)  4.13 us
  transfers between devices with their start and end apart: 11, of which 8 were waited for; matrix products, arithmetic and copies ran while one was open for 2% of the time, Pallas kernels for 22%

profile of v6, /device:TPU:0, one launch (start us, length us, event | category | flops | bytes accessed | tf_op | source)
XLA Modules:
  0.0 171.3 jit_solution(11692162627083202171)
XLA Ops:
  2.0 2.1 %leaving.1 = (bf16[400,512]{1,0:T(8,128)(2,1)S(1)}, bf16[640,512]{1,0:T(8,128)(2,1)S(1)}) custom-call(s32[1]{0:T(128)S(6)} %copy.20.slot, s32[1]{0:T(128)} %copy.21.dest, s32[2]{0:T(128)} %lengths.3, s32[2,8]{1,0:T(2,128)} %table.3, bf16[16,128,512]{2,1,0:T(8,128)(2,1)} %pool.3), custom_call_target="tpu_custom_call" | custom-call | bytes 2097152 | tf_op jit(solution)/shard_map/leaving/pallas_call | solution.py:545
  6.3 0.9 broadcast_select_fusion
  7.2 2.9 %collective-permute-start.4 = (bf16[640,512]{1,0:T(8,128)(2,1)}, bf16[640,512]{1,0:T(8,128)(2,1)S(1)}, u32[]{:S(2)}, u32[]{:S(2)}) collective-permute-start(bf16[640,512]{1,0:T(8,128)(2,1)} %broadcast_select_fusion), channel_id=1, source_target_pairs={{0,2},{1,3},{2,0},{3,1},{4,6},{5,7},{6,4},{7,5},{8,10},{9,11},{10,... | collective-permute-start | bytes 1966088 | tf_op jit(solution)/shard_map/ppermute | solution.py:571
  11.0 9.3 %front.1 = (f32[64,2048]{1,0:T(8,128)}, f32[64,64]{1,0:T(8,128)S(1)}, bf16[64,64]{1,0:T(8,128)(2,1)S(1)}, bf16[64,512]{1,0:T(8,128)(2,1)S(1)}, bf16[64,1536]{1,0...) custom-call(s32[1]{0:T(128)S(6)} %copy.20.slot, s32[2]{0:T(128)S(1)} %copy-done.11, s32[2,8]{1,0:T(2,128)S(1)} %copy-done.10, ...), custom_call_target="tpu_custom_call" | custom-call | flops 3000000000 | bytes 3000000 | tf_op jit(solution)/shard_map/front/pallas_call | solution.py:583
  20.3 4.1 %collective-permute-start.2 = (bf16[80,1536]{1,0:T(8,128)(2,1)S(1)}, bf16[80,1536]{1,0:T(8,128)(2,1)S(1)}, u32[]{:S(2)}, u32[]{:S(2)}) collective-permute-start(bf16[80,1536]{1,0:T(8,128)(2,1)S(1)} %get-tuple-element.40.staying.rest_0_), channel_id=1, source_target_pairs={{0,24},{4,28},{8,16},{12,20},{16,8},{20,12},{24,0},{28,4},{1,25},{... | collective-permute-start | bytes 737288 | tf_op jit(solution)/shard_map/ppermute | solution.py:620
  24.4 1.3 routes.1
  25.8 8.4 %collective-permute-done.3.rest_2_ = bf16[400,512]{1,0:T(8,128)(2,1)} collective-permute-done((bf16[400,512]{1,0:T(8,128)(2,1)}, bf16[400,512]{1,0:T(8,128)(2,1)}, u32[]{:S(2)}, u32[]{:S(2)}) %collective-permute-start.3) | collective-permute-done | bytes 409632 | tf_op jit(solution)/shard_map/ppermute | solution.py:571
  34.2 1.0 copy-done.7
  35.2 3.4 %early.1 = (s32[2]{0:T(128)S(1)}, bf16[2,384,128]{2,1,0:T(8,128)(2,1)S(1)}, f32[2,384,128]{2,1,0:T(8,128)S(1)}, f32[2,384,1]{2,1,0:T(8,128)S(1)}, f32[2,384,1]{2,1,0:T(8,128)S(1)}, /*index=5*/bf16[128,512]{1,0:T(8,128)(2,1)}) custom-call(s32[1]{0:T(128)S(6)} %copy.20.slot, s32[1]{0:T(128)} %bitcast.3.me, f32[64,64]{1,0:T(8,128)S(1)} %get-tuple-element.44.reach, ...), custom_call_target="tpu_custom_call" | custom-call | flops 1000000000 | bytes 2000000 | tf_op jit(solution)/shard_map/early/pallas_call | solution.py:637
  38.6 4.3 %arrival.1 = (bf16[64,1536]{1,0:T(8,128)(2,1)S(1)}, bf16[64,1536]{1,0:T(8,128)(2,1)S(1)}) custom-call(s32[1]{0:T(128)S(6)} %copy.20.slot, s32[2]{0:T(128)S(1)} %get-tuple-element.49.pick, bf16[2,384,128]{2,1,0:T(8,128)(2,1)S(1)} %get-tuple-element.50.stacked, f32[2,384,128]{2,1,0:T(8,128)S(1)} %get-tuple-element.51.mixed, ...), custom_call_target="tpu_custom_call" | custom-call | flops 2000000000 | bytes 8000000 | tf_op jit(solution)/shard_map/arrival/pallas_call | solution.py:667
  43.0 3.9 %collective-permute-start.5 = (bf16[64,1536]{1,0:T(8,128)(2,1)S(1)}, bf16[64,1536]{1,0:T(8,128)(2,1)S(1)}, u32[]{:S(2)}, u32[]{:S(2)}) collective-permute-start(bf16[64,1536]{1,0:T(8,128)(2,1)S(1)} %get-tuple-element.57.moved.rest_1_), channel_id=1, source_target_pairs={{0,24},{4,28},{8,16},{12,20},{16,8},{20,12},{24,0},{28,4},{1,25},{... | collective-permute-start | bytes 589832 | tf_op jit(solution)/shard_map/ppermute | solution.py:687
  47.5 3.4 %collective-permute-done.5.moved.rest_3_ = bf16[64,1536]{1,0:T(8,128)(2,1)S(1)} collective-permute-done((bf16[64,1536]{1,0:T(8,128)(2,1)S(1)}, bf16[64,1536]{1,0:T(8,128)(2,1)S(1)}, u32[]{:S(2)}, u32[]{:S(2)}) %collective-permute-start.5) | collective-permute-done | bytes 196640 | tf_op jit(solution)/shard_map/ppermute | solution.py:687
  50.9 1.5 pack.3
  52.5 7.4 %all-to-all-start = ((bf16[16,32,1536]{2,1,0:T(8,128)(2,1)}), bf16[16,32,1536]{2,1,0:T(8,128)(2,1)S(1)}, u32[]{:S(2)}, u32[]{:S(2)}) async-start(bf16[16,32,1536]{2,1,0:T(8,128)(2,1)} %bitcast.19), calls=%async_computation | async-start | bytes 3145728 | tf_op jit(solution)/shard_map/all_to_all | solution.py:540
  59.9 1.5 pack.2
  61.4 21.5 %all-to-all-done = bf16[16,32,1536]{2,1,0:T(8,128)(2,1)S(1)} async-done(((bf16[16,32,1536]{2,1,0:T(8,128)(2,1)}), bf16[16,32,1536]{2,1,0:T(8,128)(2,1)S(1)}, u32[]{:S(2)}, u32[]{:S(2)}) %all-to-all-start) | async-done | bytes 1572896 | tf_op jit(solution)/shard_map/all_to_all | solution.py:540
  82.9 3.9 %all-to-all-start.1 = ((bf16[16,32,1536]{2,1,0:T(8,128)(2,1)}), bf16[16,32,1536]{2,1,0:T(8,128)(2,1)S(1)}, u32[]{:S(2)}, u32[]{:S(2)}) async-start(bf16[16,32,1536]{2,1,0:T(8,128)(2,1)} %bitcast.18), calls=%async_computation.1 | async-start | bytes 3145728 | tf_op jit(solution)/shard_map/all_to_all | solution.py:540
  86.8 0.9 copy-done.1
  87.8 0.9 copy-done.3
  88.7 0.9 copy-done.5
  89.6 3.1 %shares.1 = bf16[2,2,128,512]{3,2,1,0:T(8,128)(2,1)} custom-call(s32[1]{0:T(128)} %bitcast.2.base, bf16[32,1536]{1,0:T(8,128)(2,1)} %bitcast.22, bf16[80,1536]{1,0:T(8,128)(2,1)S(1)} %get-tuple-element.40.staying.rest_0_, bf16[64,1536]{1,0:T(8,128)(2,1)S(1)} %copy-done.3, bf16[80,1536]{1,0:T(8,128)(2,1)S(1)} %copy-done.1, bf16[64,1536]{1,0:T(8,128)(2,1)S(1)} %copy-done.5, ...), custom_call_target="tpu_custom_call" | custom-call | flops 300000000 | bytes 1000000 | tf_op jit(solution)/shard_map/shares/pallas_call | solution.py:718
  92.8 7.0 %experts.2 = bf16[512,1536]{1,0:T(8,128)(2,1)} custom-call(bf16[512,1536]{1,0:T(8,128)(2,1)S(1)} %bitcast.16, bf16[1,1536,768]{2,1,0:T(8,128)(2,1)} %w_gate.3, bf16[1,1536,768]{2,1,0:T(8,128)(2,1)} %w_up.3, bf16[1,768,1536]{2,1,0:T(8,128)(2,1)} %w_down.3), custom_call_target="tpu_custom_call" | custom-call | flops 3623878656 | bytes 7077888 | tf_op jit(solution)/shard_map/experts/pallas_call | solution.py:495
  99.8 9.9 %all-to-all-done.1 = bf16[16,32,1536]{2,1,0:T(8,128)(2,1)S(1)} async-done(((bf16[16,32,1536]{2,1,0:T(8,128)(2,1)}), bf16[16,32,1536]{2,1,0:T(8,128)(2,1)S(1)}, u32[]{:S(2)}, u32[]{:S(2)}) %all-to-all-start.1) | async-done | bytes 1572896 | tf_op jit(solution)/shard_map/all_to_all | solution.py:540
  109.7 3.7 %all-to-all-start.2 = ((bf16[16,32,1536]{2,1,0:T(8,128)(2,1)}), bf16[16,32,1536]{2,1,0:T(8,128)(2,1)S(1)}, u32[]{:S(2)}, u32[]{:S(2)}) async-start(bf16[16,32,1536]{2,1,0:T(8,128)(2,1)} %bitcast.21), calls=%async_computation.2 | async-start | bytes 3145728 | tf_op jit(solution)/shard_map/all_to_all | solution.py:540
  113.4 7.1 %experts.3 = bf16[512,1536]{1,0:T(8,128)(2,1)} custom-call(bf16[512,1536]{1,0:T(8,128)(2,1)S(1)} %bitcast.17, bf16[1,1536,768]{2,1,0:T(8,128)(2,1)} %w_gate.3, bf16[1,1536,768]{2,1,0:T(8,128)(2,1)} %w_up.3, bf16[1,768,1536]{2,1,0:T(8,128)(2,1)} %w_down.3), custom_call_target="tpu_custom_call" | custom-call | flops 3623878656 | bytes 7077888 | tf_op jit(solution)/shard_map/experts/pallas_call | solution.py:495
  120.4 15.9 %all-to-all-done.2 = bf16[16,32,1536]{2,1,0:T(8,128)(2,1)S(1)} async-done(((bf16[16,32,1536]{2,1,0:T(8,128)(2,1)}), bf16[16,32,1536]{2,1,0:T(8,128)(2,1)S(1)}, u32[]{:S(2)}, u32[]{:S(2)}) %all-to-all-start.2) | async-done | bytes 1572896 | tf_op jit(solution)/shard_map/all_to_all | solution.py:540
  136.4 4.4 %all-to-all-start.3 = ((bf16[16,32,1536]{2,1,0:T(8,128)(2,1)}), bf16[16,32,1536]{2,1,0:T(8,128)(2,1)}, u32[]{:S(2)}, u32[]{:S(2)}) async-start(bf16[16,32,1536]{2,1,0:T(8,128)(2,1)} %bitcast.20), calls=%async_computation.3 | async-start | bytes 3145728 | tf_op jit(solution)/shard_map/all_to_all | solution.py:540
  140.8 1.5 partial.1
  142.3 3.0 %collective-permute-start.6 = (bf16[128,1536]{1,0:T(8,128)(2,1)S(1)}, bf16[128,1536]{1,0:T(8,128)(2,1)S(1)}, u32[]{:S(2)}, u32[]{:S(2)}) collective-permute-start(bf16[128,1536]{1,0:T(8,128)(2,1)S(1)} %partial.1), channel_id=1, source_target_pairs={{0,24},{4,28},{8,16},{12,20},{16,8},{20,12},{24,0},{28,4},{1,25},{... | collective-permute-start | bytes 1179656 | tf_op jit(solution)/shard_map/ppermute | solution.py:755
  145.4 18.5 %all-to-all-done.3 = bf16[16,32,1536]{2,1,0:T(8,128)(2,1)} async-done(((bf16[16,32,1536]{2,1,0:T(8,128)(2,1)}), bf16[16,32,1536]{2,1,0:T(8,128)(2,1)}, u32[]{:S(2)}, u32[]{:S(2)}) %all-to-all-start.3) | async-done | bytes 1572896 | tf_op jit(solution)/shard_map/all_to_all | solution.py:540
  163.9 2.3 %near.1.total = f32[128,1536]{1,0:T(8,128)S(1)} custom-call(bf16[2,2,128,512]{3,2,1,0:T(8,128)(2,1)} %shares.1, bf16[64,1536]{1,0:T(8,128)(2,1)} %copy-done.8, bf16[64,1536]{1,0:T(8,128)(2,1)} %copy-done.9, bf16[512,1536]{1,0:T(8,128)(2,1)} %bitcast.12.arrived), custom_call_target="tpu_custom_call" | custom-call | flops 400000000 | bytes 2000000 | tf_op jit(solution)/shard_map/near/pallas_call | solution.py:757
  166.2 4.3 %collective-permute-done.6.far = bf16[128,1536]{1,0:T(8,128)(2,1)S(1)} collective-permute-done((bf16[128,1536]{1,0:T(8,128)(2,1)S(1)}, bf16[128,1536]{1,0:T(8,128)(2,1)S(1)}, u32[]{:S(2)}, u32[]{:S(2)}) %collective-permute-start.6) | collective-permute-done | bytes 393248 | tf_op jit(solution)/shard_map/ppermute | solution.py:755
  (36 shorter events, 4.6 us)
Async XLA Ops:
  0.6 4.0 %copy-start.12 = (bf16[1536]{0:T(1024)(128)(2,1)S(1)}, bf16[1536]{0:T(1024)(128)(2,1)}, u32[]{:S(2)}) copy-start(bf16[1536]{0:T(1024)(128)(2,1)} %param.29) | copy-start | bytes 9220
  0.6 4.6 %copy-start.13 = (bf16[1536]{0:T(1024)(128)(2,1)S(1)}, bf16[1536]{0:T(1024)(128)(2,1)}, u32[]{:S(2)}) copy-start(bf16[1536]{0:T(1024)(128)(2,1)} %param.26) | copy-start | bytes 9220
  4.0 2.2 %collective-permute-start.1 = (bf16[640,512]{1,0:T(8,128)(2,1)S(1)}, bf16[640,512]{1,0:T(8,128)(2,1)S(1)}, u32[]{:S(2)}, u32[]{:S(2)}) collective-permute-start(bf16[640,512]{1,0:T(8,128)(2,1)S(1)} %get-tuple-element.54.rest_0_), channel_id=1, source_target_pairs={{0,1},{1,0},{2,3},{3,2},{4,5},{5,4},{6,7},{7,6},{8,9},{9,8},{10,11... | collective-permute-start | bytes 1966088 | tf_op jit(solution)/shard_map/ppermute | solution.py:562
  4.5 5.5 %collective-permute-start = (bf16[400,512]{1,0:T(8,128)(2,1)S(1)}, bf16[400,512]{1,0:T(8,128)(2,1)S(1)}, u32[]{:S(2)}, u32[]{:S(2)}) collective-permute-start(bf16[400,512]{1,0:T(8,128)(2,1)S(1)} %get-tuple-element.37.rest_0_), channel_id=1, source_target_pairs={{0,1},{1,0},{2,3},{3,2},{4,5},{5,4},{6,7},{7,6},{8,9},{9,8},{10,11... | collective-permute-start | bytes 1228808 | tf_op jit(solution)/shard_map/ppermute | solution.py:562
  5.8 5.1 %copy-start.10 = (s32[2,8]{1,0:T(2,128)S(1)}, s32[2,8]{1,0:T(2,128)}, u32[]{:S(2)}) copy-start(s32[2,8]{1,0:T(2,128)} %table.3) | copy-start | bytes 196
  5.8 5.1 %copy-start.11 = (s32[2]{0:T(128)S(1)}, s32[2]{0:T(128)}, u32[]{:S(2)}) copy-start(s32[2]{0:T(128)} %lengths.3) | copy-start | bytes 28
  7.2 31.5 %collective-permute-start.4 = (bf16[640,512]{1,0:T(8,128)(2,1)}, bf16[640,512]{1,0:T(8,128)(2,1)S(1)}, u32[]{:S(2)}, u32[]{:S(2)}) collective-permute-start(bf16[640,512]{1,0:T(8,128)(2,1)} %broadcast_select_fusion), channel_id=1, source_target_pairs={{0,2},{1,3},{2,0},{3,1},{4,6},{5,7},{6,4},{7,5},{8,10},{9,11},{10,... | collective-permute-start | bytes 1966088 | tf_op jit(solution)/shard_map/ppermute | solution.py:571
  10.1 10.2 %copy-start.6 = (bf16[400,512]{1,0:T(8,128)(2,1)}, bf16[400,512]{1,0:T(8,128)(2,1)S(1)}, u32[]{:S(2)}) copy-start(bf16[400,512]{1,0:T(8,128)(2,1)S(1)} %collective-permute-done.rest_1_) | copy-start | bytes 1228804
  10.9 23.3 %collective-permute-start.3 = (bf16[400,512]{1,0:T(8,128)(2,1)}, bf16[400,512]{1,0:T(8,128)(2,1)}, u32[]{:S(2)}, u32[]{:S(2)}) collective-permute-start(bf16[400,512]{1,0:T(8,128)(2,1)} %broadcast_select_fusion.1), channel_id=1, source_target_pairs={{0,2},{1,3},{2,0},{3,1},{4,6},{5,7},{6,4},{7,5},{8,10},{9,11},{10,... | collective-permute-start | bytes 1228808 | tf_op jit(solution)/shard_map/ppermute | solution.py:571
  20.3 18.3 %copy-start.8 = (bf16[64,1536]{1,0:T(8,128)(2,1)}, bf16[64,1536]{1,0:T(8,128)(2,1)S(1)}, u32[]{:S(2)}) copy-start(bf16[64,1536]{1,0:T(8,128)(2,1)S(1)} %get-tuple-element.65.staying) | copy-start | bytes 589828
  20.3 18.3 %collective-permute-start.2 = (bf16[80,1536]{1,0:T(8,128)(2,1)S(1)}, bf16[80,1536]{1,0:T(8,128)(2,1)S(1)}, u32[]{:S(2)}, u32[]{:S(2)}) collective-permute-start(bf16[80,1536]{1,0:T(8,128)(2,1)S(1)} %get-tuple-element.40.staying.rest_0_), channel_id=1, source_target_pairs={{0,24},{4,28},{8,16},{12,20},{16,8},{20,12},{24,0},{28,4},{1,25},{... | collective-permute-start | bytes 737288 | tf_op jit(solution)/shard_map/ppermute | solution.py:620
  34.2 1.0 copy-start.7
  38.6 12.3 %copy-start = (bf16[80,1536]{1,0:T(8,128)(2,1)}, bf16[80,1536]{1,0:T(8,128)(2,1)S(1)}, u32[]{:S(2)}) copy-start(bf16[80,1536]{1,0:T(8,128)(2,1)S(1)} %collective-permute-done.2.parcel.staying.rest_2_) | copy-start | bytes 737284
  43.0 9.4 %copy-start.9 = (bf16[64,1536]{1,0:T(8,128)(2,1)}, bf16[64,1536]{1,0:T(8,128)(2,1)S(1)}, u32[]{:S(2)}) copy-start(bf16[64,1536]{1,0:T(8,128)(2,1)S(1)} %get-tuple-element.66.moved) | copy-start | bytes 589828
  43.0 16.9 %copy-start.2 = (bf16[64,1536]{1,0:T(8,128)(2,1)}, bf16[64,1536]{1,0:T(8,128)(2,1)S(1)}, u32[]{:S(2)}) copy-start(bf16[64,1536]{1,0:T(8,128)(2,1)S(1)} %get-tuple-element.57.moved.rest_1_) | copy-start | bytes 589828
  43.0 7.9 %collective-permute-start.5 = (bf16[64,1536]{1,0:T(8,128)(2,1)S(1)}, bf16[64,1536]{1,0:T(8,128)(2,1)S(1)}, u32[]{:S(2)}, u32[]{:S(2)}) collective-permute-start(bf16[64,1536]{1,0:T(8,128)(2,1)S(1)} %get-tuple-element.57.moved.rest_1_), channel_id=1, source_target_pairs={{0,24},{4,28},{8,16},{12,20},{16,8},{20,12},{24,0},{28,4},{1,25},{... | collective-permute-start | bytes 589832 | tf_op jit(solution)/shard_map/ppermute | solution.py:687
  50.9 1.6 copy-start.4
  52.5 30.5 %all-to-all-start = ((bf16[16,32,1536]{2,1,0:T(8,128)(2,1)}), bf16[16,32,1536]{2,1,0:T(8,128)(2,1)S(1)}, u32[]{:S(2)}, u32[]{:S(2)}) async-start(bf16[16,32,1536]{2,1,0:T(8,128)(2,1)} %bitcast.19), calls=%async_computation | async-start | bytes 3145728 | tf_op jit(solution)/shard_map/all_to_all | solution.py:540
  82.9 26.7 %all-to-all-start.1 = ((bf16[16,32,1536]{2,1,0:T(8,128)(2,1)}), bf16[16,32,1536]{2,1,0:T(8,128)(2,1)S(1)}, u32[]{:S(2)}, u32[]{:S(2)}) async-start(bf16[16,32,1536]{2,1,0:T(8,128)(2,1)} %bitcast.18), calls=%async_computation.1 | async-start | bytes 3145728 | tf_op jit(solution)/shard_map/all_to_all | solution.py:540
  86.8 0.9 copy-start.1
  87.8 0.9 copy-start.3
  88.7 0.9 copy-start.5
  109.7 26.7 %all-to-all-start.2 = ((bf16[16,32,1536]{2,1,0:T(8,128)(2,1)}), bf16[16,32,1536]{2,1,0:T(8,128)(2,1)S(1)}, u32[]{:S(2)}, u32[]{:S(2)}) async-start(bf16[16,32,1536]{2,1,0:T(8,128)(2,1)} %bitcast.21), calls=%async_computation.2 | async-start | bytes 3145728 | tf_op jit(solution)/shard_map/all_to_all | solution.py:540
  136.4 27.5 %all-to-all-start.3 = ((bf16[16,32,1536]{2,1,0:T(8,128)(2,1)}), bf16[16,32,1536]{2,1,0:T(8,128)(2,1)}, u32[]{:S(2)}, u32[]{:S(2)}) async-start(bf16[16,32,1536]{2,1,0:T(8,128)(2,1)} %bitcast.20), calls=%async_computation.3 | async-start | bytes 3145728 | tf_op jit(solution)/shard_map/all_to_all | solution.py:540
  142.3 28.1 %collective-permute-start.6 = (bf16[128,1536]{1,0:T(8,128)(2,1)S(1)}, bf16[128,1536]{1,0:T(8,128)(2,1)S(1)}, u32[]{:S(2)}, u32[]{:S(2)}) collective-permute-start(bf16[128,1536]{1,0:T(8,128)(2,1)S(1)} %partial.1), channel_id=1, source_target_pairs={{0,24},{4,28},{8,16},{12,20},{16,8},{20,12},{24,0},{28,4},{1,25},{... | collective-permute-start | bytes 1179656 | tf_op jit(solution)/shard_map/ppermute | solution.py:755
